TPU v7x, 256 devices: a whole 4x4x8 slice. The times are simulated.
256 devices in a mesh: grp: 8 (over y, core), cls: 32 (over x, z).
Axes of the slice: x: 4, y: 4, z: 8, core: 2. Of those that a mesh axis runs over, the one named last changes fastest.
Arguments:
- particles: float32 [8192, 128, 128], P(('grp', 'cls')), may hold values from -6 to 6
- references: float32 [1024, 2, 128, 128], P('cls'), may hold values from -6 to 6
- class_of: int32 [8192], P(('grp', 'cls')), may hold values from 0 to 1023, as said below
- rotation_bin: int32 [8192], P(('grp', 'cls')), may hold values from 0 to 3
- shift_best: int32 [8192], P(('grp', 'cls')), may hold values from 0 to 63
- defocus_bin: int32 [8192], P(('grp', 'cls')), may hold values from 0 to 15
- shift_list: int32 [64, 2], replicated, may hold values from -8 to 8
- defocus: float32 [16], replicated, may hold values from 8 to 64
Outputs:
- scores: float32 [8192, 64], P(('grp', 'cls'))
- new_references: float32 [1024, 2, 128, 128], P(('cls', 'grp'))
Inputs may be any that keep to these rules, and one draw needn't show every extreme that they name: `class_of`: class c belongs to owner c // 32. Among the 32 particles of one device (aligned blocks of 32 rows), at most 2 belong to the classes of one owner, and in every draw one owner holds exactly 2 from every device.
All inputs are finite; a program needn't handle non-finite values.
Results may differ from a plain program's by a relative error of at most 0.0003.
Values sent between devices are 32-bit elements; how exact they have to be, the bound alone decides.
No kernel may reach another device: no remote copies, remote signals or barrier semaphores. Data moves between devices by JAX's collectives and lax.ppermute only.
A program may use at most 128 MiB of HBM per device.

v0:
```python
import math

import jax
import jax.numpy as jnp
from jax import lax
from jax.sharding import PartitionSpec as P

highest = lax.Precision.HIGHEST


def dft_tables(image_side):
    pixel_index = jnp.arange(image_side, dtype=jnp.int32)
    turn_grid = (pixel_index[:, None] * pixel_index[None, :] % image_side).astype(jnp.float32)
    angles = turn_grid * (2.0 * math.pi / image_side)
    norm_scale = 1.0 / math.sqrt(image_side)
    cos_table = jnp.cos(angles) * norm_scale
    sin_table = jnp.sin(angles) * norm_scale
    right_table = jnp.concatenate([cos_table, sin_table], axis=1)
    left_table = jnp.stack(
        [jnp.stack([cos_table, -sin_table], axis=1), jnp.stack([-sin_table, -cos_table], axis=1)],
        axis=0,
    )
    return (right_table, left_table)


def spectra(images, right_table, left_table):
    image_side = images.shape[-1]
    halfway = jnp.einsum("...jk,kl->...jl", images, right_table, precision=highest)
    halfway = halfway.reshape(halfway.shape[:-1] + (2, image_side))
    return jnp.einsum("aibj,...jbl->...ail", left_table, halfway, precision=highest)


def rotate(images, quarter_turns):
    turn_grid = quarter_turns[:, None, None]
    rot_one = jnp.rot90(images, 1, axes=(1, 2))
    rot_two = jnp.rot90(images, 2, axes=(1, 2))
    rot_three = jnp.rot90(images, 3, axes=(1, 2))
    return jnp.where(
        turn_grid == 0,
        images,
        jnp.where(turn_grid == 1, rot_one, jnp.where(turn_grid == 2, rot_two, rot_three)),
    )


def contrast_table(defocus, image_side):
    pixel_index = jnp.arange(image_side, dtype=jnp.int32)
    signed = jnp.where(pixel_index < image_side // 2, pixel_index, pixel_index - image_side).astype(
        jnp.float32
    )
    radius = (signed[:, None] * signed[:, None] + signed[None, :] * signed[None, :]) / float(
        (image_side // 2) ** 2
    )
    phases = defocus[:, None, None] * radius[None, :, :]
    return -(0.995 * jnp.sin(phases) + 0.1 * jnp.cos(phases))


def shift_tables(shift_list, image_side):
    pixel_index = jnp.arange(image_side, dtype=jnp.int32)
    turn_grid = (
        pixel_index[None, :, None] * shift_list[:, 0][:, None, None]
        + pixel_index[None, None, :] * shift_list[:, 1][:, None, None]
    ) % image_side
    angles = turn_grid.astype(jnp.float32) * (2.0 * math.pi / image_side)
    return (jnp.cos(angles), jnp.sin(angles))


def make_score_table(shift_cos, shift_sin):
    shift_count = shift_cos.shape[0]
    return jnp.concatenate(
        [shift_cos.reshape(shift_count, -1).T, -shift_sin.reshape(shift_count, -1).T], axis=0
    )


def particle_terms(spectrum, ref_rows, contrast, best_cos, best_sin, score_table, image_side):
    sign_pair = jnp.array([1.0, -1.0], jnp.float32)[None, :, None, None]
    swapped = spectrum[:, ::-1]
    ref_real = ref_rows[:, 0][:, None]
    ref_imag = ref_rows[:, 1][:, None]
    contrast_pair = contrast[:, None]
    product = contrast_pair * (spectrum * ref_real + swapped * ref_imag * sign_pair)
    item_count = spectrum.shape[0]
    scores = (
        jnp.dot(
            product.reshape(item_count, -1),
            score_table,
            precision=highest,
            preferred_element_type=jnp.float32,
        )
        / image_side
    )
    contrib = contrast_pair * (
        spectrum * best_cos[:, None] - swapped * best_sin[:, None] * sign_pair
    )
    return (scores, contrib, contrast * contrast)


def owner_terms(spectrum, slot_info, references, defocus, shift_list, score_table, bin_total):
    source_count = slot_info.shape[0]
    slot_count = slot_info.shape[1]
    item_count = source_count * slot_count
    image_side = spectrum.shape[-1]
    class_local = references.shape[0]
    flat_info = slot_info.reshape(item_count, 4).astype(jnp.int32)
    live_mask = flat_info[:, 3].astype(jnp.float32)
    contrast = contrast_table(defocus[flat_info[:, 1]], image_side) * live_mask[:, None, None]
    best_cos, best_sin = shift_tables(shift_list[flat_info[:, 2]], image_side)
    spec_flat = spectrum.reshape(item_count, 2, image_side, image_side)
    scores, contrib, weight = particle_terms(
        spec_flat,
        references[flat_info[:, 0]],
        contrast,
        best_cos,
        best_sin,
        score_table,
        image_side,
    )
    member = (flat_info[:, 0][:, None] == jnp.arange(class_local, dtype=jnp.int32)[None, :]).astype(
        jnp.float32
    ) * live_mask[:, None]
    bin_hits = (flat_info[:, 1][:, None] == jnp.arange(bin_total, dtype=jnp.int32)[None, :]).astype(
        jnp.float32
    ) * live_mask[:, None]
    return (
        scores.reshape(source_count, slot_count, -1),
        contrib.reshape(source_count, slot_count, 2, image_side, image_side),
        weight.reshape(source_count, slot_count, image_side, image_side),
        member.reshape(source_count, slot_count, class_local),
        bin_hits.reshape(source_count, slot_count, bin_total),
    )


def body(
    particles, references, class_of, rotation_bin, shift_best, defocus_bin, shift_list, defocus
):
    image_side = particles.shape[-1]
    part_rows = particles.shape[0]
    class_local = references.shape[0]
    bin_total = defocus.shape[0]
    owners = lax.axis_size("cls")
    capacity = max(2, 2 * part_rows // owners)
    slot_total = owners * capacity
    right_table, left_table = dft_tables(image_side)
    shift_cos, shift_sin = shift_tables(shift_list, image_side)
    score_table = make_score_table(shift_cos, shift_sin)
    owner_of = class_of // class_local
    local_class = class_of % class_local
    owner_hits = (owner_of[:, None] == jnp.arange(owners, dtype=jnp.int32)[None, :]).astype(
        jnp.int32
    )
    slot_rank = jnp.sum(jnp.cumsum(owner_hits, axis=0) * owner_hits, axis=1) - 1
    target = owner_of * capacity + slot_rank
    info_rows = jnp.stack(
        [local_class, defocus_bin, shift_best, jnp.ones_like(local_class)], axis=1
    ).astype(jnp.float32)
    slot_info = (
        jnp.zeros((slot_total, 4), jnp.float32)
        .at[target]
        .set(info_rows)
        .reshape(owners, capacity, 4)
    )
    turned = rotate(particles, rotation_bin)
    send_images = (
        jnp.zeros((slot_total, image_side, image_side), jnp.float32).at[target].set(turned)
    )
    send_images = send_images.reshape(owners, capacity, image_side, image_side)
    outcome = owner_terms(
        spectra(
            lax.all_to_all(send_images, "cls", split_axis=0, concat_axis=0, tiled=True),
            right_table,
            left_table,
        ),
        lax.all_to_all(slot_info, "cls", split_axis=0, concat_axis=0, tiled=True),
        references,
        defocus,
        shift_list,
        score_table,
        bin_total,
    )
    slot_scores, contrib, weight, member, bin_hits = outcome
    home_scores = lax.all_to_all(slot_scores, "cls", split_axis=0, concat_axis=0, tiled=True)
    scores = home_scores.reshape(slot_total, -1)[target]
    item_count = member.shape[0] * member.shape[1]
    member_flat = member.reshape(item_count, class_local)
    numerator = jnp.einsum(
        "mc,mf->cf", member_flat, contrib.reshape(item_count, -1), precision=highest
    )
    numerator = numerator.reshape(class_local, 2, image_side, image_side)
    weight_sum = jnp.einsum(
        "mc,mf->cf", member_flat, weight.reshape(item_count, -1), precision=highest
    )
    weight_sum = weight_sum.reshape(class_local, image_side, image_side)
    numer_share, denominator = (
        lax.psum_scatter(numerator, "grp", scatter_dimension=0, tiled=True),
        lax.psum_scatter(weight_sum, "grp", scatter_dimension=0, tiled=True),
    )
    fresh_refs = numer_share / (denominator[:, None] + 1.0)
    return (scores, fresh_refs)


def solution(mesh):
    return jax.shard_map(
        body,
        mesh=mesh,
        in_specs=(
            P(("grp", "cls"), None, None),
            P("cls", None, None, None),
            P(("grp", "cls")),
            P(("grp", "cls")),
            P(("grp", "cls")),
            P(("grp", "cls")),
            P(),
            P(),
        ),
        out_specs=(P(("grp", "cls"), None), P(("cls", "grp"), None, None, None)),
        check_vma=False,
    )
```

profile of v0, /device:TPU:1, one launch (start us, length us, event | category | flops | bytes accessed | tf_op | source)
XLA Modules:
  0.0 308.8 jit_solution(14370013345577841537)
XLA Ops:
  7.2 0.7 fusion.73
  8.0 0.2 select_reduce_fusion
  8.2 0.7 add_convert_fusion
  9.1 1.2 scatter_custom_fusion
  10.3 11.9 %all-to-all-start = ((f32[32,2,4]{2,1,0:T(2,128)}), f32[32,2,4]{2,1,0:T(2,128)S(1)}, u32[]{:S(2)}, u32[]{:S(2)}) async-start(f32[32,2,4]{2,1,0:T(2,128)} %bitcast.3), calls=%async_computation | async-start | bytes 65536 | tf_op jit(solution)/shard_map/all_to_all | solution.py:172
  22.2 1.9 copy.40
  24.1 17.4 %rev.20 = f32[32,128,128]{2,1,0:T(8,128)} reverse(f32[32,128,128]{2,1,0:T(8,128)} %param.9), dimensions={1,2} | reverse | bytes 4194304 | tf_op jit(solution)/shard_map/jit(rot90)/jit(_flip)/rev | solution.py:36
  41.6 10.1 %rev.19 = f32[32,128,128]{1,2,0:T(8,128)} reverse(f32[32,128,128]{1,2,0:T(8,128)S(1)} %copy.40), dimensions={2} | reverse | bytes 4194304 | tf_op jit(solution)/shard_map/jit(rot90)/jit(_flip)/rev | solution.py:35
  51.7 11.4 %rev.21 = f32[32,128,128]{2,1,0:T(8,128)} reverse(f32[32,128,128]{2,1,0:T(8,128)S(1)} %bitcast.99), dimensions={2} | reverse | bytes 4194304 | tf_op jit(solution)/shard_map/jit(rot90)/jit(_flip)/rev | solution.py:37
  63.1 4.0 %fusion.28 = f32[32,128,128]{2,1,0:T(8,128)S(1)} fusion(f32[32,128,128]{2,1,0:T(8,128)} %param.9, f32[32,128,128]{1,2,0:T(8,128)} %rev.19, f32[32,128,128]{2,1,0:T(8,128)} %rev.20, f32[32,128,128]{2,1,0:T(8,128)} %rev.21, pred[32]{0:T(512)(128)(4,1)S(1)} %get-tuple-element.29, pred[32]{0:T(512)(128)(4,1)S(1)} %get-tuple-element.30, ...), kind=kLoop, calls=%fused_computation.52 | loop fusion | flops 1572864 | bytes 10485856 | tf_op jit(solution)/shard_map/jit(_where)/select_n | solution.py:38
  67.0 2.5 broadcast_in_dim.26
  69.5 5.4 %scatter_fusion = f32[64,128,128]{2,1,0:T(8,128)} fusion(f32[64,128,128]{2,1,0:T(8,128)} %broadcast_in_dim.26, s32[32]{0:T(128)S(1)} %compare_select_fusion.4, f32[32,128,128]{2,1,0:T(8,128)S(1)} %fusion.28), kind=kCustom, calls=%fused_computation.5 | custom fusion | bytes 6291584 | tf_op jit(solution)/shard_map/scatter | solution.py:163
  74.9 9.5 %all-to-all-start.1 = ((f32[32,2,128,128]{3,2,1,0:T(8,128)}), f32[32,2,128,128]{3,2,1,0:T(8,128)}, u32[]{:S(2)}, u32[]{:S(2)}) async-start(f32[32,2,128,128]{3,2,1,0:T(8,128)} %bitcast.98), calls=%async_computation.1 | async-start | bytes 8388608 | tf_op jit(solution)/shard_map/all_to_all | solution.py:168
  84.4 0.2 reduce-scatter.5.cloned.1.call-start
  84.8 0.3 fusion.63
  85.0 0.3 sine_multiply_fusion
  85.3 0.3 multiply_negate_fusion
  85.7 0.2 slice_reduce_fusion.2
  86.0 0.8 gather_fusion
  86.7 0.2 fusion.62
  86.9 17.8 %fusion.18 = f32[32,128,128]{2,0,1:T(8,128)S(1)} fusion(f32[64]{0:T(128)S(1)} %fusion.62, f32[128,128]{1,0:T(8,128)S(1)} %add_multiply_fusion.1, f32[64]{0:T(128)S(1)} %gather_fusion, s32[64]{0:T(128)S(1)} %get-tuple-element.8), kind=kOutput, calls=%fused_computation.39 | convolution fusion | flops 409997312 | bytes 2163456 | tf_op jit(solution)/shard_map/mc,mf->cf/dot_general | solution.py:188
  104.7 2.6 copy.49
  107.3 0.4 reduce-scatter.3.cloned.1.call-start
  107.8 0.6 gather_fusion.3
  108.4 6.5 %gather_fusion.1 = f32[64,2,128,128]{3,2,1,0:T(8,128)} fusion(f32[32,2,128,128]{3,2,1,0:T(8,128)} %param.10, s32[1024]{0:T(1024)S(1)} %get-tuple-element.38), kind=kCustom, calls=%fused_computation.1 | custom fusion | bytes 16777472 | tf_op jit(solution)/shard_map/gather | solution.py:110
  115.0 16.7 %fusion.11 = f32[64,128,128]{2,1,0:T(8,128)} fusion(f32[64]{0:T(128)S(1)} %fusion.62, f32[128,128]{1,0:T(8,128)S(1)} %add_multiply_fusion.1, f32[64]{0:T(128)S(1)} %gather_fusion), kind=kLoop, calls=%fused_computation.32 | loop fusion | flops 6291456 | bytes 4260352 | tf_op jit(solution)/shard_map/mul | solution.py:105
  131.7 8.1 %slice_bitcast_fusion.1 = (f32[64,128,128]{2,1,0:T(8,128)}, f32[64,128,128]{2,1,0:T(8,128)}) fusion(f32[64,2,128,128]{3,2,1,0:T(8,128)} %gather_fusion.1), kind=kLoop, calls=%fused_computation.48 | loop fusion | bytes 16777216 | tf_op jit(solution)/shard_map/mul | solution.py:80
  139.9 18.8 %fusion.35 = (f32[64,128,128]{2,1,0:T(8,128)}, f32[64,128,128]{2,1,0:T(8,128)}) fusion(s32[64,128]{1,0:T(8,128)S(1)} %iota_multiply_fusion, s32[64,128]{1,0:T(8,128)S(1)} %iota_multiply_fusion.1), kind=kLoop, calls=%fused_computation.59 | loop fusion | flops 14680064 | bytes 8454144 | tf_op jit(solution)/shard_map/cos | solution.py:64
  158.7 18.5 %all-to-all-done.1 = f32[32,2,128,128]{3,2,1,0:T(8,128)} async-done(((f32[32,2,128,128]{3,2,1,0:T(8,128)}), f32[32,2,128,128]{3,2,1,0:T(8,128)}, u32[]{:S(2)}, u32[]{:S(2)}) %all-to-all-start.1) | async-done | bytes 4194336 | tf_op jit(solution)/shard_map/all_to_all | solution.py:168
  177.2 8.8 %fusion.44 = f32[32,2,128,256]{2,3,1,0:T(8,128)S(1)} fusion(f32[32,2,128,128]{3,2,1,0:T(8,128)} %all-to-all-done.1, f32[128,128]{1,0:T(8,128)S(1)} %get-tuple-element.33, f32[128,128]{1,0:T(8,128)S(1)} %get-tuple-element.34), kind=kOutput, calls=%fused_computation.68 | convolution fusion | flops 3221258240 | bytes 12713984 | tf_op jit(solution)/shard_map/reshape | solution.py:29
  186.0 8.9 %fusion.41 = f32[32,2,128,2,128,1]{4,2,5,3,1,0:T(8,128)} fusion(f32[32,2,128,2,128,1]{2,4,3,5,1,0:T(8,128)S(1)} %bitcast.91, f32[1,128,2,128]{3,1,2,0:T(8,128)S(1)} %get-tuple-element.23, f32[1,128,2,128]{3,1,2,0:T(8,128)S(1)} %get-tuple-element.22), kind=kOutput, calls=%fused_computation.63 | convolution fusion | flops 6442516480 | bytes 17039360 | tf_op jit(solution)/shard_map/aibj,...jbl->...ail/dot_general | solution.py:30
  194.9 9.0 %copy.43 = f32[64,2,128,128]{3,2,1,0:T(8,128)} copy(f32[64,2,128,128]{2,3,1,0:T(8,128)} %bitcast.92) | data formatting | bytes 16777216 | tf_op jit(solution)/shard_map/reshape | solution.py:107
  203.9 20.5 %subtract_multiply_fusion = (f32[64,2,128,128]{3,2,1,0:T(8,128)}, f32[64,2,128,128]{3,2,1,0:T(8,128)}) fusion(f32[64,2,128,128]{3,2,1,0:T(8,128)} %copy.43, f32[64,128,128]{2,1,0:T(8,128)} %get-tuple-element.21, f32[64,128,128]{2,1,0:T(8,128)} %get-tuple-element.20, f32[2]{0:T(128)S(1)} %copy-done.3, f32[64,128,128]{2,1,0:T(8,128)} %fusion.11, ...), kind=kLoop, calls=%fused_computation.15 | loop fusion | flops 20971520 | bytes 46137352 | tf_op jit(solution)/shard_map/mul | solution.py:91
  224.4 8.1 %copy.76 = f32[8,8,256,128]{3,1,2,0:T(8,128)S(1)} copy(f32[8,8,256,128]{3,2,1,0:T(8,128)} %bitcast.97) | data formatting | bytes 16777216
  232.5 1.5 copy.59
  234.0 10.2 %fusion.6 = f32[32,2,128,128]{3,0,2,1:T(8,128)S(1)} fusion(f32[2,128,128,64]{2,1,0,3:T(8,128)S(1)} %bitcast.93, f32[64]{0:T(128)S(1)} %fusion.62, s32[64]{0:T(128)S(1)} %get-tuple-element.8), kind=kOutput, calls=%fused_computation.13 | convolution fusion | flops 805310464 | bytes 12583424 | tf_op jit(solution)/shard_map/mc,mf->cf/dot_general | solution.py:184
  244.2 4.4 %copy.48 = f32[32,2,128,128]{3,2,1,0:T(8,128)} copy(f32[32,2,128,128]{3,0,2,1:T(8,128)S(1)} %fusion.6) | data formatting | bytes 8388608 | tf_op jit(solution)/shard_map/mc,mf->cf/dot_general | solution.py:184
  248.7 1.2 broadcast_add_fusion
  249.9 17.5 %cosine_bitcast_fusion = (f32[16384,64]{0,1:T(8,128)S(1)}, f32[16384,64]{0,1:T(8,128)S(1)}) fusion(s32[8,8,128,128]{3,2,1,0:T(8,128)S(1)} %bitcast.100), kind=kLoop, calls=%fused_computation.50 | loop fusion | flops 14680064 | bytes 12582912 | tf_op jit(solution)/shard_map/transpose | solution.py:70
  267.5 11.3 %fusion.36 = f32[64,64]{1,0:T(8,128)S(1)} fusion(f32[16384,64]{0,1:T(8,128)S(1)} %get-tuple-element.19, f32[16384,64]{0,1:T(8,128)S(1)} %get-tuple-element.18, f32[8,8,256,128]{3,2,1,0:T(8,128)S(1)} %bitcast.96), kind=kOutput, calls=%fused_computation.61 | convolution fusion | flops 1612713984 | bytes 16793600 | tf_op jit(solution)/shard_map/dot_general | solution.py:83
  278.8 0.7 reshape.404
  279.5 9.4 %all-to-all-start.2 = ((f32[32,1,128]{2,1,0:T(1,128)}), f32[32,1,128]{2,1,0:T(1,128)S(1)}, u32[]{:S(2)}, u32[]{:S(2)}) async-start(f32[32,1,128]{2,1,0:T(1,128)} %reshape.404), calls=%async_computation.2 | async-start | bytes 32768 | tf_op jit(solution)/shard_map/all_to_all | solution.py:180
  288.9 1.0 broadcast_add_fusion.1
  289.9 7.6 %all-to-all-done.2 = f32[32,1,128]{2,1,0:T(1,128)S(1)} async-done(((f32[32,1,128]{2,1,0:T(1,128)}), f32[32,1,128]{2,1,0:T(1,128)S(1)}, u32[]{:S(2)}, u32[]{:S(2)}) %all-to-all-start.2) | async-done | bytes 16416 | tf_op jit(solution)/shard_map/all_to_all | solution.py:180
  297.4 0.5 broadcast.519
  297.9 0.7 reduce.14
  298.7 1.2 gather_fusion.2
  299.9 1.9 broadcast_divide_fusion
  (40 shorter events, 1.1 us)
Async XLA Ops:
  7.2 78.8 %copy-start = (f32[16]{0:T(128)S(1)}, f32[16]{0:T(128)}, u32[]{:S(2)}) copy-start(f32[16]{0:T(128)} %param.16) | copy-start | bytes 196
  10.3 64.6 %all-to-all-start = ((f32[32,2,4]{2,1,0:T(2,128)}), f32[32,2,4]{2,1,0:T(2,128)S(1)}, u32[]{:S(2)}, u32[]{:S(2)}) async-start(f32[32,2,4]{2,1,0:T(2,128)} %bitcast.3), calls=%async_computation | async-start | bytes 65536 | tf_op jit(solution)/shard_map/all_to_all | solution.py:172
  22.2 19.4 %copy-start.4 = (s32[32]{0:T(128)S(1)}, s32[32]{0:T(128)}, u32[]{:S(2)}) copy-start(s32[32]{0:T(128)} %param.12) | copy-start | bytes 388
  74.9 9.7 %copy-start.2 = (s32[64,2]{0,1:T(2,128)S(1)}, s32[64,2]{0,1:T(2,128)}, u32[]{:S(2)}) copy-start(s32[64,2]{0,1:T(2,128)} %param.15) | copy-start | bytes 1540
  74.9 102.3 %all-to-all-start.1 = ((f32[32,2,128,128]{3,2,1,0:T(8,128)}), f32[32,2,128,128]{3,2,1,0:T(8,128)}, u32[]{:S(2)}, u32[]{:S(2)}) async-start(f32[32,2,128,128]{3,2,1,0:T(8,128)} %bitcast.98), calls=%async_computation.1 | async-start | bytes 8388608 | tf_op jit(solution)/shard_map/all_to_all | solution.py:168
  84.4 204.4 %reduce-scatter.5.cloned.1.call-start = ((), (), s32[]{:S(2)}) async-start(), calls=%async_computation.6 | async-start | bytes 2359296 | tf_op jit(solution)/shard_map/reduce_scatter | solution.py:194
  107.3 192.6 %reduce-scatter.3.cloned.1.call-start = ((), (), s32[]{:S(2)}) async-start(), calls=%async_computation.5 | async-start | bytes 4718592 | tf_op jit(solution)/shard_map/reduce_scatter | solution.py:193
  194.9 9.0 %copy-start.3 = (f32[2]{0:T(128)S(1)}, f32[2]{0:T(128)}, u32[]{:S(2)}) copy-start(f32[2]{0:T(128)} %constant.105.clone) | copy-start | bytes 28
  248.7 18.7 %slice-start = ((s8[8388608]{0:T(1024)(128)(4,1)}), s8[4194304]{0:T(1024)(128)(4,1)S(1)}, s32[]{:S(2)}) async-start(s8[8388608]{0:T(1024)(128)(4,1)} %bitcast.94), calls=%async_computation.7 | async-start | bytes 8388608
  249.9 17.6 %slice-start.1 = ((s8[8388608]{0:T(1024)(128)(4,1)}), s8[4194304]{0:T(1024)(128)(4,1)S(1)}, s32[]{:S(2)}) async-start(s8[8388608]{0:T(1024)(128)(4,1)} %bitcast.94), calls=%async_computation.8 | async-start | bytes 8388608
  267.5 34.3 %copy-start.1 = (f32[16]{0:T(128)S(1)}, f32[16]{0:T(128)}, u32[]{:S(2)}) copy-start(f32[16]{0:T(128)} %param.16) | copy-start | bytes 196
  279.5 17.9 %all-to-all-start.2 = ((f32[32,1,128]{2,1,0:T(1,128)}), f32[32,1,128]{2,1,0:T(1,128)S(1)}, u32[]{:S(2)}, u32[]{:S(2)}) async-start(f32[32,1,128]{2,1,0:T(1,128)} %reshape.404), calls=%async_computation.2 | async-start | bytes 32768 | tf_op jit(solution)/shard_map/all_to_all | solution.py:180
Sparse Core Ops, SparseCore 0:
  107.4 36.6 reduce-scatter.4
  248.7 38.5 reduce-scatter.2
where the time goes:
time: 314 us; the launch traced here: 309 us
  local copies, waits for them, and re-layouts  94.4 us (30%)
  other arithmetic  85.4 us (27%)
  matrix products  56.9 us (18%)
  starting transfers between devices  31.4 us (10%)
  waiting for transfers between devices  26.1 us (8%)
  between operations  14.6 us (5%)
    mul x1, other arithmetic, particle_terms(): contrast_pair * (spectrum * best_cos[:, None] - swapped * best_sin[:, Non...  20.5 us
    cos x1, other arithmetic, shift_tables(): return (jnp.cos(angles), jnp.sin(angles))  18.8 us
    all_to_all x1, waiting for transfers between devices, body(): lax.all_to_all(send_images, 'cls', split_axis=0, concat_axis=0, tiled=True)  18.5 us
    dot_general x1, matrix products, body(): jnp.einsum('mc,mf->cf', member_flat, weight.reshape(item_count, -1), prec...  17.8 us
    transpose x1, other arithmetic, make_score_table(): shift_cos.reshape(shift_count, -1)  17.5 us
    rev x1, local copies, waits for them, and re-layouts, rotate(): rot_two = jnp.rot90(images, 2, axes=(1, 2))  17.4 us
    mul x1, other arithmetic, owner_terms(): contrast_table(defocus[flat_info[:, 1]], image_side)  16.7 us
    unnamed x20, local copies, waits for them, and re-layouts  12.4 us
  transfers between devices with their start and end apart: 5, of which 2 were waited for; matrix products, arithmetic and copies ran while one was open for 75% of the time, Pallas kernels for 0%

commit v1 on v0

v1 whole, which is shorter than its diff:
```python
import functools
import math

import jax
import jax.numpy as jnp
import numpy as np
from jax import lax
from jax.experimental import pallas as pl
from jax.experimental.pallas import tpu as pltpu
from jax.sharding import PartitionSpec as P

HALF = 72
MIB = 1 << 20


def split_np(table):
    high = table.astype(jnp.bfloat16)
    low = (table - high.astype(np.float32)).astype(jnp.bfloat16)
    return high, low


def split(values):
    high = values.astype(jnp.bfloat16)
    low = (values - high.astype(jnp.float32)).astype(jnp.bfloat16)
    return high, low


def dft_constants(side):
    grid = np.outer(np.arange(side), np.arange(side)) % side
    angles = grid * (2.0 * np.pi / side)
    cos_table = (np.cos(angles) / np.sqrt(side)).astype(np.float32)
    sin_table = (np.sin(angles) / np.sqrt(side)).astype(np.float32)
    rows = side // 2 + 1
    left = np.zeros((2, HALF, side), np.float32)
    left[0, :rows] = cos_table[:rows]
    left[1, :rows] = sin_table[:rows]
    left_high, left_low = split_np(left.reshape(2 * HALF, side))
    left_table = np.concatenate(
        [
            np.concatenate([left_high, left_high], axis=1),
            np.concatenate([left_low, np.zeros_like(left_low)], axis=1),
        ],
        axis=0,
    )
    right = np.block([[cos_table, -sin_table], [-sin_table, -cos_table]]).astype(np.float32)
    right_high, right_low = split_np(right)
    return left_table, right_high, right_low


def turn_constants(side):
    row = np.arange(HALF)[:, None] + 0 * np.arange(side)[None, :]
    col = 0 * np.arange(HALF)[:, None] + np.arange(side)[None, :]
    shifts = np.stack([0 * row, row, row + col, col]) % side
    angles = shifts * (2.0 * np.pi / side)
    return np.concatenate([np.cos(angles), np.sin(angles)], axis=2).astype(np.float32)


def flip_constants(side):
    lanes = np.zeros((side, side), np.float32)
    lanes[(-np.arange(side)) % side, np.arange(side)] = 1.0
    fold = np.zeros((HALF, side), np.float32)
    for u in range(1, side // 2):
        fold[u, side - u] = 1.0
    unfold = np.zeros((side // 2, HALF), np.float32)
    for r in range(side // 2):
        unfold[r, side // 2 - r] = 1.0
    return lanes, fold, unfold


def scatter_kernel(class_local, class_ref, image_ref, slot_ref, count_ref, sems):
    for owner in range(count_ref.shape[0]):
        count_ref[owner] = 0
    copies = []
    for item in range(class_ref.shape[0]):
        owner = lax.div(class_ref[item], class_local)
        rank = count_ref[owner]
        count_ref[owner] = rank + 1
        copy = pltpu.make_async_copy(image_ref.at[item], slot_ref.at[owner * 2 + rank], sems.at[item])
        copy.start()
        copies.append(copy)
    for copy in copies:
        copy.wait()


def place_slots(class_of, particles, owners, class_local):
    count, side, _ = particles.shape
    return pl.pallas_call(
        functools.partial(scatter_kernel, class_local),
        out_shape=jax.ShapeDtypeStruct((owners * 2, side, side), jnp.float32),
        in_specs=[pl.BlockSpec(memory_space=pltpu.SMEM), pl.BlockSpec(memory_space=pl.ANY)],
        out_specs=pl.BlockSpec(memory_space=pl.ANY),
        scratch_shapes=[pltpu.SMEM((owners,), jnp.int32), pltpu.SemaphoreType.DMA((count,))],
        name="place_slots",
    )(class_of, particles)


def pair_step(source, block_at, info_ref, image_ref, ref_ref, contrast_ref, turn_ref, best_ref, left_ref,
              right_high_ref, right_low_ref, col_ref, row_ref, score_ref, numer_ref):
    side = image_ref.shape[-1]
    turns = [info_ref[1, 2 * source + k] for k in range(2)]
    highs, lows = [], []
    for k in range(2):
        image = image_ref[block_at, k]
        odd = lax.rem(turns[k], 2) == 1
        image = jnp.where(odd, image.T, image)
        high, low = split(image)
        highs.append(high)
        lows.append(low)
    stacked = jnp.concatenate(
        [jnp.concatenate(highs, axis=1), jnp.concatenate(lows, axis=1)], axis=0
    )
    halfway = jnp.dot(left_ref[...], stacked, preferred_element_type=jnp.float32)
    halfway = halfway[: 2 * HALF] + halfway[2 * HALF :]
    parts = []
    for k in range(2):
        sign = jnp.where(lax.rem(turns[k], 2) == 1, -1.0, 1.0).astype(jnp.float32)
        lanes = slice(k * side, (k + 1) * side)
        parts.append(jnp.concatenate([halfway[:HALF, lanes], sign * halfway[HALF:, lanes]], axis=1))
    high, low = split(jnp.concatenate(parts, axis=0))
    spectrum = (
        jnp.dot(high, right_high_ref[...], preferred_element_type=jnp.float32)
        + jnp.dot(low, right_high_ref[...], preferred_element_type=jnp.float32)
        + jnp.dot(high, right_low_ref[...], preferred_element_type=jnp.float32)
    )
    products = []
    filtered = []
    for k in range(2):
        slot = 2 * source + k
        rows = slice(k * HALF, (k + 1) * HALF)
        sign = jnp.where(turns[k] >= 2, -1.0, 1.0).astype(jnp.float32)
        real = spectrum[rows, :side]
        imag = sign * spectrum[rows, side:]
        turn = turn_ref[turns[k]]
        contrast = contrast_ref[info_ref[3, slot]]
        turn_real, turn_imag = turn[:, :side], turn[:, side:]
        filt_real = contrast * (real * turn_real - imag * turn_imag)
        filt_imag = contrast * (real * turn_imag + imag * turn_real)
        filtered.append((filt_real, filt_imag))
        ref = ref_ref[info_ref[0, slot]]
        ref_real, ref_imag = ref[:, :side], ref[:, side:]
        products.append(
            jnp.concatenate(
                [
                    filt_real * ref_real + filt_imag * ref_imag,
                    filt_imag * ref_real - filt_real * ref_imag,
                ],
                axis=1,
            )
        )
    high, low = split(jnp.concatenate(products, axis=0))
    by_col = jnp.dot(high, col_ref[...], preferred_element_type=jnp.float32)
    by_col = (
        by_col[:, :side]
        + by_col[:, side:]
        + jnp.dot(low, col_ref[:, :side], preferred_element_type=jnp.float32)
    )
    sums = []
    for k in range(2):
        total = jnp.sum(by_col[k * HALF : (k + 1) * HALF] * row_ref[...], axis=0, keepdims=True)
        sums.append(total + pltpu.roll(total, side // 2, axis=1))
    lane = lax.broadcasted_iota(jnp.int32, (1, side), 1)
    score_ref[pl.ds(source, 1), :] = jnp.where(lane < side // 2, sums[0], sums[1])
    for k in range(2):
        slot = 2 * source + k

        @pl.when(info_ref[4, slot] > 0)
        def _(k=k, slot=slot):
            best = best_ref[info_ref[2, slot]]
            best_real, best_imag = best[:, :side], best[:, side:]
            filt_real, filt_imag = filtered[k]
            local = info_ref[0, slot]
            numer_ref[local, :, :side] += filt_real * best_real - filt_imag * best_imag
            numer_ref[local, :, side:] += filt_real * best_imag + filt_imag * best_real


def owner_kernel(step_sources, info_ref, image_ref, *refs):
    numer_ref = refs[-1]

    @pl.when(pl.program_id(0) == 0)
    def _():
        numer_ref[...] = jnp.zeros_like(numer_ref)

    for at in range(step_sources):
        pair_step(pl.program_id(0) * step_sources + at, at, info_ref, image_ref, *refs)


def owner_terms(info, images, refs, contrast, turn, best, left, right_high, right_low, col, row):
    sources, _, side, _ = images.shape
    step_sources = 4
    whole = lambda x: pl.BlockSpec(x.shape, lambda i: (0,) * x.ndim)
    tables = (refs, contrast, turn, best, left, right_high, right_low, col, row)
    return pl.pallas_call(
        functools.partial(owner_kernel, step_sources),
        grid=(sources // step_sources,),
        out_shape=(
            jax.ShapeDtypeStruct((sources, side), jnp.float32),
            jax.ShapeDtypeStruct((refs.shape[0], HALF, 2 * side), jnp.float32),
        ),
        in_specs=[
            pl.BlockSpec(memory_space=pltpu.SMEM),
            pl.BlockSpec((step_sources, 2, side, side), lambda i: (i, 0, 0, 0)),
        ]
        + [whole(table) for table in tables],
        out_specs=(
            pl.BlockSpec((sources, side), lambda i: (0, 0)),
            pl.BlockSpec((refs.shape[0], HALF, 2 * side), lambda i: (0, 0, 0)),
        ),
        compiler_params=pltpu.CompilerParams(vmem_limit_bytes=40 * MIB),
        name="owner_terms",
    )(info, images, *tables)


def finish_kernel(a_ref, b_ref, c_ref, d_ref, denom_ref, lanes_ref, unfold_ref, out_ref):
    side = out_ref.shape[-1]
    for at in range(out_ref.shape[0]):
        total = (a_ref[at] + b_ref[at]) + (c_ref[at] + d_ref[at])
        for part in range(2):
            ratio = total[:, part * side : (part + 1) * side] / denom_ref[at]
            back = jnp.dot(
                ratio, lanes_ref[...], precision=lax.Precision.HIGHEST, preferred_element_type=jnp.float32
            )
            back = jnp.dot(
                unfold_ref[...], back, precision=lax.Precision.HIGHEST, preferred_element_type=jnp.float32
            )
            out_ref[at, part, : side // 2] = ratio[: side // 2]
            out_ref[at, part, side // 2 :] = back if part == 0 else -back


def finish(blocks, denom, lanes, unfold, side):
    return pl.pallas_call(
        finish_kernel,
        out_shape=jax.ShapeDtypeStruct((denom.shape[0], 2, side, side), jnp.float32),
        compiler_params=pltpu.CompilerParams(vmem_limit_bytes=16 * MIB),
        name="finish",
    )(*blocks, denom, lanes, unfold)


def body(
    particles, references, class_of, rotation_bin, shift_best, defocus_bin, shift_list,
    defocus, chips_y,
):
    side = particles.shape[-1]
    class_local = references.shape[0]
    bins = defocus.shape[0]
    owners = lax.axis_size("cls")
    groups = lax.axis_size("grp")
    me_cls, me_grp = lax.axis_index("cls"), lax.axis_index("grp")
    unit = 2.0 * math.pi / side

    send = place_slots(class_of, particles, owners, class_local)
    images = lax.all_to_all(
        send.reshape(owners, 2, side, side), "cls", split_axis=0, concat_axis=0, tiled=True
    )

    ints = jnp.stack([class_of, rotation_bin, shift_best, defocus_bin])[None]
    everyone = lax.all_gather(ints, ("grp", "cls"), axis=0, tiled=True)

    group = lax.dynamic_slice_in_dim(everyone, me_grp * owners, owners, 0)
    mine = group[:, 0] // class_local == me_cls
    rank = jnp.cumsum(mine.astype(jnp.int32), axis=1) - 1
    chosen = mine[:, None, :] & (rank[:, None, :] == jnp.arange(2, dtype=jnp.int32)[None, :, None])
    fields = jnp.stack(
        [group[:, 0] % class_local, group[:, 1], group[:, 2], group[:, 3], jnp.ones_like(group[:, 0])]
    )
    info = jnp.sum(jnp.where(chosen[None], fields[:, :, None, :], 0), axis=-1).reshape(5, 2 * owners)

    own_classes = class_local // groups
    own = me_cls * class_local + me_grp * own_classes + jnp.arange(own_classes, dtype=jnp.int32)
    flat_class = everyone[:, 0].reshape(-1)
    flat_bin = everyone[:, 3].reshape(-1)
    counts = jnp.sum(
        (
            (flat_class[None, None, :] == own[:, None, None])
            & (flat_bin[None, None, :] == jnp.arange(bins, dtype=jnp.int32)[None, :, None])
        ).astype(jnp.float32),
        axis=-1,
    )

    pixel = jnp.arange(side, dtype=jnp.int32)
    signed = jnp.where(pixel < side // 2, pixel, pixel - side).astype(jnp.float32)
    half = jnp.arange(HALF, dtype=jnp.int32)
    half_signed = jnp.where(half < side // 2, half, half - side).astype(jnp.float32)
    radius = (half_signed[:, None] ** 2 + signed[None, :] ** 2) / float((side // 2) ** 2)
    angle = defocus[:, None, None] * radius[None]
    contrast = -(0.995 * jnp.sin(angle) + 0.1 * jnp.cos(angle))
    denom = 1.0 + jnp.sum(counts[:, :, None, None] * (contrast * contrast)[None], axis=1)

    row_angle = ((half[None, :] * shift_list[:, 0][:, None]) % side).astype(jnp.float32) * unit
    col_angle = ((pixel[None, :] * shift_list[:, 1][:, None]) % side).astype(jnp.float32) * unit
    row_cos, row_sin = jnp.cos(row_angle), jnp.sin(row_angle)
    col_cos, col_sin = jnp.cos(col_angle), jnp.sin(col_angle)
    best = jnp.concatenate(
        [
            row_cos[:, :, None] * col_cos[:, None, :] - row_sin[:, :, None] * col_sin[:, None, :],
            row_sin[:, :, None] * col_cos[:, None, :] + row_cos[:, :, None] * col_sin[:, None, :],
        ],
        axis=2,
    )
    col = jnp.concatenate(
        [
            jnp.concatenate([col_cos.T, col_sin.T], axis=1),
            jnp.concatenate([-col_sin.T, col_cos.T], axis=1),
        ],
        axis=0,
    )
    col_high = lax.reduce_precision(col, exponent_bits=8, mantissa_bits=7)
    col = jnp.concatenate([col_high, col - col_high], axis=1).astype(jnp.bfloat16)
    row = jnp.concatenate([row_cos.T, -row_sin.T], axis=1) / side

    lanes, fold, unfold = flip_constants(side)
    live_rows = (half <= side // 2).astype(jnp.float32)[:, None]
    folded = jnp.einsum("ua,ciab->ciub", fold, references, precision=lax.Precision.HIGH)
    folded = jnp.einsum("ciub,bv->ciuv", folded, lanes, precision=lax.Precision.HIGH)
    top = references[:, :, :HALF] * live_rows
    refs = jnp.concatenate([top[:, 0] + folded[:, 0], top[:, 1] - folded[:, 1]], axis=2)

    left, right_high, right_low = dft_constants(side)
    slot_scores, numer = owner_terms(
        info, images, refs, contrast, jnp.asarray(turn_constants(side)), best, jnp.asarray(left),
        jnp.asarray(right_high), jnp.asarray(right_low), col, row,
    )

    cores = groups // chips_y
    core, me_y = me_grp % cores, me_grp // cores
    parts = numer.reshape(chips_y, cores, own_classes, HALF, 2 * side)
    keep = lax.dynamic_index_in_dim(parts, core, 1, keepdims=False)
    give = lax.dynamic_index_in_dim(parts, 1 - core, 1, keepdims=False)
    got = lax.ppermute(give, "grp", [(i, i ^ 1) for i in range(groups)])
    chip = keep + got
    blocks = [lax.dynamic_index_in_dim(chip, me_y, 0, keepdims=False)]
    for step in range(1, chips_y):
        block = lax.dynamic_index_in_dim(chip, (me_y + step) % chips_y, 0, keepdims=False)
        blocks.append(
            lax.ppermute(
                block,
                "grp",
                [(i, ((i // cores + step) % chips_y) * cores + i % cores) for i in range(groups)],
            )
        )

    home = lax.all_to_all(
        slot_scores.reshape(owners, 1, side), "cls", split_axis=0, concat_axis=0, tiled=True
    ).reshape(2 * owners, side // 2)
    owner_of = class_of // class_local
    earlier = jnp.tril(owner_of[:, None] == owner_of[None, :], -1)
    target = owner_of * 2 + jnp.sum(earlier.astype(jnp.int32), axis=1)
    scores = home[target]

    fresh_refs = finish(blocks, denom, jnp.asarray(lanes), jnp.asarray(unfold), side)
    return (scores, fresh_refs)


def solution(mesh):
    chips_y = mesh.shape["grp"] // 2
    return jax.shard_map(
        functools.partial(body, chips_y=chips_y),
        mesh=mesh,
        in_specs=(
            P(("grp", "cls"), None, None),
            P("cls", None, None, None),
            P(("grp", "cls")),
            P(("grp", "cls")),
            P(("grp", "cls")),
            P(("grp", "cls")),
            P(),
            P(),
        ),
        out_specs=(P(("grp", "cls"), None), P(("cls", "grp"), None, None, None)),
        check_vma=False,
    )
```

time: 314 us -> 314 us (level); the launches traced: 309 us -> 312 us
  blocking collectives: 0 us -> 154 us
  Pallas kernels: 0 us -> 96.9 us
  local copies, waits for them, and re-layouts: 94.4 us -> 8.48 us
  other arithmetic: 85.4 us -> 14.8 us
  matrix products: 56.9 us -> 2.73 us
  waiting for transfers between devices: 26.1 us -> 9.94 us
  between operations: 14.6 us -> 1.23 us
  starting transfers between devices: 31.4 us -> 23.7 us
    all_gather x0 -> x1, blocking collectives: none -> 154 us  [body(): everyone = lax.all_gather(ints, ('grp', 'cls'), axis=0, tiled=True)]
    pallas_call x0 -> x3, Pallas kernels: none -> 96.9 us  [the longest x1 65.6 us: place_slots(): pl.pallas_call(functools.partial(scatter_kernel, class_local), out_shape=...]
    dot_general x4 -> x2, matrix products: 48.1 us -> 2.73 us  [the longest x1 1.65 us: body(): jnp.einsum('ua,ciab->ciub', fold, references, precision=lax.Precision.HIGH)]
    rev x3 -> x0, local copies, waits for them, and re-layouts: 38.9 us -> none  [the longest x1 17.4 us: rotate(): rot_two = jnp.rot90(images, 2, axes=(1, 2))]
    mul x7 -> x2, other arithmetic: 37.7 us -> 5.24 us  [the longest x1 3.19 us: body(): contrast * contrast]
    cos x1 -> x3, other arithmetic: 18.8 us -> 0.59 us  [the longest x2 0.38 us: body(): row_cos, row_sin = (jnp.cos(row_angle), jnp.sin(row_angle))]
    transpose x1 -> x0, other arithmetic: 17.5 us -> none  [make_score_table(): shift_cos.reshape(shift_count, -1)]
    all_to_all x3 -> x2, waiting for transfers between devices: 26 us -> 8.55 us  [the longest x1 8.55 us: body(): lax.all_to_all(slot_scores.reshape(owners, 1, side), 'cls', split_axis=0,...]
  transfers between devices with their start and end apart: 5 -> 6, of which waited for: 2 -> 2; matrix products, arithmetic and copies ran while one was open for 75% -> 6% of each run, Pallas kernels for 0% -> 0%
where the time goes in v1:
time: 314 us; the launch traced here: 312 us
  blocking collectives  154 us (49%)
  Pallas kernels  96.9 us (31%)
  starting transfers between devices  23.7 us (8%)
  other arithmetic  14.8 us (5%)
  waiting for transfers between devices  9.94 us (3%)
  local copies, waits for them, and re-layouts  8.48 us (3%)
    all_gather x1, blocking collectives, body(): everyone = lax.all_gather(ints, ('grp', 'cls'), axis=0, tiled=True)  154 us
    pallas_call x1, Pallas kernels, place_slots(): pl.pallas_call(functools.partial(scatter_kernel, class_local), out_shape=...  65.6 us
    pallas_call x1, Pallas kernels, owner_terms(): pl.pallas_call(functools.partial(owner_kernel, step_sources), grid=(sourc...  28.6 us
    all_to_all x1, starting transfers between devices, body(): lax.all_to_all(send.reshape(owners, 2, side, side), 'cls', split_axis=0,...  12.1 us
    all_to_all x1, waiting for transfers between devices, body(): lax.all_to_all(slot_scores.reshape(owners, 1, side), 'cls', split_axis=0,...  8.55 us
    all_to_all x1, starting transfers between devices, body(): lax.all_to_all(slot_scores.reshape(owners, 1, side), 'cls', split_axis=0,...  6.63 us
  transfers between devices with their start and end apart: 6, of which 2 were waited for; matrix products, arithmetic and copies ran while one was open for 6% of the time, Pallas kernels for 0%

profile of v1, /device:TPU:1, one launch (start us, length us, event | category | flops | bytes accessed | tf_op | source)
XLA Modules:
  0.0 312.1 jit_solution(5061198536194962527)
XLA Ops:
  0.6 65.6 %place_slots.1 = f32[64,128,128]{2,1,0:T(8,128)} custom-call(s32[32]{0:T(128)} %class_ref.1, f32[32,128,128]{2,1,0:T(8,128)} %image_ref.1), custom_call_target="tpu_custom_call" | custom-call | tf_op jit(solution)/shard_map/place_slots/pallas_call | solution.py:87
  66.3 12.1 %all-to-all-start = ((f32[32,2,128,128]{3,2,1,0:T(8,128)}), f32[32,2,128,128]{3,2,1,0:T(8,128)}, u32[]{:S(2)}, u32[]{:S(2)}) async-start(f32[32,2,128,128]{3,2,1,0:T(8,128)} %bitcast.66), calls=%async_computation | async-start | bytes 8388608 | tf_op jit(solution)/shard_map/all_to_all | solution.py:251
  78.5 154.4 %all-gather.1 = s32[256,4,32]{2,1,0:T(4,128)S(1)} all-gather(s32[1,4,32]{2,1,0:T(4,128)S(1)} %add_bitcast_fusion), channel_id=2, replica_groups=mesh['grp'=8,'cls'=32] {'grp','cls'}, dimensions={0}, use_global_device_ids=true | all-gather | bytes 131584 | tf_op jit(solution)/shard_map/all_gather | solution.py:256
  232.9 0.7 slice_reduce_fusion.1
  233.6 0.7 eq.97
  234.4 0.2 reduce_window_sum.14
  234.6 0.7 eq.101
  235.4 0.3 select_reduce_fusion
  235.7 0.1 copy.42
  235.9 0.2 fusion.38
  236.1 0.1 maximum_multiply_fusion.refs_8_
  236.2 0.3 fusion.28
  236.5 0.1 reduce-precision_convert_fusion
  236.6 2.0 copy_multiply_fusion
  238.7 0.8 copy-done.7
  239.5 1.6 convolution_bitcast_fusion
  241.2 1.1 fusion
  242.3 0.2 fusion.3
  242.5 0.2 pad_maximum_fusion.1.refs_0_
  242.7 0.1 add_multiply_fusion
  242.8 0.2 fusion.46
  243.0 0.2 fusion.44
  243.2 1.3 multiply_subtract_fusion
  244.5 2.4 pad_maximum_fusion.refs_3_
  247.0 3.2 %fusion.7 = (f32[16,72,128]{2,1,0:T(8,128)}, f32[16,72,128]{2,1,0:T(8,128)S(1)}) fusion(f32[72,128]{1,0:T(8,128)S(1)} %add_multiply_fusion, f32[16]{0:T(128)S(1)} %copy-done.16), kind=kLoop, calls=%fused_computation.22 | loop fusion | flops 884736 | bytes 1216576 | tf_op jit(solution)/shard_map/mul | solution.py:286
  250.2 0.7 iota_compare_fusion
  250.9 0.9 copy-done.2
  251.8 0.9 copy-done.4
  252.7 28.6 %owner_terms.1 = (f32[32,128]{1,0:T(8,128)}, f32[32,72,256]{2,1,0:T(8,128)S(1)}) custom-call(s32[5,64]{1,0:T(8,128)S(1)} %copy.46.info_ref, f32[32,2,128,128]{3,2,1,0:T(8,128)} %all-to-all-done.image_ref, f32[32,72,256]{2,1,0:T(8,128)S(1)} %pad_maximum_fusion.1.refs_0_, f32[16,72,128]{2,1,0:T(8,128)S(1)} %get-tuple-element.25.refs_1_, ...), custom_call_target="tpu_custom_call" | custom-call | tf_op jit(solution)/shard_map/owner_terms/pallas_call | solution.py:192
  281.3 1.4 copy-done
  282.7 0.1 dynamic-slice_bitcast_fusion
  282.8 3.3 %collective-permute-start = (f32[4,4,72,256]{3,2,1,0:T(8,128)S(1)}, f32[4,4,72,256]{3,2,1,0:T(8,128)S(1)}, u32[]{:S(2)}, u32[]{:S(2)}) collective-permute-start(f32[4,4,72,256]{3,2,1,0:T(8,128)S(1)} %dynamic-slice_bitcast_fusion), channel_id=1, source_target_pairs={{0,32},{32,0},{64,96},{96,64},{128,160},{160,128},{192,224},{224,1... | collective-permute-start | bytes 3538952 | tf_op jit(solution)/shard_map/ppermute | solution.py:328
  286.1 0.1 broadcast_compare_fusion
  286.4 0.2 convert_reduce_fusion.1
  286.6 0.4 convert_reduce_fusion
  286.9 0.2 multiply_reduce_fusion
  287.2 1.4 collective-permute-done
  288.6 1.4 bitcast_add_fusion
  290.0 0.1 dynamic-slice_bitcast_fusion.1
  290.1 0.6 collective-permute-start.3
  290.7 1.0 collective-permute-start.1
  291.7 6.6 %all-to-all-start.1 = ((f32[32,1,128]{2,1,0:T(1,128)}), f32[32,1,128]{2,1,0:T(1,128)S(1)}, u32[]{:S(2)}, u32[]{:S(2)}) async-start(f32[32,1,128]{2,1,0:T(1,128)} %bitcast.21), calls=%async_computation.1 | async-start | bytes 32768 | tf_op jit(solution)/shard_map/all_to_all | solution.py:341
  298.3 8.5 %all-to-all-done.1 = f32[32,1,128]{2,1,0:T(1,128)S(1)} async-done(((f32[32,1,128]{2,1,0:T(1,128)}), f32[32,1,128]{2,1,0:T(1,128)S(1)}, u32[]{:S(2)}, u32[]{:S(2)}) %all-to-all-start.1) | async-done | bytes 16416 | tf_op jit(solution)/shard_map/all_to_all | solution.py:341
  306.9 0.5 broadcast.432
  307.4 0.7 reduce.11
  308.1 0.1 reshape.324
  308.2 1.2 gather_fusion
  309.4 2.7 finish.1
  (63 shorter events, 0.4 us)
Async XLA Ops:
  66.2 12.2 %copy-start.14 = (s32[32]{0:T(128)S(1)}, s32[32]{0:T(128)}, u32[]{:S(2)}) copy-start(s32[32]{0:T(128)} %class_ref.1) | copy-start | bytes 388
  66.2 12.2 %copy-start.17 = (s32[32]{0:T(128)S(1)}, s32[32]{0:T(128)}, u32[]{:S(2)}) copy-start(s32[32]{0:T(128)} %param.21) | copy-start | bytes 388
  66.3 12.2 %copy-start.18 = (s32[32]{0:T(128)S(1)}, s32[32]{0:T(128)}, u32[]{:S(2)}) copy-start(s32[32]{0:T(128)} %param.20) | copy-start | bytes 388
  66.3 12.2 %copy-start.19 = (s32[32]{0:T(128)S(1)}, s32[32]{0:T(128)}, u32[]{:S(2)}) copy-start(s32[32]{0:T(128)} %param.19) | copy-start | bytes 388
  66.3 169.6 %copy-start.15 = (s32[64,2]{0,1:T(2,128)S(1)}, s32[64,2]{0,1:T(2,128)}, u32[]{:S(2)}) copy-start(s32[64,2]{0,1:T(2,128)} %param.22) | copy-start | bytes 1540
  66.3 184.6 %all-to-all-start = ((f32[32,2,128,128]{3,2,1,0:T(8,128)}), f32[32,2,128,128]{3,2,1,0:T(8,128)}, u32[]{:S(2)}, u32[]{:S(2)}) async-start(f32[32,2,128,128]{3,2,1,0:T(8,128)} %bitcast.66), calls=%async_computation | async-start | bytes 8388608 | tf_op jit(solution)/shard_map/all_to_all | solution.py:251
  236.6 2.9 copy-start.7
  236.6 2.9 copy-start.13
  239.5 1.7 copy-start.12
  244.5 2.5 copy-start.16
  244.5 5.7 %copy-start.10 = (s32[8192]{0:T(1024)S(1)}, s32[8192]{0:T(1024)}, u32[]{:S(2)}) copy-start(s32[8192]{0:T(1024)} %eq.101) | copy-start | bytes 98308
  244.5 6.4 %copy-start.1 = (f32[4,72,256]{2,1,0:T(8,128)S(1)}, f32[4,72,256]{2,1,0:T(8,128)}, u32[]{:S(2)}) copy-start(f32[4,72,256]{2,1,0:T(8,128)} %constant.188.clone.refs_2_) | copy-start | bytes 884740
  244.5 6.4 %copy-start.3 = (bf16[256,256]{1,0:T(8,128)(2,1)S(1)}, bf16[256,256]{1,0:T(8,128)(2,1)}, u32[]{:S(2)}) copy-start(bf16[256,256]{1,0:T(8,128)(2,1)} %constant.191.clone.refs_6_) | copy-start | bytes 393220
  250.9 0.9 copy-start.2
  251.8 0.9 copy-start.4
  281.3 1.4 copy-start
  281.3 4.9 %copy-start.11 = (s32[8192]{0:T(1024)S(1)}, s32[8192]{0:T(1024)}, u32[]{:S(2)}) copy-start(s32[8192]{0:T(1024)} %eq.97) | copy-start | bytes 98308
  281.3 5.3 %copy-start.9 = (pred[16,8192]{1,0:T(8,128)(4,1)S(1)}, pred[16,8192]{1,0:T(8,128)(4,1)}, u32[]{:S(2)}) copy-start(pred[16,8192]{1,0:T(8,128)(4,1)} %iota_compare_fusion) | copy-start | bytes 393220
  281.3 5.7 %copy-start.8 = (f32[16,72,128]{2,1,0:T(8,128)S(1)}, f32[16,72,128]{2,1,0:T(8,128)}, u32[]{:S(2)}) copy-start(f32[16,72,128]{2,1,0:T(8,128)} %get-tuple-element.24) | copy-start | bytes 1769476
  282.8 5.8 %collective-permute-start = (f32[4,4,72,256]{3,2,1,0:T(8,128)S(1)}, f32[4,4,72,256]{3,2,1,0:T(8,128)S(1)}, u32[]{:S(2)}, u32[]{:S(2)}) collective-permute-start(f32[4,4,72,256]{3,2,1,0:T(8,128)S(1)} %dynamic-slice_bitcast_fusion), channel_id=1, source_target_pairs={{0,32},{32,0},{64,96},{96,64},{128,160},{160,128},{192,224},{224,1... | collective-permute-start | bytes 3538952 | tf_op jit(solution)/shard_map/ppermute | solution.py:328
  287.2 22.1 %copy-start.5 = (f32[128,128]{1,0:T(8,128)S(1)}, f32[128,128]{1,0:T(8,128)}, u32[]{:S(2)}) copy-start(f32[128,128]{1,0:T(8,128)} %constant.187.clone.lanes_ref) | copy-start | bytes 196612
  287.2 22.1 %copy-start.6 = (f32[64,72]{1,0:T(8,128)S(1)}, f32[64,72]{1,0:T(8,128)}, u32[]{:S(2)}) copy-start(f32[64,72]{1,0:T(8,128)} %constant.192.clone.unfold_ref) | copy-start | bytes 55300
  290.1 19.2 %collective-permute-start.3 = (f32[4,72,256]{2,1,0:T(8,128)S(1)}, f32[4,72,256]{2,1,0:T(8,128)S(1)}, u32[]{:S(2)}, u32[]{:S(2)}) collective-permute-start(f32[4,72,256]{2,1,0:T(8,128)S(1)} %get-tuple-element.12), channel_id=1, source_target_pairs={{0,192},{32,224},{64,0},{96,32},{128,64},{160,96},{192,128},{224,1... | collective-permute-start | bytes 884744 | tf_op jit(solution)/shard_map/ppermute | solution.py:334
  290.7 18.6 %collective-permute-start.2 = (f32[4,72,256]{2,1,0:T(8,128)S(1)}, f32[4,72,256]{2,1,0:T(8,128)S(1)}, u32[]{:S(2)}, u32[]{:S(2)}) collective-permute-start(f32[4,72,256]{2,1,0:T(8,128)S(1)} %get-tuple-element.13), channel_id=1, source_target_pairs={{0,128},{32,160},{64,192},{96,224},{128,0},{160,32},{192,64},{224,... | collective-permute-start | bytes 884744 | tf_op jit(solution)/shard_map/ppermute | solution.py:334
  290.7 18.6 %collective-permute-start.1 = (f32[4,72,256]{2,1,0:T(8,128)S(1)}, f32[4,72,256]{2,1,0:T(8,128)S(1)}, u32[]{:S(2)}, u32[]{:S(2)}) collective-permute-start(f32[4,72,256]{2,1,0:T(8,128)S(1)} %get-tuple-element.14), channel_id=1, source_target_pairs={{0,64},{32,96},{64,128},{96,160},{128,192},{160,224},{192,0},{224,... | collective-permute-start | bytes 884744 | tf_op jit(solution)/shard_map/ppermute | solution.py:334
  291.7 15.2 %all-to-all-start.1 = ((f32[32,1,128]{2,1,0:T(1,128)}), f32[32,1,128]{2,1,0:T(1,128)S(1)}, u32[]{:S(2)}, u32[]{:S(2)}) async-start(f32[32,1,128]{2,1,0:T(1,128)} %bitcast.21), calls=%async_computation.1 | async-start | bytes 32768 | tf_op jit(solution)/shard_map/all_to_all | solution.py:341

commit v2 on v1

v2 whole, which is shorter than its diff:
```python
import functools
import math

import jax
import jax.numpy as jnp
import numpy as np
from jax import lax
from jax.experimental import pallas as pl
from jax.experimental.pallas import tpu as pltpu
from jax.sharding import PartitionSpec as P

HALF = 72
TAG = 8
COUNT = HALF - 1
MIB = 1 << 20


def split_np(table):
    high = table.astype(jnp.bfloat16)
    low = (table - high.astype(np.float32)).astype(jnp.bfloat16)
    return high, low


def split(values):
    high = values.astype(jnp.bfloat16)
    low = (values - high.astype(jnp.float32)).astype(jnp.bfloat16)
    return high, low


def dft_constants(side):
    grid = np.outer(np.arange(side), np.arange(side)) % side
    angles = grid * (2.0 * np.pi / side)
    cos_table = (np.cos(angles) / np.sqrt(side)).astype(np.float32)
    sin_table = (np.sin(angles) / np.sqrt(side)).astype(np.float32)
    rows = side // 2 + 1
    left = np.zeros((2, HALF, side), np.float32)
    left[0, :rows] = cos_table[:rows]
    left[1, :rows] = sin_table[:rows]
    left_high, left_low = split_np(left.reshape(2 * HALF, side))
    left_table = np.concatenate(
        [
            np.concatenate([left_high, left_high], axis=1),
            np.concatenate([left_low, np.zeros_like(left_low)], axis=1),
        ],
        axis=0,
    )
    right = np.block([[cos_table, -sin_table], [-sin_table, -cos_table]]).astype(np.float32)
    right_high, right_low = split_np(right)
    return left_table, np.concatenate([right_high, right_high, right_low], axis=0)


def turn_constants(side):
    row = np.arange(HALF)[:, None] + 0 * np.arange(side)[None, :]
    col = 0 * np.arange(HALF)[:, None] + np.arange(side)[None, :]
    shifts = np.stack([0 * row, row, row + col, col]) % side
    angles = shifts * (2.0 * np.pi / side)
    return np.concatenate([np.cos(angles), np.sin(angles)], axis=2).astype(np.float32)


def flip_constants(side):
    lanes = np.zeros((side, side), np.float32)
    lanes[(-np.arange(side)) % side, np.arange(side)] = 1.0
    fold = np.zeros((HALF, side), np.float32)
    for u in range(1, side // 2):
        fold[u, side - u] = 1.0
    unfold = np.zeros((side // 2, HALF), np.float32)
    for r in range(side // 2):
        unfold[r, side // 2 - r] = 1.0
    return lanes, fold, unfold


def scatter_kernel(class_local, class_ref, turn_ref, shift_ref, bin_ref, image_ref, slot_ref,
                   count_ref, hold_ref, tag_ref, in_sems, out_sems, tag_sem):
    items, side, _ = hold_ref.shape
    loads = []
    for item in range(items):
        load = pltpu.make_async_copy(image_ref.at[item], hold_ref.at[item], in_sems.at[item])
        load.start()
        loads.append(load)
    for owner in range(count_ref.shape[0]):
        count_ref[owner] = 0
    tag_ref[...] = jnp.zeros_like(tag_ref)
    lane = lax.broadcasted_iota(jnp.int32, (1, side), 1)
    stores = []
    for item in range(items):
        owner = lax.div(class_ref[item], class_local)
        rank = count_ref[owner]
        count_ref[owner] = rank + 1
        loads[item].wait()
        store = pltpu.make_async_copy(
            hold_ref.at[item],
            slot_ref.at[owner, pl.ds(pl.multiple_of(rank * side, side), side), :],
            out_sems.at[item],
        )
        store.start()
        stores.append(store)
        fields = (class_ref[item] - owner * class_local, turn_ref[item], shift_ref[item], bin_ref[item], 1)
        tag = jnp.zeros((1, side), jnp.int32)
        for at, value in enumerate(fields):
            tag = jnp.where(lane == at, value, tag)
        tag_ref[owner, pl.ds(rank, 1), :] = tag.astype(jnp.float32)
    store = pltpu.make_async_copy(tag_ref, slot_ref.at[:, pl.ds(2 * side, TAG), :], tag_sem)
    store.start()
    stores.append(store)
    for store in stores:
        store.wait()


def place_slots(particles, class_of, rotation_bin, shift_best, defocus_bin, owners, class_local):
    count, side, _ = particles.shape
    return pl.pallas_call(
        functools.partial(scatter_kernel, class_local),
        out_shape=jax.ShapeDtypeStruct((owners, 2 * side + TAG, side), jnp.float32),
        in_specs=[pl.BlockSpec(memory_space=pltpu.SMEM)] * 4 + [pl.BlockSpec(memory_space=pltpu.HBM)],
        out_specs=pl.BlockSpec(memory_space=pltpu.HBM),
        scratch_shapes=[
            pltpu.SMEM((owners,), jnp.int32),
            pltpu.VMEM((count, side, side), jnp.float32),
            pltpu.VMEM((owners, TAG, side), jnp.float32),
            pltpu.SemaphoreType.DMA((count,)),
            pltpu.SemaphoreType.DMA((count,)),
            pltpu.SemaphoreType.DMA,
        ],
        compiler_params=pltpu.CompilerParams(vmem_limit_bytes=16 * MIB),
        name="place_slots",
    )(class_of, rotation_bin, shift_best, defocus_bin, particles)


def spectrum_kernel(step_sources, info_ref, image_ref, contrast_ref, turn_ref, best_ref, left_ref, right_ref,
                    keep_ref, give_ref, filt_ref, numer_ref, sems):
    side = image_ref.shape[-1]
    first = pl.program_id(0) * step_sources * 2
    lane = lax.broadcasted_iota(jnp.int32, (1, side), 1)

    @pl.when(pl.program_id(0) == 0)
    def _():
        numer_ref[...] = jnp.zeros_like(numer_ref)

    turns = [info_ref[1, first + item] for item in range(2 * step_sources)]
    parts = []
    for at in range(step_sources):
        highs, lows = [], []
        for k in range(2):
            image = image_ref[at, k * side : (k + 1) * side]
            odd = lax.rem(turns[2 * at + k], 2) == 1
            high, low = split(jnp.where(odd, image.T, image))
            highs.append(high)
            lows.append(low)
        stacked = jnp.concatenate(
            [jnp.concatenate(highs, axis=1), jnp.concatenate(lows, axis=1)], axis=0
        )
        halfway = jnp.dot(left_ref[...], stacked, preferred_element_type=jnp.float32)
        halfway = halfway[: 2 * HALF] + halfway[2 * HALF :]
        for k in range(2):
            odd = lax.rem(turns[2 * at + k], 2) == 1
            sign = jnp.where(odd, -1.0, 1.0).astype(jnp.float32)
            lanes = slice(k * side, (k + 1) * side)
            parts.append(
                jnp.concatenate([halfway[:HALF, lanes], sign * halfway[HALF:, lanes]], axis=1)
            )
    high, low = split(jnp.concatenate(parts, axis=0))
    spectrum = jnp.dot(
        jnp.concatenate([high, low, high], axis=1), right_ref[...], preferred_element_type=jnp.float32
    )
    for item in range(2 * step_sources):
        slot = first + item
        rows = slice(item * HALF, (item + 1) * HALF)
        sign = jnp.where(turns[item] >= 2, -1.0, 1.0).astype(jnp.float32)
        real = spectrum[rows, :side]
        imag = sign * spectrum[rows, side:]
        turn = turn_ref[turns[item]]
        contrast = contrast_ref[info_ref[3, slot]]
        turn_real, turn_imag = turn[:, :side], turn[:, side:]
        filt_real = contrast * (real * turn_real - imag * turn_imag)
        filt_imag = contrast * (real * turn_imag + imag * turn_real)
        filt_ref[item, :, :side] = filt_real
        filt_ref[item, :, side:] = filt_imag

        @pl.when(info_ref[4, slot] > 0)
        def _(slot=slot, filt_real=filt_real, filt_imag=filt_imag):
            best = best_ref[info_ref[2, slot]]
            best_real, best_imag = best[:, :side], best[:, side:]
            target = info_ref[5, slot]
            numer_ref[target, :, :side] += filt_real * best_real - filt_imag * best_imag
            numer_ref[target, :, side:] += filt_real * best_imag + filt_imag * best_real
            hit = (lane == info_ref[3, slot]).astype(jnp.float32)
            numer_ref[target, COUNT : COUNT + 1, :side] += hit

    @pl.when(pl.program_id(0) == pl.num_programs(0) - 1)
    def _():
        half = numer_ref.shape[0] // 2
        copies = [
            pltpu.make_async_copy(numer_ref.at[pl.ds(half, half)], give_ref, sems.at[0]),
            pltpu.make_async_copy(numer_ref.at[pl.ds(0, half)], keep_ref, sems.at[1]),
        ]
        for copy in copies:
            copy.start()
        for copy in copies:
            copy.wait()


def score_kernel(step_sources, info_ref, filt_ref, ref_ref, col_ref, row_ref, score_ref):
    side = score_ref.shape[-1]
    first = pl.program_id(0) * step_sources * 2
    products = []
    for item in range(2 * step_sources):
        ref = ref_ref[info_ref[0, first + item]]
        ref_real, ref_imag = ref[:, :side], ref[:, side:]
        filt_real, filt_imag = filt_ref[item, :, :side], filt_ref[item, :, side:]
        products.append(
            jnp.concatenate(
                [
                    filt_real * ref_real + filt_imag * ref_imag,
                    filt_imag * ref_real - filt_real * ref_imag,
                ],
                axis=1,
            )
        )
    high, low = split(jnp.concatenate(products, axis=0))
    by_col = jnp.dot(
        jnp.concatenate([high, low], axis=1), col_ref[...], preferred_element_type=jnp.float32
    )
    by_col = by_col[:, :side] + by_col[:, side:]
    lane = lax.broadcasted_iota(jnp.int32, (1, side), 1)
    for at in range(step_sources):
        sums = []
        for k in range(2):
            item = 2 * at + k
            total = jnp.sum(
                by_col[item * HALF : (item + 1) * HALF] * row_ref[...], axis=0, keepdims=True
            )
            sums.append(total + pltpu.roll(total, side // 2, axis=1))
        score_ref[at] = jnp.where(lane < side // 2, sums[0], sums[1])


def owner_spectra(info, images, contrast, turn, best, left, right, class_local):
    sources, _, side = images.shape
    step_sources = 4
    whole = lambda x: pl.BlockSpec(x.shape, lambda i: (0,) * x.ndim)
    tables = (contrast, turn, best, left, right)
    half = jax.ShapeDtypeStruct((class_local // 2, HALF, 2 * side), jnp.float32)
    return pl.pallas_call(
        functools.partial(spectrum_kernel, step_sources),
        grid=(sources // step_sources,),
        out_shape=(
            half,
            half,
            jax.ShapeDtypeStruct((2 * sources, HALF, 2 * side), jnp.float32),
        ),
        in_specs=[
            pl.BlockSpec(memory_space=pltpu.SMEM),
            pl.BlockSpec((step_sources, 2 * side, side), lambda i: (i, 0, 0)),
        ]
        + [whole(table) for table in tables],
        out_specs=(
            pl.BlockSpec(memory_space=pltpu.HBM),
            pl.BlockSpec(memory_space=pltpu.HBM),
            pl.BlockSpec((2 * step_sources, HALF, 2 * side), lambda i: (i, 0, 0)),
        ),
        scratch_shapes=[
            pltpu.VMEM((class_local, HALF, 2 * side), jnp.float32),
            pltpu.SemaphoreType.DMA((2,)),
        ],
        compiler_params=pltpu.CompilerParams(vmem_limit_bytes=32 * MIB),
        name="owner_spectra",
    )(info, images, *tables)


def owner_scores(info, filtered, refs, col, row):
    items, _, wide = filtered.shape
    step_sources = 4
    whole = lambda x: pl.BlockSpec(x.shape, lambda i: (0,) * x.ndim)
    return pl.pallas_call(
        functools.partial(score_kernel, step_sources),
        grid=(items // 2 // step_sources,),
        out_shape=jax.ShapeDtypeStruct((items // 2, 1, wide // 2), jnp.float32),
        in_specs=[
            pl.BlockSpec(memory_space=pltpu.SMEM),
            pl.BlockSpec((2 * step_sources, HALF, wide), lambda i: (i, 0, 0)),
            whole(refs), whole(col), whole(row),
        ],
        out_specs=pl.BlockSpec((step_sources, 1, wide // 2), lambda i: (i, 0, 0)),
        compiler_params=pltpu.CompilerParams(vmem_limit_bytes=24 * MIB),
        name="owner_scores",
    )(info, filtered, refs, col, row)


def finish_kernel(mine_ref, a_ref, b_ref, c_ref, square_ref, lanes_ref, unfold_ref, out_ref):
    side = out_ref.shape[-1]
    for at in range(out_ref.shape[0]):
        total = (mine_ref[at] + a_ref[at]) + (b_ref[at] + c_ref[at])
        weight = jnp.zeros((HALF, side), jnp.float32)
        for which in range(square_ref.shape[0]):
            weight += total[COUNT : COUNT + 1, which : which + 1] * square_ref[which]
        inverse = 1.0 / (weight + 1.0)
        for part in range(2):
            ratio = total[:, part * side : (part + 1) * side] * inverse
            back = jnp.dot(
                ratio, lanes_ref[...], precision=lax.Precision.HIGHEST, preferred_element_type=jnp.float32
            )
            back = jnp.dot(
                unfold_ref[...], back, precision=lax.Precision.HIGHEST, preferred_element_type=jnp.float32
            )
            out_ref[at, part, : side // 2] = ratio[: side // 2]
            out_ref[at, part, side // 2 :] = back if part == 0 else -back


def finish(blocks, square, lanes, unfold, side):
    return pl.pallas_call(
        finish_kernel,
        out_shape=jax.ShapeDtypeStruct((blocks[0].shape[0], 2, side, side), jnp.float32),
        compiler_params=pltpu.CompilerParams(vmem_limit_bytes=16 * MIB),
        name="finish",
    )(*blocks, square, lanes, unfold)


def pick_kernel(target_ref, home_ref, out_ref):
    items, shifts = out_ref.shape
    for item in range(items):
        target = target_ref[item]
        row = home_ref[lax.div(target, 2)]
        row = jnp.where(lax.rem(target, 2) == 1, pltpu.roll(row, shifts, axis=1), row)
        out_ref[item : item + 1, :] = row[:, :shifts]


def pick(target, home):
    return pl.pallas_call(
        pick_kernel,
        out_shape=jax.ShapeDtypeStruct((target.shape[0], home.shape[-1] // 2), jnp.float32),
        in_specs=[pl.BlockSpec(memory_space=pltpu.SMEM), pl.BlockSpec(memory_space=pltpu.VMEM)],
        compiler_params=pltpu.CompilerParams(vmem_limit_bytes=16 * MIB),
        name="pick",
    )(target, home)


def body(
    particles, references, class_of, rotation_bin, shift_best, defocus_bin, shift_list,
    defocus, chips_y,
):
    side = particles.shape[-1]
    class_local = references.shape[0]
    owners = lax.axis_size("cls")
    groups = lax.axis_size("grp")
    me_grp = lax.axis_index("grp")
    unit = 2.0 * math.pi / side

    send = place_slots(
        particles, class_of, rotation_bin, shift_best, defocus_bin, owners, class_local
    )
    images = lax.all_to_all(send, "cls", split_axis=0, concat_axis=0, tiled=True)

    cores = groups // chips_y
    core, me_y = me_grp % cores, me_grp // cores
    own_classes = class_local // groups
    tags = images[:, 2 * side : 2 * side + 2, :5].astype(jnp.int32).reshape(2 * owners, 5)
    local = tags[:, 0]
    place = local // own_classes
    target = (
        ((place % cores - core) % cores) * chips_y + (place // cores - me_y) % chips_y
    ) * own_classes + local % own_classes
    info = jnp.concatenate([tags, target[:, None]], axis=1).T

    pixel = jnp.arange(side, dtype=jnp.int32)
    signed = jnp.where(pixel < side // 2, pixel, pixel - side).astype(jnp.float32)
    half = jnp.arange(HALF, dtype=jnp.int32)
    half_signed = jnp.where(half < side // 2, half, half - side).astype(jnp.float32)
    radius = (half_signed[:, None] ** 2 + signed[None, :] ** 2) / float((side // 2) ** 2)
    angle = defocus[:, None, None] * radius[None]
    contrast = -(0.995 * jnp.sin(angle) + 0.1 * jnp.cos(angle))

    row_angle = ((half[None, :] * shift_list[:, 0][:, None]) % side).astype(jnp.float32) * unit
    col_angle = ((pixel[None, :] * shift_list[:, 1][:, None]) % side).astype(jnp.float32) * unit
    row_cos, row_sin = jnp.cos(row_angle), jnp.sin(row_angle)
    col_cos, col_sin = jnp.cos(col_angle), jnp.sin(col_angle)
    best = jnp.concatenate(
        [
            row_cos[:, :, None] * col_cos[:, None, :] - row_sin[:, :, None] * col_sin[:, None, :],
            row_sin[:, :, None] * col_cos[:, None, :] + row_cos[:, :, None] * col_sin[:, None, :],
        ],
        axis=2,
    )
    col = jnp.concatenate(
        [
            jnp.concatenate([col_cos.T, col_sin.T], axis=1),
            jnp.concatenate([-col_sin.T, col_cos.T], axis=1),
        ],
        axis=0,
    )
    col_high = lax.reduce_precision(col, exponent_bits=8, mantissa_bits=7)
    col = jnp.concatenate([col_high, col - col_high], axis=1).astype(jnp.bfloat16)
    col = jnp.concatenate([col, col], axis=0)
    row = jnp.concatenate([row_cos.T, -row_sin.T], axis=1) / side

    lanes, fold, unfold = flip_constants(side)
    live_rows = (half <= side // 2).astype(jnp.float32)[:, None]
    folded = jnp.einsum("ua,ciab->ciub", fold, references, precision=lax.Precision.HIGH)
    folded = jnp.einsum("ciub,bv->ciuv", folded, lanes, precision=lax.Precision.HIGH)
    top = references[:, :, :HALF] * live_rows
    refs = jnp.concatenate([top[:, 0] + folded[:, 0], top[:, 1] - folded[:, 1]], axis=2)

    left, right = dft_constants(side)
    keep, give, filtered = owner_spectra(
        info, images, contrast, jnp.asarray(turn_constants(side)), best, jnp.asarray(left),
        jnp.asarray(right), class_local,
    )
    slot_scores = owner_scores(info, filtered, refs, col, row)

    got = lax.ppermute(give, "grp", [(i, i ^ 1) for i in range(groups)])
    blocks = []
    for step in range(chips_y):
        part = slice(step * own_classes, (step + 1) * own_classes)
        block = keep[part] + got[part]
        pairs = [(i, ((i // cores + step) % chips_y) * cores + i % cores) for i in range(groups)]
        blocks.append(lax.ppermute(block, "grp", pairs) if step else block)

    home = lax.all_to_all(slot_scores, "cls", split_axis=0, concat_axis=0, tiled=True)
    owner_of = class_of // class_local
    earlier = jnp.tril(owner_of[:, None] == owner_of[None, :], -1)
    scores = pick(owner_of * 2 + jnp.sum(earlier.astype(jnp.int32), axis=1), home)

    fresh_refs = finish(
        blocks, contrast * contrast, jnp.asarray(lanes), jnp.asarray(unfold), side
    )
    return (scores, fresh_refs)


def solution(mesh):
    chips_y = mesh.shape["grp"] // 2
    return jax.shard_map(
        functools.partial(body, chips_y=chips_y),
        mesh=mesh,
        in_specs=(
            P(("grp", "cls"), None, None),
            P("cls", None, None, None),
            P(("grp", "cls")),
            P(("grp", "cls")),
            P(("grp", "cls")),
            P(("grp", "cls")),
            P(),
            P(),
        ),
        out_specs=(P(("grp", "cls"), None), P(("cls", "grp"), None, None, None)),
        check_vma=False,
    )
```

time: 314 us -> 172 us (0.55)
  blocking collectives: 154 us -> 0 us
  waiting for transfers between devices: 9.94 us -> 92.4 us
  Pallas kernels: 96.9 us -> 26.6 us
  other arithmetic: 14.8 us -> 10.7 us
  starting transfers between devices: 23.7 us -> 27.3 us
    all_gather x1 -> x0, blocking collectives: 154 us -> none  [body(): everyone = lax.all_gather(ints, ('grp', 'cls'), axis=0, tiled=True)]
    all_to_all x2, waiting for transfers between devices: 8.55 us -> 92.3 us  [the longest x1 83.8 us: body(): lax.all_to_all(send, 'cls', split_axis=0, concat_axis=0, tiled=True)]
    pallas_call x1, Pallas kernels: 65.6 us -> 7.03 us  [place_slots(): pl.pallas_call(functools.partial(scatter_kernel, class_local), out_shape=...]
    pallas_call x2 -> x4, Pallas kernels: 31.3 us -> 19.5 us  [the longest x1 10.3 us: owner_spectra(): pl.pallas_call(functools.partial(spectrum_kernel, step_sources), grid=(so...]
    unnamed x43 -> x40, local copies, waits for them, and re-layouts: 4.16 us -> 9.29 us
    ppermute x3, starting transfers between devices: 1.55 us -> 5.2 us  [body(): blocks.append(lax.ppermute(block, 'grp', pairs) if step else block)]
  transfers between devices with their start and end apart: 6 -> 6, of which waited for: 2 -> 2; matrix products, arithmetic and copies ran while one was open for 6% -> 8% of each run, Pallas kernels for 0% -> 4%
where the time goes in v2:
time: 172 us; the launch traced here: 171 us
  waiting for transfers between devices  92.4 us (54%)
  starting transfers between devices  27.3 us (16%)
  Pallas kernels  26.6 us (15%)
  other arithmetic  10.7 us (6%)
  local copies, waits for them, and re-layouts  9.36 us (5%)
  matrix products  3.88 us (2%)
    all_to_all x1, waiting for transfers between devices, body(): lax.all_to_all(send, 'cls', split_axis=0, concat_axis=0, tiled=True)  83.8 us
    all_to_all x1, starting transfers between devices, body(): lax.all_to_all(send, 'cls', split_axis=0, concat_axis=0, tiled=True)  12.1 us
    pallas_call x1, Pallas kernels, owner_spectra(): pl.pallas_call(functools.partial(spectrum_kernel, step_sources), grid=(so...  10.3 us
    unnamed x40, local copies, waits for them, and re-layouts  9.29 us
    all_to_all x1, waiting for transfers between devices, body(): lax.all_to_all(slot_scores, 'cls', split_axis=0, concat_axis=0, tiled=True)  8.54 us
    pallas_call x1, Pallas kernels, place_slots(): pl.pallas_call(functools.partial(scatter_kernel, class_local), out_shape=...  7.03 us
    ppermute x1, starting transfers between devices, body(): got = lax.ppermute(give, 'grp', [(i, i ^ 1) for i in range(groups)])  5.47 us
    ppermute x3, starting transfers between devices, body(): blocks.append(lax.ppermute(block, 'grp', pairs) if step else block)  5.2 us
  transfers between devices with their start and end apart: 6, of which 2 were waited for; matrix products, arithmetic and copies ran while one was open for 8% of the time, Pallas kernels for 4%

profile of v2, /device:TPU:1, one launch (start us, length us, event | category | flops | bytes accessed | tf_op | source)
XLA Modules:
  0.0 171.2 jit_solution(15189778869453934009)
XLA Ops:
  0.6 1.6 copy-done.2
  2.2 0.7 copy-done.8
  2.9 0.7 copy-done.9
  3.5 0.7 copy-done.10
  4.2 0.7 copy-done.11
  4.8 7.0 %place_slots.1 = f32[32,264,128]{2,1,0:T(8,128)S(1)} custom-call(s32[32]{0:T(128)S(1)} %copy-done.11, s32[32]{0:T(128)S(1)} %copy-done.8, s32[32]{0:T(128)S(1)} %copy-done.9, s32[32]{0:T(128)S(1)} %copy-done.10, f32[32,128,128]{2,1,0:T(8,128)S(1)} %copy-done.2), custom_call_target="tpu_custom_call" | custom-call | tf_op jit(solution)/shard_map/place_slots/pallas_call | solution.py:111
  11.9 2.1 %copy-done.1 = f32[32,264,128]{2,1,0:T(8,128)} copy-done((f32[32,264,128]{2,1,0:T(8,128)}, f32[32,264,128]{2,1,0:T(8,128)S(1)}, u32[]{:S(2)}) %copy-start.1) | copy-done | bytes 4325400
  14.0 12.1 %all-to-all-start = ((f32[32,264,128]{2,1,0:T(8,128)}), f32[32,264,128]{2,1,0:T(8,128)}, u32[]{:S(2)}, u32[]{:S(2)}) async-start(f32[32,264,128]{2,1,0:T(8,128)} %copy-done.1), calls=%async_computation | async-start | bytes 8650752 | tf_op jit(solution)/shard_map/all_to_all | solution.py:350
  26.2 0.3 fusion.28
  26.5 0.1 reduce-precision_convert_fusion
  26.7 0.1 add_multiply_fusion
  26.8 0.2 fusion.39
  27.0 0.2 fusion.41
  27.2 1.3 multiply_subtract_fusion
  28.5 0.0 copy-start.19
  28.5 0.0 copy-start.13
  28.5 2.7 %pad_maximum_fusion.best_ref = f32[64,72,256]{2,1,0:T(8,128)} fusion(f32[64,72,128]{2,1,0:T(8,128)S(1)} %get-tuple-element.17, f32[64,72,128]{2,1,0:T(8,128)S(1)} %get-tuple-element.16), kind=kLoop, calls=%fused_computation | loop fusion | flops 1179648 | bytes 9437184 | tf_op jit(solution)/shard_map/concatenate | solution.py:375
  31.2 2.2 %fusion.7 = (f32[16,72,128]{2,1,0:T(8,128)S(1)}, f32[16,72,128]{2,1,0:T(8,128)S(1)}) fusion(f32[72,128]{1,0:T(8,128)S(1)} %add_multiply_fusion, f32[16]{0:T(128)S(1)} %copy-done.19), kind=kLoop, calls=%fused_computation.17 | loop fusion | flops 884736 | bytes 1216576 | tf_op jit(solution)/shard_map/mul | solution.py:422
  33.4 0.0 copy-start.17
  33.4 1.7 copy_multiply_fusion
  35.1 2.8 %convolution_bitcast_fusion = f32[32,2,72,128]{3,2,1,0:T(8,128)} fusion(f32[72,128,1,1]{1,0,3,2:T(8,128)S(1)} %copy-done.17, f32[32,2,128,128]{3,2,1,0:T(8,128)S(1)} %copy-done.13), kind=kOutput, calls=%fused_computation.7 | convolution fusion | flops 452984832 | bytes 6590464 | tf_op jit(solution)/shard_map/ua,ciab->ciub/dot_general | solution.py:396
  37.9 83.8 %all-to-all-done.image_ref = f32[32,264,128]{2,1,0:T(8,128)} async-done(((f32[32,264,128]{2,1,0:T(8,128)}), f32[32,264,128]{2,1,0:T(8,128)}, u32[]{:S(2)}, u32[]{:S(2)}) %all-to-all-start) | async-done | bytes 4325408 | tf_op jit(solution)/shard_map/all_to_all | solution.py:350
  121.7 0.9 slice_convert_fusion
  122.6 0.1 copy.27
  122.8 2.3 %copy-done = f32[64,72,256]{2,1,0:T(8,128)S(1)} copy-done((f32[64,72,256]{2,1,0:T(8,128)S(1)}, f32[64,72,256]{2,1,0:T(8,128)}, u32[]{:S(2)}) %copy-start) | copy-done | bytes 4718616
  125.1 10.3 %owner_spectra.1 = (f32[16,72,256]{2,1,0:T(8,128)S(1)}, f32[16,72,256]{2,1,0:T(8,128)S(1)}, f32[64,72,256]{2,1,0:T(8,128)S(1)}) custom-call(s32[6,64]{1,0:T(8,128)S(1)} %add_bitcast_fusion.info_ref, f32[32,264,128]{2,1,0:T(8,128)} %all-to-all-done.image_ref, f32[16,72,128]{2,1,0:T(8,128)S(1)} %get-tuple-element.19.contrast_ref, f32[4,72,256]{2,1,0:T(8,128)S(1)} %copy-done.4, ...), custom_call_target="tpu_custom_call" | custom-call | tf_op jit(solution)/shard_map/owner_spectra/pallas_call | solution.py:242
  135.5 5.5 %collective-permute-start = (f32[16,72,256]{2,1,0:T(8,128)S(1)}, f32[16,72,256]{2,1,0:T(8,128)S(1)}, u32[]{:S(2)}, u32[]{:S(2)}) collective-permute-start(f32[16,72,256]{2,1,0:T(8,128)S(1)} %get-tuple-element.7), channel_id=1, source_target_pairs={{0,32},{32,0},{64,96},{96,64},{128,160},{160,128},{192,224},{224,1... | collective-permute-start | bytes 3538952 | tf_op jit(solution)/shard_map/ppermute | solution.py:408
  140.9 0.2 convert_reduce_fusion
  141.1 1.1 fusion
  142.2 0.6 copy-done.14
  142.8 0.2 fusion.3
  143.0 0.2 pad_maximum_fusion.1.ref_ref
  143.2 0.2 fusion.37
  143.4 0.0 collective-permute-done
  143.4 0.2 slice_add_fusion.1
  143.6 1.6 collective-permute-start.1
  145.1 2.6 %collective-permute-start.2 = (f32[4,72,256]{2,1,0:T(8,128)S(1)}, f32[4,72,256]{2,1,0:T(8,128)S(1)}, u32[]{:S(2)}, u32[]{:S(2)}) collective-permute-start(f32[4,72,256]{2,1,0:T(8,128)S(1)} %get-tuple-element.11), channel_id=1, source_target_pairs={{0,128},{32,160},{64,192},{96,224},{128,0},{160,32},{192,64},{224,... | collective-permute-start | bytes 884744 | tf_op jit(solution)/shard_map/ppermute | solution.py:414
  147.7 1.1 collective-permute-start.3
  148.8 0.1 maximum_multiply_fusion.row_ref
  148.9 0.0 copy-start.7
  148.9 5.0 %owner_scores.1 = f32[32,1,128]{2,1,0:T(1,128)} custom-call(s32[6,64]{1,0:T(8,128)S(1)} %add_bitcast_fusion.info_ref, f32[64,72,256]{2,1,0:T(8,128)S(1)} %get-tuple-element.5.filt_ref, f32[32,72,256]{2,1,0:T(8,128)S(1)} %pad_maximum_fusion.1.ref_ref, bf16[512,256]{1,0:T(8,128)(2,1)S(1)} %maximum_maximum_fusion.col_ref, ...), custom_call_target="tpu_custom_call" | custom-call | tf_op jit(solution)/shard_map/owner_scores/pallas_call | solution.py:273
  153.9 4.5 %all-to-all-start.1 = ((f32[32,1,128]{2,1,0:T(1,128)}), f32[32,1,128]{2,1,0:T(1,128)S(1)}, u32[]{:S(2)}, u32[]{:S(2)}) async-start(f32[32,1,128]{2,1,0:T(1,128)} %owner_scores.1), calls=%async_computation.1 | async-start | bytes 32768 | tf_op jit(solution)/shard_map/all_to_all | solution.py:416
  158.4 8.5 %all-to-all-done.1.home_ref = f32[32,1,128]{2,1,0:T(1,128)S(1)} async-done(((f32[32,1,128]{2,1,0:T(1,128)}), f32[32,1,128]{2,1,0:T(1,128)S(1)}, u32[]{:S(2)}, u32[]{:S(2)}) %all-to-all-start.1) | async-done | bytes 16416 | tf_op jit(solution)/shard_map/all_to_all | solution.py:416
  167.0 1.3 pick.1
  168.3 0.0 collective-permute-done.1.a_ref
  168.3 0.0 collective-permute-done.2.b_ref
  168.3 0.0 collective-permute-done.3.c_ref
  168.3 2.9 %finish.1 = f32[4,2,128,128]{3,2,1,0:T(8,128)} custom-call(f32[4,72,256]{2,1,0:T(8,128)S(1)} %get-tuple-element.13.mine_ref, f32[4,72,256]{2,1,0:T(8,128)S(1)} %collective-permute-done.1.a_ref, f32[4,72,256]{2,1,0:T(8,128)S(1)} %collective-permute-done.2.b_ref, f32[4,72,256]{2,1,0:T(8,128)S(1)} %collective-permute-done.3.c_ref, ...), custom_call_target="tpu_custom_call" | custom-call | tf_op jit(solution)/shard_map/finish/pallas_call | solution.py:309
  (38 shorter events, 0.2 us)
Async XLA Ops:
  0.6 1.6 copy-start.2
  2.2 0.7 copy-start.8
  2.9 0.7 copy-start.9
  3.5 0.7 copy-start.10
  4.2 0.7 copy-start.11
  11.9 2.1 %copy-start.1 = (f32[32,264,128]{2,1,0:T(8,128)}, f32[32,264,128]{2,1,0:T(8,128)S(1)}, u32[]{:S(2)}) copy-start(f32[32,264,128]{2,1,0:T(8,128)S(1)} %place_slots.1) | copy-start | bytes 12976132
  14.0 12.2 %copy-start.18 = (s32[64,2]{0,1:T(2,128)S(1)}, s32[64,2]{0,1:T(2,128)}, u32[]{:S(2)}) copy-start(s32[64,2]{0,1:T(2,128)} %param.21) | copy-start | bytes 1540
  14.0 12.6 %copy-start.12 = (s32[32]{0:T(128)S(1)}, s32[32]{0:T(128)}, u32[]{:S(2)}) copy-start(s32[32]{0:T(128)} %class_ref.1) | copy-start | bytes 388
  14.0 107.7 %all-to-all-start = ((f32[32,264,128]{2,1,0:T(8,128)}), f32[32,264,128]{2,1,0:T(8,128)}, u32[]{:S(2)}, u32[]{:S(2)}) async-start(f32[32,264,128]{2,1,0:T(8,128)} %copy-done.1), calls=%async_computation | async-start | bytes 8650752 | tf_op jit(solution)/shard_map/all_to_all | solution.py:350
  28.5 2.7 %copy-start.19 = (f32[16]{0:T(128)S(1)}, f32[16]{0:T(128)}, u32[]{:S(2)}) copy-start(f32[16]{0:T(128)} %param.22) | copy-start | bytes 196
  28.5 4.9 %copy-start.13 = (f32[32,2,128,128]{3,2,1,0:T(8,128)S(1)}, f32[32,2,128,128]{3,2,1,0:T(8,128)}, u32[]{:S(2)}) copy-start(f32[32,2,128,128]{3,2,1,0:T(8,128)} %param.16) | copy-start | bytes 12582916
  33.4 1.7 copy-start.17
  35.1 87.6 %copy-start.3 = (bf16[768,256]{1,0:T(8,128)(2,1)S(1)}, bf16[768,256]{1,0:T(8,128)(2,1)}, u32[]{:S(2)}) copy-start(bf16[768,256]{1,0:T(8,128)(2,1)} %constant.160.clone.right_ref) | copy-start | bytes 1179652
  35.1 87.6 %copy-start.4 = (f32[4,72,256]{2,1,0:T(8,128)S(1)}, f32[4,72,256]{2,1,0:T(8,128)}, u32[]{:S(2)}) copy-start(f32[4,72,256]{2,1,0:T(8,128)} %constant.158.clone.turn_ref) | copy-start | bytes 884740
  35.1 87.6 %copy-start.5 = (bf16[288,256]{1,0:T(8,128)(2,1)S(1)}, bf16[288,256]{1,0:T(8,128)(2,1)}, u32[]{:S(2)}) copy-start(bf16[288,256]{1,0:T(8,128)(2,1)} %constant.159.clone.left_ref) | copy-start | bytes 442372
  122.8 2.3 %copy-start = (f32[64,72,256]{2,1,0:T(8,128)S(1)}, f32[64,72,256]{2,1,0:T(8,128)}, u32[]{:S(2)}) copy-start(f32[64,72,256]{2,1,0:T(8,128)} %pad_maximum_fusion.best_ref) | copy-start | bytes 14155780
  125.1 16.0 %copy-start.15 = (f32[32,2,72,128]{3,2,1,0:T(8,128)S(1)}, f32[32,2,72,128]{3,2,1,0:T(8,128)}, u32[]{:S(2)}) copy-start(f32[32,2,72,128]{3,2,1,0:T(8,128)} %convolution_bitcast_fusion) | copy-start | bytes 7077892
  125.1 16.0 %copy-start.16 = (f32[128,128,1,1]{1,0,2,3:T(8,128)S(1)}, f32[128,128,1,1]{1,0,2,3:T(8,128)}, u32[]{:S(2)}) copy-start(f32[128,128,1,1]{1,0,2,3:T(8,128)} %constant.168) | copy-start | bytes 196612
  135.5 7.9 %collective-permute-start = (f32[16,72,256]{2,1,0:T(8,128)S(1)}, f32[16,72,256]{2,1,0:T(8,128)S(1)}, u32[]{:S(2)}, u32[]{:S(2)}) collective-permute-start(f32[16,72,256]{2,1,0:T(8,128)S(1)} %get-tuple-element.7), channel_id=1, source_target_pairs={{0,32},{32,0},{64,96},{96,64},{128,160},{160,128},{192,224},{224,1... | collective-permute-start | bytes 3538952 | tf_op jit(solution)/shard_map/ppermute | solution.py:408
  141.1 1.7 copy-start.14
  143.6 24.7 %collective-permute-start.1 = (f32[4,72,256]{2,1,0:T(8,128)S(1)}, f32[4,72,256]{2,1,0:T(8,128)S(1)}, u32[]{:S(2)}, u32[]{:S(2)}) collective-permute-start(f32[4,72,256]{2,1,0:T(8,128)S(1)} %get-tuple-element.12), channel_id=1, source_target_pairs={{0,64},{32,96},{64,128},{96,160},{128,192},{160,224},{192,0},{224,... | collective-permute-start | bytes 884744 | tf_op jit(solution)/shard_map/ppermute | solution.py:414
  145.1 23.1 %collective-permute-start.2 = (f32[4,72,256]{2,1,0:T(8,128)S(1)}, f32[4,72,256]{2,1,0:T(8,128)S(1)}, u32[]{:S(2)}, u32[]{:S(2)}) collective-permute-start(f32[4,72,256]{2,1,0:T(8,128)S(1)} %get-tuple-element.11), channel_id=1, source_target_pairs={{0,128},{32,160},{64,192},{96,224},{128,0},{160,32},{192,64},{224,... | collective-permute-start | bytes 884744 | tf_op jit(solution)/shard_map/ppermute | solution.py:414
  147.7 20.6 %collective-permute-start.3 = (f32[4,72,256]{2,1,0:T(8,128)S(1)}, f32[4,72,256]{2,1,0:T(8,128)S(1)}, u32[]{:S(2)}, u32[]{:S(2)}) collective-permute-start(f32[4,72,256]{2,1,0:T(8,128)S(1)} %get-tuple-element.10), channel_id=1, source_target_pairs={{0,192},{32,224},{64,0},{96,32},{128,64},{160,96},{192,128},{224,1... | collective-permute-start | bytes 884744 | tf_op jit(solution)/shard_map/ppermute | solution.py:414
  148.8 19.4 %copy-start.6 = (f32[128,128]{1,0:T(8,128)S(1)}, f32[128,128]{1,0:T(8,128)}, u32[]{:S(2)}) copy-start(f32[128,128]{1,0:T(8,128)} %constant.157.clone.lanes_ref) | copy-start | bytes 196612
  148.9 19.4 %copy-start.7 = (f32[64,72]{1,0:T(8,128)S(1)}, f32[64,72]{1,0:T(8,128)}, u32[]{:S(2)}) copy-start(f32[64,72]{1,0:T(8,128)} %constant.161.clone.unfold_ref) | copy-start | bytes 55300
  153.9 13.1 %all-to-all-start.1 = ((f32[32,1,128]{2,1,0:T(1,128)}), f32[32,1,128]{2,1,0:T(1,128)S(1)}, u32[]{:S(2)}, u32[]{:S(2)}) async-start(f32[32,1,128]{2,1,0:T(1,128)} %owner_scores.1), calls=%async_computation.1 | async-start | bytes 32768 | tf_op jit(solution)/shard_map/all_to_all | solution.py:416

commit v3 on v2

--- a/solution.py
+++ b/solution.py
@@ -12,6 +12,7 @@
 HALF = 72
 TAG = 8
 COUNT = HALF - 1
+SHIFT = 8
 MIB = 1 << 20
 
 
@@ -57,6 +58,16 @@
     return np.concatenate([np.cos(angles), np.sin(angles)], axis=2).astype(np.float32)
 
 
+def shift_constants(side):
+    steps = np.arange(-SHIFT, SHIFT + 1)[:, None]
+    row = np.broadcast_to((steps * np.arange(HALF) % side)[:, :, None], (2 * SHIFT + 1, HALF, side))
+    col = (steps * np.arange(side) % side)[:, None, :]
+    return [
+        np.concatenate([np.cos(t * (2.0 * np.pi / side)), np.sin(t * (2.0 * np.pi / side))], axis=2).astype(np.float32)
+        for t in (row, col)
+    ]
+
+
 def flip_constants(side):
     lanes = np.zeros((side, side), np.float32)
     lanes[(-np.arange(side)) % side, np.arange(side)] = 1.0
@@ -69,9 +80,14 @@
     return lanes, fold, unfold
 
 
-def scatter_kernel(class_local, class_ref, turn_ref, shift_ref, bin_ref, image_ref, slot_ref,
-                   count_ref, hold_ref, tag_ref, in_sems, out_sems, tag_sem):
+def scatter_kernel(class_local, chips_y, class_hbm, turn_hbm, best_hbm, bin_hbm, shift_hbm, image_ref, slot_ref,
+                   class_ref, turn_ref, best_ref, bin_ref, shift_ref, count_ref, hold_ref, tag_ref,
+                   int_sems, in_sems, out_sems, tag_sem):
     items, side, _ = hold_ref.shape
+    pairs = ((class_hbm, class_ref), (turn_hbm, turn_ref), (best_hbm, best_ref), (bin_hbm, bin_ref), (shift_hbm, shift_ref))
+    ints = [pltpu.make_async_copy(a, b, int_sems.at[at]) for at, (a, b) in enumerate(pairs)]
+    for load in ints:
+        load.start()
     loads = []
     for item in range(items):
         load = pltpu.make_async_copy(image_ref.at[item], hold_ref.at[item], in_sems.at[item])
@@ -81,9 +97,16 @@
         count_ref[owner] = 0
     tag_ref[...] = jnp.zeros_like(tag_ref)
     lane = lax.broadcasted_iota(jnp.int32, (1, side), 1)
+    groups = lax.axis_size("grp")
+    me_grp = lax.axis_index("grp")
+    cores, own = groups // chips_y, class_local // groups
+    core, me_y = lax.rem(me_grp, cores), lax.div(me_grp, cores)
+    for load in ints:
+        load.wait()
     stores = []
     for item in range(items):
         owner = lax.div(class_ref[item], class_local)
+        local = class_ref[item] - owner * class_local
         rank = count_ref[owner]
         count_ref[owner] = rank + 1
         loads[item].wait()
@@ -94,7 +117,12 @@
         )
         store.start()
         stores.append(store)
-        fields = (class_ref[item] - owner * class_local, turn_ref[item], shift_ref[item], bin_ref[item], 1)
+        place = lax.div(local, own)
+        other = lax.rem(lax.rem(place, cores) - core + cores, cores)
+        step = lax.rem(lax.div(place, cores) - me_y + chips_y, chips_y)
+        target = (other * chips_y + step) * own + lax.rem(local, own)
+        best = best_ref[item]
+        fields = (local, turn_ref[item], shift_ref[0, best] + SHIFT, shift_ref[1, best] + SHIFT, bin_ref[item], target, 1)
         tag = jnp.zeros((1, side), jnp.int32)
         for at, value in enumerate(fields):
             tag = jnp.where(lane == at, value, tag)
@@ -106,37 +134,41 @@
         store.wait()
 
 
-def place_slots(particles, class_of, rotation_bin, shift_best, defocus_bin, owners, class_local):
+def place_slots(particles, class_of, rotation_bin, shift_best, defocus_bin, shift_list, owners, class_local, chips_y):
     count, side, _ = particles.shape
     return pl.pallas_call(
-        functools.partial(scatter_kernel, class_local),
+        functools.partial(scatter_kernel, class_local, chips_y),
         out_shape=jax.ShapeDtypeStruct((owners, 2 * side + TAG, side), jnp.float32),
-        in_specs=[pl.BlockSpec(memory_space=pltpu.SMEM)] * 4 + [pl.BlockSpec(memory_space=pltpu.HBM)],
+        in_specs=[pl.BlockSpec(memory_space=pltpu.HBM)] * 6,
         out_specs=pl.BlockSpec(memory_space=pltpu.HBM),
-        scratch_shapes=[
+        scratch_shapes=[pltpu.SMEM((count,), jnp.int32)] * 4
+        + [
+            pltpu.SMEM(shift_list.shape[::-1], jnp.int32),
             pltpu.SMEM((owners,), jnp.int32),
             pltpu.VMEM((count, side, side), jnp.float32),
             pltpu.VMEM((owners, TAG, side), jnp.float32),
+            pltpu.SemaphoreType.DMA((5,)),
             pltpu.SemaphoreType.DMA((count,)),
             pltpu.SemaphoreType.DMA((count,)),
             pltpu.SemaphoreType.DMA,
         ],
-        compiler_params=pltpu.CompilerParams(vmem_limit_bytes=16 * MIB),
+        compiler_params=pltpu.CompilerParams(vmem_limit_bytes=58 * MIB),
         name="place_slots",
-    )(class_of, rotation_bin, shift_best, defocus_bin, particles)
-
-
-def spectrum_kernel(step_sources, info_ref, image_ref, contrast_ref, turn_ref, best_ref, left_ref, right_ref,
-                    keep_ref, give_ref, filt_ref, numer_ref, sems):
+    )(class_of, rotation_bin, shift_best, defocus_bin, shift_list.T, particles)
+
+
+def spectrum_kernel(step_sources, info_ref, image_ref, contrast_ref, turn_ref, row_ref, col_ref, left_ref, right_ref,
+                    *refs):
+    keep_ref, give_ref, filt_ref, numer_ref, sems = refs[-5:]
     side = image_ref.shape[-1]
-    first = pl.program_id(0) * step_sources * 2
+    first = pl.program_id(0) * step_sources
     lane = lax.broadcasted_iota(jnp.int32, (1, side), 1)
 
     @pl.when(pl.program_id(0) == 0)
     def _():
         numer_ref[...] = jnp.zeros_like(numer_ref)
 
-    turns = [info_ref[1, first + item] for item in range(2 * step_sources)]
+    turns = [info_ref[first + item // 2, item % 2, 1] for item in range(2 * step_sources)]
     parts = []
     for at in range(step_sources):
         highs, lows = [], []
@@ -163,27 +195,29 @@
         jnp.concatenate([high, low, high], axis=1), right_ref[...], preferred_element_type=jnp.float32
     )
     for item in range(2 * step_sources):
-        slot = first + item
+        info = [info_ref[first + item // 2, item % 2, at] for at in range(7)]
         rows = slice(item * HALF, (item + 1) * HALF)
         sign = jnp.where(turns[item] >= 2, -1.0, 1.0).astype(jnp.float32)
         real = spectrum[rows, :side]
         imag = sign * spectrum[rows, side:]
         turn = turn_ref[turns[item]]
-        contrast = contrast_ref[info_ref[3, slot]]
+        contrast = contrast_ref[info[4]]
         turn_real, turn_imag = turn[:, :side], turn[:, side:]
         filt_real = contrast * (real * turn_real - imag * turn_imag)
         filt_imag = contrast * (real * turn_imag + imag * turn_real)
         filt_ref[item, :, :side] = filt_real
         filt_ref[item, :, side:] = filt_imag
 
-        @pl.when(info_ref[4, slot] > 0)
-        def _(slot=slot, filt_real=filt_real, filt_imag=filt_imag):
-            best = best_ref[info_ref[2, slot]]
-            best_real, best_imag = best[:, :side], best[:, side:]
-            target = info_ref[5, slot]
-            numer_ref[target, :, :side] += filt_real * best_real - filt_imag * best_imag
-            numer_ref[target, :, side:] += filt_real * best_imag + filt_imag * best_real
-            hit = (lane == info_ref[3, slot]).astype(jnp.float32)
+        @pl.when(info[6] > 0)
+        def _(info=info, filt_real=filt_real, filt_imag=filt_imag):
+            target = info[5]
+            row_real, row_imag = row_ref[info[2], :, :side], row_ref[info[2], :, side:]
+            half_real = filt_real * row_real - filt_imag * row_imag
+            half_imag = filt_real * row_imag + filt_imag * row_real
+            col_real, col_imag = col_ref[info[3], :, :side], col_ref[info[3], :, side:]
+            numer_ref[target, :, :side] += half_real * col_real - half_imag * col_imag
+            numer_ref[target, :, side:] += half_real * col_imag + half_imag * col_real
+            hit = (lane == info[4]).astype(jnp.float32)
             numer_ref[target, COUNT : COUNT + 1, :side] += hit
 
     @pl.when(pl.program_id(0) == pl.num_programs(0) - 1)
@@ -201,10 +235,10 @@
 
 def score_kernel(step_sources, info_ref, filt_ref, ref_ref, col_ref, row_ref, score_ref):
     side = score_ref.shape[-1]
-    first = pl.program_id(0) * step_sources * 2
+    first = pl.program_id(0) * step_sources
     products = []
     for item in range(2 * step_sources):
-        ref = ref_ref[info_ref[0, first + item]]
+        ref = ref_ref[info_ref[first + item // 2, item % 2, 0]]
         ref_real, ref_imag = ref[:, :side], ref[:, side:]
         filt_real, filt_imag = filt_ref[item, :, :side], filt_ref[item, :, side:]
         products.append(
@@ -233,11 +267,11 @@
         score_ref[at] = jnp.where(lane < side // 2, sums[0], sums[1])
 
 
-def owner_spectra(info, images, contrast, turn, best, left, right, class_local):
+def owner_spectra(info, images, contrast, turn, row, col, left, right, ready, class_local):
     sources, _, side = images.shape
     step_sources = 4
     whole = lambda x: pl.BlockSpec(x.shape, lambda i: (0,) * x.ndim)
-    tables = (contrast, turn, best, left, right)
+    tables = (contrast, turn, row, col, left, right)
     half = jax.ShapeDtypeStruct((class_local // 2, HALF, 2 * side), jnp.float32)
     return pl.pallas_call(
         functools.partial(spectrum_kernel, step_sources),
@@ -251,7 +285,8 @@
             pl.BlockSpec(memory_space=pltpu.SMEM),
             pl.BlockSpec((step_sources, 2 * side, side), lambda i: (i, 0, 0)),
         ]
-        + [whole(table) for table in tables],
+        + [whole(table) for table in tables]
+        + [pl.BlockSpec(memory_space=pl.ANY)] * len(ready),
         out_specs=(
             pl.BlockSpec(memory_space=pltpu.HBM),
             pl.BlockSpec(memory_space=pltpu.HBM),
@@ -261,9 +296,9 @@
             pltpu.VMEM((class_local, HALF, 2 * side), jnp.float32),
             pltpu.SemaphoreType.DMA((2,)),
         ],
-        compiler_params=pltpu.CompilerParams(vmem_limit_bytes=32 * MIB),
+        compiler_params=pltpu.CompilerParams(vmem_limit_bytes=24 * MIB),
         name="owner_spectra",
-    )(info, images, *tables)
+    )(info, images, *tables, *ready)
 
 
 def owner_scores(info, filtered, refs, col, row):
@@ -285,13 +320,14 @@
     )(info, filtered, refs, col, row)
 
 
-def finish_kernel(mine_ref, a_ref, b_ref, c_ref, square_ref, lanes_ref, unfold_ref, out_ref):
+def finish_kernel(mine_ref, a_ref, b_ref, c_ref, contrast_ref, lanes_ref, unfold_ref, out_ref):
     side = out_ref.shape[-1]
     for at in range(out_ref.shape[0]):
         total = (mine_ref[at] + a_ref[at]) + (b_ref[at] + c_ref[at])
         weight = jnp.zeros((HALF, side), jnp.float32)
-        for which in range(square_ref.shape[0]):
-            weight += total[COUNT : COUNT + 1, which : which + 1] * square_ref[which]
+        for which in range(contrast_ref.shape[0]):
+            contrast = contrast_ref[which]
+            weight += total[COUNT : COUNT + 1, which : which + 1] * (contrast * contrast)
         inverse = 1.0 / (weight + 1.0)
         for part in range(2):
             ratio = total[:, part * side : (part + 1) * side] * inverse
@@ -305,13 +341,13 @@
             out_ref[at, part, side // 2 :] = back if part == 0 else -back
 
 
-def finish(blocks, square, lanes, unfold, side):
+def finish(blocks, contrast, lanes, unfold, side):
     return pl.pallas_call(
         finish_kernel,
         out_shape=jax.ShapeDtypeStruct((blocks[0].shape[0], 2, side, side), jnp.float32),
         compiler_params=pltpu.CompilerParams(vmem_limit_bytes=16 * MIB),
         name="finish",
-    )(*blocks, square, lanes, unfold)
+    )(*blocks, contrast, lanes, unfold)
 
 
 def pick_kernel(target_ref, home_ref, out_ref):
@@ -341,24 +377,15 @@
     class_local = references.shape[0]
     owners = lax.axis_size("cls")
     groups = lax.axis_size("grp")
-    me_grp = lax.axis_index("grp")
     unit = 2.0 * math.pi / side
 
+    cores = groups // chips_y
+    own_classes = class_local // groups
+
     send = place_slots(
-        particles, class_of, rotation_bin, shift_best, defocus_bin, owners, class_local
+        particles, class_of, rotation_bin, shift_best, defocus_bin, shift_list, owners, class_local, chips_y
     )
     images = lax.all_to_all(send, "cls", split_axis=0, concat_axis=0, tiled=True)
-
-    cores = groups // chips_y
-    core, me_y = me_grp % cores, me_grp // cores
-    own_classes = class_local // groups
-    tags = images[:, 2 * side : 2 * side + 2, :5].astype(jnp.int32).reshape(2 * owners, 5)
-    local = tags[:, 0]
-    place = local // own_classes
-    target = (
-        ((place % cores - core) % cores) * chips_y + (place // cores - me_y) % chips_y
-    ) * own_classes + local % own_classes
-    info = jnp.concatenate([tags, target[:, None]], axis=1).T
 
     pixel = jnp.arange(side, dtype=jnp.int32)
     signed = jnp.where(pixel < side // 2, pixel, pixel - side).astype(jnp.float32)
@@ -372,13 +399,6 @@
     col_angle = ((pixel[None, :] * shift_list[:, 1][:, None]) % side).astype(jnp.float32) * unit
     row_cos, row_sin = jnp.cos(row_angle), jnp.sin(row_angle)
     col_cos, col_sin = jnp.cos(col_angle), jnp.sin(col_angle)
-    best = jnp.concatenate(
-        [
-            row_cos[:, :, None] * col_cos[:, None, :] - row_sin[:, :, None] * col_sin[:, None, :],
-            row_sin[:, :, None] * col_cos[:, None, :] + row_cos[:, :, None] * col_sin[:, None, :],
-        ],
-        axis=2,
-    )
     col = jnp.concatenate(
         [
             jnp.concatenate([col_cos.T, col_sin.T], axis=1),
@@ -398,14 +418,18 @@
     top = references[:, :, :HALF] * live_rows
     refs = jnp.concatenate([top[:, 0] + folded[:, 0], top[:, 1] - folded[:, 1]], axis=2)
 
+    refs = pltpu.with_memory_space_constraint(refs, pltpu.HBM)
+    info = images[:, 2 * side : 2 * side + 2, :8].astype(jnp.int32)
     left, right = dft_constants(side)
+    best_row, best_col = shift_constants(side)
     keep, give, filtered = owner_spectra(
-        info, images, contrast, jnp.asarray(turn_constants(side)), best, jnp.asarray(left),
-        jnp.asarray(right), class_local,
+        info, images, contrast, jnp.asarray(turn_constants(side)), jnp.asarray(best_row),
+        jnp.asarray(best_col), jnp.asarray(left), jnp.asarray(right), (refs, col, row), class_local,
     )
     slot_scores = owner_scores(info, filtered, refs, col, row)
 
     got = lax.ppermute(give, "grp", [(i, i ^ 1) for i in range(groups)])
+    got, slot_scores = lax.optimization_barrier((got, slot_scores))
     blocks = []
     for step in range(chips_y):
         part = slice(step * own_classes, (step + 1) * own_classes)
@@ -414,13 +438,14 @@
         blocks.append(lax.ppermute(block, "grp", pairs) if step else block)
 
     home = lax.all_to_all(slot_scores, "cls", split_axis=0, concat_axis=0, tiled=True)
+    fresh_refs = finish(
+        blocks, contrast, jnp.asarray(lanes), jnp.asarray(unfold), side
+    )
+    home, fresh_refs = lax.optimization_barrier((home, fresh_refs))
     owner_of = class_of // class_local
     earlier = jnp.tril(owner_of[:, None] == owner_of[None, :], -1)
     scores = pick(owner_of * 2 + jnp.sum(earlier.astype(jnp.int32), axis=1), home)
 
-    fresh_refs = finish(
-        blocks, contrast * contrast, jnp.asarray(lanes), jnp.asarray(unfold), side
-    )
     return (scores, fresh_refs)
 
 

time: 172 us -> 156 us (0.907)
  local copies, waits for them, and re-layouts: 9.36 us -> 0.91 us
  other arithmetic: 10.7 us -> 8.09 us
  Pallas kernels: 26.6 us -> 24 us
    all_to_all x1, waiting for transfers between devices: 8.54 us -> 0.01 us  [body(): lax.all_to_all(slot_scores, 'cls', split_axis=0, concat_axis=0, tiled=True)]
    unnamed x40 -> x26, local copies, waits for them, and re-layouts: 9.29 us -> 0.9 us
    ppermute x3, waiting for transfers between devices: 0.01 us -> 8.14 us  [body(): blocks.append(lax.ppermute(block, 'grp', pairs) if step else block)]
    pallas_call x1, Pallas kernels: 7.03 us -> 3.01 us  [place_slots(): pl.pallas_call(functools.partial(scatter_kernel, class_local, chips_y), o...]
    concatenate x1 -> x0, other arithmetic: 2.7 us -> none  [body(): jnp.concatenate([row_cos[:, :, None] * col_cos[:, None, :] - row_sin[:, :...]
    mul x1 -> x0, other arithmetic: 2.2 us -> none  [body(): contrast * contrast]
    neg x0 -> x1, other arithmetic: none -> 2.19 us  [body(): contrast = -(0.995 * jnp.sin(angle) + 0.1 * jnp.cos(angle))]
  transfers between devices with their start and end apart: 6 -> 6, of which waited for: 2 -> 3; matrix products, arithmetic and copies ran while one was open for 8% -> 6% of each run, Pallas kernels for 4% -> 6%
where the time goes in v3:
time: 156 us
  waiting for transfers between devices  93.3 us (60%)
  starting transfers between devices  26.3 us (17%)
  Pallas kernels  24 us (15%)
  other arithmetic  8.09 us (5%)
  matrix products  2.73 us (2%)
    all_to_all x1, waiting for transfers between devices, body(): lax.all_to_all(send, 'cls', split_axis=0, concat_axis=0, tiled=True)  85.2 us
    all_to_all x1, starting transfers between devices, body(): lax.all_to_all(send, 'cls', split_axis=0, concat_axis=0, tiled=True)  12 us
    pallas_call x1, Pallas kernels, owner_spectra(): pl.pallas_call(functools.partial(spectrum_kernel, step_sources), grid=(so...  10.7 us
    ppermute x3, waiting for transfers between devices, body(): blocks.append(lax.ppermute(block, 'grp', pairs) if step else block)  8.14 us
    pallas_call x1, Pallas kernels, owner_scores(): pl.pallas_call(functools.partial(score_kernel, step_sources), grid=(items...  6.11 us
    ppermute x1, starting transfers between devices, body(): got = lax.ppermute(give, 'grp', [(i, i ^ 1) for i in range(groups)])  5.32 us
    ppermute x3, starting transfers between devices, body(): blocks.append(lax.ppermute(block, 'grp', pairs) if step else block)  5 us
    all_to_all x1, starting transfers between devices, body(): lax.all_to_all(slot_scores, 'cls', split_axis=0, concat_axis=0, tiled=True)  4.05 us
  transfers between devices with their start and end apart: 6, of which 3 were waited for; matrix products, arithmetic and copies ran while one was open for 6% of the time, Pallas kernels for 6%

profile of v3, /device:TPU:1, one launch (start us, length us, event | category | flops | bytes accessed | tf_op | source)
XLA Modules:
  0.0 156.2 jit_solution(6306036820459224581)
XLA Ops:
  0.6 3.0 %place_slots.1 = f32[32,264,128]{2,1,0:T(8,128)} custom-call(s32[32]{0:T(128)} %class_hbm.1, s32[32]{0:T(128)} %turn_hbm.1, s32[32]{0:T(128)} %best_hbm.1, s32[32]{0:T(128)} %bin_hbm.1, s32[2,64]{1,0:T(2,128)} %bitcast.18, f32[32,128,128]{2,1,0:T(8,128)} %image_ref.1), custom_call_target="tpu_custom_call" | custom-call | tf_op jit(solution)/shard_map/place_slots/pallas_call | solution.py:139
  3.6 0.0 copy-start.10
  3.7 12.0 %all-to-all-start = ((f32[32,264,128]{2,1,0:T(8,128)}), f32[32,264,128]{2,1,0:T(8,128)}, u32[]{:S(2)}, u32[]{:S(2)}) async-start(f32[32,264,128]{2,1,0:T(8,128)} %place_slots.1), calls=%async_computation | async-start | bytes 8650752 | tf_op jit(solution)/shard_map/all_to_all | solution.py:388
  15.7 0.2 fusion.24
  15.9 0.1 maximum_multiply_fusion.refs_2_.row_ref
  15.9 0.3 fusion.21
  16.2 0.1 reduce-precision_convert_fusion
  16.4 0.0 copy-start.7
  16.4 0.0 copy-start.9
  16.4 2.0 %copy_multiply_fusion = f32[32,2,72,128]{3,2,0,1:T(8,128)S(1)} fusion(f32[72]{0:T(128)S(1)} %compare_convert_fusion, f32[32,2,128,128]{3,2,1,0:T(8,128)} %param.18), kind=kLoop, calls=%fused_computation.1 | loop fusion | flops 589824 | bytes 4718880 | tf_op jit(solution)/shard_map/mul | solution.py:418
  18.4 0.8 copy-done.7
  19.3 0.0 copy-done.9
  19.3 1.6 %convolution_bitcast_fusion = f32[32,2,72,128]{3,2,1,0:T(8,128)S(1)} fusion(f32[72,128,1,1]{1,0,3,2:T(8,128)S(1)} %copy-done.9, f32[32,2,128,128]{3,2,1,0:T(8,128)S(1)} %copy-done.7), kind=kOutput, calls=%fused_computation.4 | convolution fusion | flops 452984832 | bytes 6590464 | tf_op jit(solution)/shard_map/ua,ciab->ciub/dot_general | solution.py:416
  20.9 1.1 fusion
  22.0 0.2 fusion.3
  22.3 0.0 copy-start.12
  22.3 0.0 copy-start
  22.3 0.0 copy-start.1
  22.3 0.0 copy-start.2
  22.3 0.0 copy-start.3
  22.3 0.0 copy-start.6
  22.4 1.6 %pad_maximum_fusion.refs_0_.ref_ref = f32[32,72,256]{2,1,0:T(8,128)} fusion(f32[32,72,128]{2,1,0:T(8,128)S(1)} %get-tuple-element.17, f32[32,72,128]{2,1,0:T(8,128)S(1)} %get-tuple-element.16), kind=kLoop, calls=%fused_computation | loop fusion | flops 589824 | bytes 4718592 | tf_op jit(solution)/shard_map/concatenate | solution.py:419
  24.0 0.1 add_multiply_fusion
  24.0 2.2 %fusion.6.contrast_ref = f32[16,72,128]{2,1,0:T(8,128)S(1)} fusion(f32[72,128]{1,0:T(8,128)S(1)} %add_multiply_fusion, f32[16]{0:T(128)S(1)} %copy-done.12), kind=kLoop, calls=%fused_computation.13 | loop fusion | flops 737280 | bytes 626752 | tf_op jit(solution)/shard_map/neg | solution.py:396
  26.2 85.2 %all-to-all-done.image_ref = f32[32,264,128]{2,1,0:T(8,128)} async-done(((f32[32,264,128]{2,1,0:T(8,128)}), f32[32,264,128]{2,1,0:T(8,128)}, u32[]{:S(2)}, u32[]{:S(2)}) %all-to-all-start) | async-done | bytes 4325408 | tf_op jit(solution)/shard_map/all_to_all | solution.py:388
  111.4 0.9 slice_convert_fusion.info_ref
  112.3 0.0 copy-done
  112.3 0.0 copy-done.1
  112.3 0.0 copy-done.2
  112.3 0.0 copy-done.3
  112.3 0.0 copy-done.6
  112.4 0.0 copy-start.11
  112.4 10.7 %owner_spectra.1 = (f32[16,72,256]{2,1,0:T(8,128)S(1)}, f32[16,72,256]{2,1,0:T(8,128)S(1)}, f32[64,72,256]{2,1,0:T(8,128)S(1)}) custom-call(s32[32,2,8]{2,1,0:T(2,128)S(1)} %slice_convert_fusion.info_ref, f32[32,264,128]{2,1,0:T(8,128)} %all-to-all-done.image_ref, f32[16,72,128]{2,1,0:T(8,128)S(1)} %fusion.6.contrast_ref, f32[4,72,256]{2,1,0:T(8,128)S(1)} %copy-done.2, ...), custom_call_target="tpu_custom_call" | custom-call | tf_op jit(solution)/shard_map/owner_spectra/pallas_call | solution.py:276
  123.0 5.3 %collective-permute-start = (f32[16,72,256]{2,1,0:T(8,128)S(1)}, f32[16,72,256]{2,1,0:T(8,128)S(1)}, u32[]{:S(2)}, u32[]{:S(2)}) collective-permute-start(f32[16,72,256]{2,1,0:T(8,128)S(1)} %get-tuple-element.9), channel_id=1, source_target_pairs={{0,32},{32,0},{64,96},{96,64},{128,160},{160,128},{192,224},{224,1... | collective-permute-start | bytes 3538952 | tf_op jit(solution)/shard_map/ppermute | solution.py:431
  128.4 6.1 %owner_scores.1 = f32[32,1,128]{2,1,0:T(1,128)} custom-call(s32[32,2,8]{2,1,0:T(2,128)S(1)} %slice_convert_fusion.info_ref, f32[64,72,256]{2,1,0:T(8,128)S(1)} %get-tuple-element.10.filt_ref, f32[32,72,256]{2,1,0:T(8,128)} %pad_maximum_fusion.refs_0_.ref_ref, bf16[512,256]{1,0:T(8,128)(2,1)S(1)} %maximum_maximum_fusion.refs_1_.col_ref, ...), custom_call_target="tpu_custom_call" | custom-call | tf_op jit(solution)/shard_map/owner_scores/pallas_call | solution.py:308
  134.5 0.0 collective-permute-done
  134.5 0.2 slice_add_fusion.1
  134.6 1.4 collective-permute-start.1
  136.0 2.5 %collective-permute-start.2 = (f32[4,72,256]{2,1,0:T(8,128)S(1)}, f32[4,72,256]{2,1,0:T(8,128)S(1)}, u32[]{:S(2)}, u32[]{:S(2)}) collective-permute-start(f32[4,72,256]{2,1,0:T(8,128)S(1)} %get-tuple-element.19), channel_id=1, source_target_pairs={{0,128},{32,160},{64,192},{96,224},{128,0},{160,32},{192,64},{224,... | collective-permute-start | bytes 884744 | tf_op jit(solution)/shard_map/ppermute | solution.py:438
  138.6 1.1 collective-permute-start.3
  139.6 0.2 convert_reduce_fusion
  139.8 4.0 %all-to-all-start.1 = ((f32[32,1,128]{2,1,0:T(1,128)}), f32[32,1,128]{2,1,0:T(1,128)S(1)}, u32[]{:S(2)}, u32[]{:S(2)}) async-start(f32[32,1,128]{2,1,0:T(1,128)} %owner_scores.1), calls=%async_computation.1 | async-start | bytes 32768 | tf_op jit(solution)/shard_map/all_to_all | solution.py:440
  143.9 0.7 collective-permute-done.1.a_ref
  144.6 7.5 %collective-permute-done.2.b_ref = f32[4,72,256]{2,1,0:T(8,128)S(1)} collective-permute-done((f32[4,72,256]{2,1,0:T(8,128)S(1)}, f32[4,72,256]{2,1,0:T(8,128)S(1)}, u32[]{:S(2)}, u32[]{:S(2)}) %collective-permute-start.2) | collective-permute-done | bytes 294944 | tf_op jit(solution)/shard_map/ppermute | solution.py:438
  152.0 0.0 collective-permute-done.3.c_ref
  152.0 2.9 %finish.1 = f32[4,2,128,128]{3,2,1,0:T(8,128)} custom-call(f32[4,72,256]{2,1,0:T(8,128)S(1)} %get-tuple-element.21.mine_ref, f32[4,72,256]{2,1,0:T(8,128)S(1)} %collective-permute-done.1.a_ref, f32[4,72,256]{2,1,0:T(8,128)S(1)} %collective-permute-done.2.b_ref, f32[4,72,256]{2,1,0:T(8,128)S(1)} %collective-permute-done.3.c_ref, ...), custom_call_target="tpu_custom_call" | custom-call | tf_op jit(solution)/shard_map/finish/pallas_call | solution.py:345
  154.9 0.0 all-to-all-done.1.home_ref
  154.9 1.3 pick.1
  (17 shorter events, 0.1 us)
Async XLA Ops:
  3.6 12.0 %copy-start.10 = (s32[64,2]{0,1:T(2,128)S(1)}, s32[64,2]{0,1:T(2,128)}, u32[]{:S(2)}) copy-start(s32[64,2]{0,1:T(2,128)} %param.23) | copy-start | bytes 1540
  3.7 107.7 %all-to-all-start = ((f32[32,264,128]{2,1,0:T(8,128)}), f32[32,264,128]{2,1,0:T(8,128)}, u32[]{:S(2)}, u32[]{:S(2)}) async-start(f32[32,264,128]{2,1,0:T(8,128)} %place_slots.1), calls=%async_computation | async-start | bytes 8650752 | tf_op jit(solution)/shard_map/all_to_all | solution.py:388
  16.4 2.9 %copy-start.7 = (f32[32,2,128,128]{3,2,1,0:T(8,128)S(1)}, f32[32,2,128,128]{3,2,1,0:T(8,128)}, u32[]{:S(2)}) copy-start(f32[32,2,128,128]{3,2,1,0:T(8,128)} %param.18) | copy-start | bytes 12582916
  16.4 2.9 %copy-start.9 = (f32[72,128,1,1]{1,0,3,2:T(8,128)S(1)}, f32[72,128,1,1]{1,0,3,2:T(8,128)}, u32[]{:S(2)}) copy-start(f32[72,128,1,1]{1,0,3,2:T(8,128)} %constant.96) | copy-start | bytes 110596
  19.3 1.7 %copy-start.8 = (f32[128,128,1,1]{1,0,2,3:T(8,128)S(1)}, f32[128,128,1,1]{1,0,2,3:T(8,128)}, u32[]{:S(2)}) copy-start(f32[128,128,1,1]{1,0,2,3:T(8,128)} %constant.97) | copy-start | bytes 196612
  22.3 1.8 %copy-start.12 = (f32[16]{0:T(128)S(1)}, f32[16]{0:T(128)}, u32[]{:S(2)}) copy-start(f32[16]{0:T(128)} %param.24) | copy-start | bytes 196
  22.3 90.0 %copy-start = (f32[17,72,256]{2,1,0:T(8,128)S(1)}, f32[17,72,256]{2,1,0:T(8,128)}, u32[]{:S(2)}) copy-start(f32[17,72,256]{2,1,0:T(8,128)} %constant.86.clone.row_ref) | copy-start | bytes 3760132
  22.3 90.0 %copy-start.1 = (bf16[768,256]{1,0:T(8,128)(2,1)S(1)}, bf16[768,256]{1,0:T(8,128)(2,1)}, u32[]{:S(2)}) copy-start(bf16[768,256]{1,0:T(8,128)(2,1)} %constant.89.clone.right_ref) | copy-start | bytes 1179652
  22.3 90.0 %copy-start.2 = (f32[4,72,256]{2,1,0:T(8,128)S(1)}, f32[4,72,256]{2,1,0:T(8,128)}, u32[]{:S(2)}) copy-start(f32[4,72,256]{2,1,0:T(8,128)} %constant.85.clone.turn_ref) | copy-start | bytes 884740
  22.3 90.0 %copy-start.3 = (bf16[288,256]{1,0:T(8,128)(2,1)S(1)}, bf16[288,256]{1,0:T(8,128)(2,1)}, u32[]{:S(2)}) copy-start(bf16[288,256]{1,0:T(8,128)(2,1)} %constant.88.clone.left_ref) | copy-start | bytes 442372
  22.3 90.0 %copy-start.6 = (f32[17,1,256]{2,1,0:T(1,128)S(1)}, f32[17,1,256]{2,1,0:T(1,128)}, u32[]{:S(2)}) copy-start(f32[17,1,256]{2,1,0:T(1,128)} %constant.87.clone.col_ref) | copy-start | bytes 52228
  112.4 16.0 %copy-start.11 = (s32[32]{0:T(128)S(1)}, s32[32]{0:T(128)}, u32[]{:S(2)}) copy-start(s32[32]{0:T(128)} %class_hbm.1) | copy-start | bytes 388
  123.0 11.5 %collective-permute-start = (f32[16,72,256]{2,1,0:T(8,128)S(1)}, f32[16,72,256]{2,1,0:T(8,128)S(1)}, u32[]{:S(2)}, u32[]{:S(2)}) collective-permute-start(f32[16,72,256]{2,1,0:T(8,128)S(1)} %get-tuple-element.9), channel_id=1, source_target_pairs={{0,32},{32,0},{64,96},{96,64},{128,160},{160,128},{192,224},{224,1... | collective-permute-start | bytes 3538952 | tf_op jit(solution)/shard_map/ppermute | solution.py:431
  134.5 17.6 %copy-start.4 = (f32[128,128]{1,0:T(8,128)S(1)}, f32[128,128]{1,0:T(8,128)}, u32[]{:S(2)}) copy-start(f32[128,128]{1,0:T(8,128)} %constant.84.clone.lanes_ref) | copy-start | bytes 196612
  134.5 17.6 %copy-start.5 = (f32[64,72]{1,0:T(8,128)S(1)}, f32[64,72]{1,0:T(8,128)}, u32[]{:S(2)}) copy-start(f32[64,72]{1,0:T(8,128)} %constant.90.clone.unfold_ref) | copy-start | bytes 55300
  134.6 9.9 %collective-permute-start.1 = (f32[4,72,256]{2,1,0:T(8,128)S(1)}, f32[4,72,256]{2,1,0:T(8,128)S(1)}, u32[]{:S(2)}, u32[]{:S(2)}) collective-permute-start(f32[4,72,256]{2,1,0:T(8,128)S(1)} %get-tuple-element.20), channel_id=1, source_target_pairs={{0,64},{32,96},{64,128},{96,160},{128,192},{160,224},{192,0},{224,... | collective-permute-start | bytes 884744 | tf_op jit(solution)/shard_map/ppermute | solution.py:438
  136.0 16.0 %collective-permute-start.2 = (f32[4,72,256]{2,1,0:T(8,128)S(1)}, f32[4,72,256]{2,1,0:T(8,128)S(1)}, u32[]{:S(2)}, u32[]{:S(2)}) collective-permute-start(f32[4,72,256]{2,1,0:T(8,128)S(1)} %get-tuple-element.19), channel_id=1, source_target_pairs={{0,128},{32,160},{64,192},{96,224},{128,0},{160,32},{192,64},{224,... | collective-permute-start | bytes 884744 | tf_op jit(solution)/shard_map/ppermute | solution.py:438
  138.6 13.5 %collective-permute-start.3 = (f32[4,72,256]{2,1,0:T(8,128)S(1)}, f32[4,72,256]{2,1,0:T(8,128)S(1)}, u32[]{:S(2)}, u32[]{:S(2)}) collective-permute-start(f32[4,72,256]{2,1,0:T(8,128)S(1)} %get-tuple-element.18), channel_id=1, source_target_pairs={{0,192},{32,224},{64,0},{96,32},{128,64},{160,96},{192,128},{224,1... | collective-permute-start | bytes 884744 | tf_op jit(solution)/shard_map/ppermute | solution.py:438
  139.8 15.1 %all-to-all-start.1 = ((f32[32,1,128]{2,1,0:T(1,128)}), f32[32,1,128]{2,1,0:T(1,128)S(1)}, u32[]{:S(2)}, u32[]{:S(2)}) async-start(f32[32,1,128]{2,1,0:T(1,128)} %owner_scores.1), calls=%async_computation.1 | async-start | bytes 32768 | tf_op jit(solution)/shard_map/all_to_all | solution.py:440

commit v4 on v3

--- a/solution.py
+++ b/solution.py
@@ -74,7 +74,7 @@
     fold = np.zeros((HALF, side), np.float32)
     for u in range(1, side // 2):
         fold[u, side - u] = 1.0
-    unfold = np.zeros((side // 2, HALF), np.float32)
+    unfold = np.zeros((side // 2, HALF + 8), np.float32)
     for r in range(side // 2):
         unfold[r, side // 2 - r] = 1.0
     return lanes, fold, unfold
@@ -112,7 +112,7 @@
         loads[item].wait()
         store = pltpu.make_async_copy(
             hold_ref.at[item],
-            slot_ref.at[owner, pl.ds(pl.multiple_of(rank * side, side), side), :],
+            slot_ref.at[owner, pl.ds(pl.multiple_of(rank * side, side), side), 0, :],
             out_sems.at[item],
         )
         store.start()
@@ -125,9 +125,9 @@
         fields = (local, turn_ref[item], shift_ref[0, best] + SHIFT, shift_ref[1, best] + SHIFT, bin_ref[item], target, 1)
         tag = jnp.zeros((1, side), jnp.int32)
         for at, value in enumerate(fields):
-            tag = jnp.where(lane == at, value, tag)
-        tag_ref[owner, pl.ds(rank, 1), :] = tag.astype(jnp.float32)
-    store = pltpu.make_async_copy(tag_ref, slot_ref.at[:, pl.ds(2 * side, TAG), :], tag_sem)
+            tag = jnp.where(lane == rank * TAG + at, value, tag)
+        tag_ref[owner] += tag.astype(jnp.float32)
+    store = pltpu.make_async_copy(tag_ref, slot_ref.at[:, 2 * side], tag_sem)
     store.start()
     stores.append(store)
     for store in stores:
@@ -138,7 +138,7 @@
     count, side, _ = particles.shape
     return pl.pallas_call(
         functools.partial(scatter_kernel, class_local, chips_y),
-        out_shape=jax.ShapeDtypeStruct((owners, 2 * side + TAG, side), jnp.float32),
+        out_shape=jax.ShapeDtypeStruct((owners, 2 * side + 1, 1, side), jnp.float32),
         in_specs=[pl.BlockSpec(memory_space=pltpu.HBM)] * 6,
         out_specs=pl.BlockSpec(memory_space=pltpu.HBM),
         scratch_shapes=[pltpu.SMEM((count,), jnp.int32)] * 4
@@ -146,7 +146,7 @@
             pltpu.SMEM(shift_list.shape[::-1], jnp.int32),
             pltpu.SMEM((owners,), jnp.int32),
             pltpu.VMEM((count, side, side), jnp.float32),
-            pltpu.VMEM((owners, TAG, side), jnp.float32),
+            pltpu.VMEM((owners, 1, side), jnp.float32),
             pltpu.SemaphoreType.DMA((5,)),
             pltpu.SemaphoreType.DMA((count,)),
             pltpu.SemaphoreType.DMA((count,)),
@@ -159,21 +159,38 @@
 
 def spectrum_kernel(step_sources, info_ref, image_ref, contrast_ref, turn_ref, row_ref, col_ref, left_ref, right_ref,
                     *refs):
-    keep_ref, give_ref, filt_ref, numer_ref, sems = refs[-5:]
+    keep_ref, give_ref, filt_ref, numer_ref, hold_ref, sems, in_sems = refs[-7:]
     side = image_ref.shape[-1]
     first = pl.program_id(0) * step_sources
+
+    def load(step):
+        part = pl.ds(step * step_sources, step_sources)
+        return pltpu.make_async_copy(
+            image_ref.at[part, pl.ds(0, 2 * side), 0, :], hold_ref.at[part], in_sems.at[step]
+        )
+
+    @pl.when(pl.program_id(0) == 0)
+    def _():
+        load(0).start()
+
     lane = lax.broadcasted_iota(jnp.int32, (1, side), 1)
 
     @pl.when(pl.program_id(0) == 0)
     def _():
         numer_ref[...] = jnp.zeros_like(numer_ref)
+
+    load(pl.program_id(0)).wait()
+
+    @pl.when(pl.program_id(0) < pl.num_programs(0) - 1)
+    def _():
+        load(pl.program_id(0) + 1).start()
 
     turns = [info_ref[first + item // 2, item % 2, 1] for item in range(2 * step_sources)]
     parts = []
     for at in range(step_sources):
         highs, lows = [], []
         for k in range(2):
-            image = image_ref[at, k * side : (k + 1) * side]
+            image = hold_ref[first + at, k * side : (k + 1) * side]
             odd = lax.rem(turns[2 * at + k], 2) == 1
             high, low = split(jnp.where(odd, image.T, image))
             highs.append(high)
@@ -268,8 +285,8 @@
 
 
 def owner_spectra(info, images, contrast, turn, row, col, left, right, ready, class_local):
-    sources, _, side = images.shape
-    step_sources = 4
+    sources, _, _, side = images.shape
+    step_sources = 8
     whole = lambda x: pl.BlockSpec(x.shape, lambda i: (0,) * x.ndim)
     tables = (contrast, turn, row, col, left, right)
     half = jax.ShapeDtypeStruct((class_local // 2, HALF, 2 * side), jnp.float32)
@@ -283,7 +300,7 @@
         ),
         in_specs=[
             pl.BlockSpec(memory_space=pltpu.SMEM),
-            pl.BlockSpec((step_sources, 2 * side, side), lambda i: (i, 0, 0)),
+            pl.BlockSpec(memory_space=pltpu.HBM),
         ]
         + [whole(table) for table in tables]
         + [pl.BlockSpec(memory_space=pl.ANY)] * len(ready),
@@ -294,16 +311,18 @@
         ),
         scratch_shapes=[
             pltpu.VMEM((class_local, HALF, 2 * side), jnp.float32),
+            pltpu.VMEM((sources, 2 * side, side), jnp.float32),
             pltpu.SemaphoreType.DMA((2,)),
+            pltpu.SemaphoreType.DMA((sources // step_sources,)),
         ],
-        compiler_params=pltpu.CompilerParams(vmem_limit_bytes=24 * MIB),
+        compiler_params=pltpu.CompilerParams(vmem_limit_bytes=32 * MIB),
         name="owner_spectra",
     )(info, images, *tables, *ready)
 
 
 def owner_scores(info, filtered, refs, col, row):
     items, _, wide = filtered.shape
-    step_sources = 4
+    step_sources = 16
     whole = lambda x: pl.BlockSpec(x.shape, lambda i: (0,) * x.ndim)
     return pl.pallas_call(
         functools.partial(score_kernel, step_sources),
@@ -315,58 +334,60 @@
             whole(refs), whole(col), whole(row),
         ],
         out_specs=pl.BlockSpec((step_sources, 1, wide // 2), lambda i: (i, 0, 0)),
-        compiler_params=pltpu.CompilerParams(vmem_limit_bytes=24 * MIB),
+        compiler_params=pltpu.CompilerParams(vmem_limit_bytes=40 * MIB),
         name="owner_scores",
     )(info, filtered, refs, col, row)
 
 
-def finish_kernel(mine_ref, a_ref, b_ref, c_ref, contrast_ref, lanes_ref, unfold_ref, out_ref):
-    side = out_ref.shape[-1]
-    for at in range(out_ref.shape[0]):
+def finish_kernel(target_ref, mine_ref, a_ref, b_ref, c_ref, contrast_ref, lanes_ref, unfold_ref, home_ref,
+                  fresh_ref, score_ref):
+    classes, _, _, side = fresh_ref.shape
+    squares = [contrast_ref[which] * contrast_ref[which] for which in range(contrast_ref.shape[0])]
+    ratios = []
+    for at in range(classes):
         total = (mine_ref[at] + a_ref[at]) + (b_ref[at] + c_ref[at])
         weight = jnp.zeros((HALF, side), jnp.float32)
-        for which in range(contrast_ref.shape[0]):
-            contrast = contrast_ref[which]
-            weight += total[COUNT : COUNT + 1, which : which + 1] * (contrast * contrast)
+        for which, square in enumerate(squares):
+            weight += total[COUNT : COUNT + 1, which : which + 1] * square
         inverse = 1.0 / (weight + 1.0)
         for part in range(2):
             ratio = total[:, part * side : (part + 1) * side] * inverse
-            back = jnp.dot(
-                ratio, lanes_ref[...], precision=lax.Precision.HIGHEST, preferred_element_type=jnp.float32
-            )
-            back = jnp.dot(
-                unfold_ref[...], back, precision=lax.Precision.HIGHEST, preferred_element_type=jnp.float32
-            )
-            out_ref[at, part, : side // 2] = ratio[: side // 2]
-            out_ref[at, part, side // 2 :] = back if part == 0 else -back
-
-
-def finish(blocks, contrast, lanes, unfold, side):
-    return pl.pallas_call(
-        finish_kernel,
-        out_shape=jax.ShapeDtypeStruct((blocks[0].shape[0], 2, side, side), jnp.float32),
-        compiler_params=pltpu.CompilerParams(vmem_limit_bytes=16 * MIB),
-        name="finish",
-    )(*blocks, contrast, lanes, unfold)
-
-
-def pick_kernel(target_ref, home_ref, out_ref):
-    items, shifts = out_ref.shape
+            fresh_ref[at, part, : side // 2] = ratio[: side // 2]
+            ratios.append(ratio)
+    high, low = split(jnp.concatenate(ratios, axis=0))
+    flipped = jnp.dot(high, lanes_ref[...], preferred_element_type=jnp.float32) + jnp.dot(
+        low, lanes_ref[...], preferred_element_type=jnp.float32
+    )
+    flipped = [flipped[at * HALF : (at + 1) * HALF] for at in range(2 * classes)]
+    pad = jnp.zeros((unfold_ref.shape[1] - HALF, 2 * classes * side), jnp.float32)
+    high, low = split(jnp.concatenate([jnp.concatenate(flipped, axis=1), pad], axis=0))
+    back = jnp.dot(unfold_ref[...], high, preferred_element_type=jnp.float32) + jnp.dot(
+        unfold_ref[...], low, preferred_element_type=jnp.float32
+    )
+    for at in range(classes):
+        for part in range(2):
+            first = (2 * at + part) * side
+            block = back[:, first : first + side]
+            fresh_ref[at, part, side // 2 :] = block if part == 0 else -block
+    items, shifts = score_ref.shape
     for item in range(items):
         target = target_ref[item]
         row = home_ref[lax.div(target, 2)]
         row = jnp.where(lax.rem(target, 2) == 1, pltpu.roll(row, shifts, axis=1), row)
-        out_ref[item : item + 1, :] = row[:, :shifts]
-
-
-def pick(target, home):
+        score_ref[item : item + 1, :] = row[:, :shifts]
+
+
+def finish(target, blocks, contrast, lanes, unfold, home, side):
     return pl.pallas_call(
-        pick_kernel,
-        out_shape=jax.ShapeDtypeStruct((target.shape[0], home.shape[-1] // 2), jnp.float32),
-        in_specs=[pl.BlockSpec(memory_space=pltpu.SMEM), pl.BlockSpec(memory_space=pltpu.VMEM)],
+        finish_kernel,
+        out_shape=(
+            jax.ShapeDtypeStruct((blocks[0].shape[0], 2, side, side), jnp.float32),
+            jax.ShapeDtypeStruct((target.shape[0], side // 2), jnp.float32),
+        ),
+        in_specs=[pl.BlockSpec(memory_space=pltpu.SMEM)] + [pl.BlockSpec(memory_space=pltpu.VMEM)] * 8,
         compiler_params=pltpu.CompilerParams(vmem_limit_bytes=16 * MIB),
-        name="pick",
-    )(target, home)
+        name="finish",
+    )(target, *blocks, contrast, lanes, unfold, home)
 
 
 def body(
@@ -419,7 +440,7 @@
     refs = jnp.concatenate([top[:, 0] + folded[:, 0], top[:, 1] - folded[:, 1]], axis=2)
 
     refs = pltpu.with_memory_space_constraint(refs, pltpu.HBM)
-    info = images[:, 2 * side : 2 * side + 2, :8].astype(jnp.int32)
+    info = images[:, 2 * side, 0, : 2 * TAG].astype(jnp.int32).reshape(owners, 2, TAG)
     left, right = dft_constants(side)
     best_row, best_col = shift_constants(side)
     keep, give, filtered = owner_spectra(
@@ -430,22 +451,21 @@
 
     got = lax.ppermute(give, "grp", [(i, i ^ 1) for i in range(groups)])
     got, slot_scores = lax.optimization_barrier((got, slot_scores))
-    blocks = []
-    for step in range(chips_y):
+    blocks = {}
+    for step in (2, 1, 3, 0):
         part = slice(step * own_classes, (step + 1) * own_classes)
         block = keep[part] + got[part]
         pairs = [(i, ((i // cores + step) % chips_y) * cores + i % cores) for i in range(groups)]
-        blocks.append(lax.ppermute(block, "grp", pairs) if step else block)
+        blocks[step] = lax.ppermute(block, "grp", pairs) if step else block
 
     home = lax.all_to_all(slot_scores, "cls", split_axis=0, concat_axis=0, tiled=True)
-    fresh_refs = finish(
-        blocks, contrast, jnp.asarray(lanes), jnp.asarray(unfold), side
-    )
-    home, fresh_refs = lax.optimization_barrier((home, fresh_refs))
     owner_of = class_of // class_local
     earlier = jnp.tril(owner_of[:, None] == owner_of[None, :], -1)
-    scores = pick(owner_of * 2 + jnp.sum(earlier.astype(jnp.int32), axis=1), home)
-
+    target = owner_of * 2 + jnp.sum(earlier.astype(jnp.int32), axis=1)
+    fresh_refs, scores = finish(
+        target, [blocks[step] for step in range(chips_y)], contrast, jnp.asarray(lanes, jnp.bfloat16),
+        jnp.asarray(unfold, jnp.bfloat16), home, side,
+    )
     return (scores, fresh_refs)
 
 

time: 156 us -> 150 us (0.962)
  Pallas kernels: 24 us -> 19.1 us
  waiting for transfers between devices: 93.3 us -> 91 us
    all_to_all x1, waiting for transfers between devices: 0.01 us -> 8.55 us  [body(): lax.all_to_all(slot_scores, 'cls', split_axis=0, concat_axis=0, tiled=True)]
    ppermute x3, waiting for transfers between devices: 8.14 us -> 0.01 us  [body(): blocks[step] = lax.ppermute(block, 'grp', pairs) if step else block]
    all_to_all x1, waiting for transfers between devices: 85.2 us -> 82.5 us  [body(): lax.all_to_all(send, 'cls', split_axis=0, concat_axis=0, tiled=True)]
    pallas_call x2 -> x1, Pallas kernels: 4.2 us -> 2.11 us  [finish(): pl.pallas_call(finish_kernel, out_shape=(jax.ShapeDtypeStruct((blocks[0]....]
    pallas_call x1, Pallas kernels: 6.11 us -> 4.16 us  [owner_scores(): pl.pallas_call(functools.partial(score_kernel, step_sources), grid=(items...]
  transfers between devices with their start and end apart: 6 -> 6, of which waited for: 3 -> 2; matrix products, arithmetic and copies ran while one was open for 6% -> 7% of each run, Pallas kernels for 6% -> 3%
where the time goes in v4:
time: 150 us; the launch traced here: 149 us
  waiting for transfers between devices  91 us (61%)
  starting transfers between devices  26.5 us (18%)
  Pallas kernels  19.1 us (13%)
  other arithmetic  7.95 us (5%)
  matrix products  2.73 us (2%)
    all_to_all x1, waiting for transfers between devices, body(): lax.all_to_all(send, 'cls', split_axis=0, concat_axis=0, tiled=True)  82.5 us
    all_to_all x1, starting transfers between devices, body(): lax.all_to_all(send, 'cls', split_axis=0, concat_axis=0, tiled=True)  12 us
    pallas_call x1, Pallas kernels, owner_spectra(): pl.pallas_call(functools.partial(spectrum_kernel, step_sources), grid=(so...  9.8 us
    all_to_all x1, waiting for transfers between devices, body(): lax.all_to_all(slot_scores, 'cls', split_axis=0, concat_axis=0, tiled=True)  8.55 us
    ppermute x1, starting transfers between devices, body(): got = lax.ppermute(give, 'grp', [(i, i ^ 1) for i in range(groups)])  5.43 us
    ppermute x3, starting transfers between devices, body(): blocks[step] = lax.ppermute(block, 'grp', pairs) if step else block  5.27 us
    pallas_call x1, Pallas kernels, owner_scores(): pl.pallas_call(functools.partial(score_kernel, step_sources), grid=(items...  4.16 us
    all_to_all x1, starting transfers between devices, body(): lax.all_to_all(slot_scores, 'cls', split_axis=0, concat_axis=0, tiled=True)  3.84 us
  transfers between devices with their start and end apart: 6, of which 2 were waited for; matrix products, arithmetic and copies ran while one was open for 7% of the time, Pallas kernels for 3%

profile of v4, /device:TPU:1, one launch (start us, length us, event | category | flops | bytes accessed | tf_op | source)
XLA Modules:
  0.0 149.4 jit_solution(4892107234435013830)
XLA Ops:
  0.6 3.1 %place_slots.1 = f32[32,257,1,128]{3,2,1,0:T(1,128)} custom-call(s32[32]{0:T(128)} %class_hbm.1, s32[32]{0:T(128)} %turn_hbm.1, s32[32]{0:T(128)} %best_hbm.1, s32[32]{0:T(128)} %bin_hbm.1, s32[2,64]{1,0:T(2,128)} %bitcast.20, f32[32,128,128]{2,1,0:T(8,128)} %image_ref.1), custom_call_target="tpu_custom_call" | custom-call | tf_op jit(solution)/shard_map/place_slots/pallas_call | solution.py:139
  3.7 0.0 copy-start.10
  3.7 12.0 %all-to-all-start = ((f32[32,257,1,128]{3,2,1,0:T(1,128)}), f32[32,257,1,128]{3,2,1,0:T(1,128)}, u32[]{:S(2)}, u32[]{:S(2)}) async-start(f32[32,257,1,128]{3,2,1,0:T(1,128)} %place_slots.1), calls=%async_computation | async-start | bytes 8421376 | tf_op jit(solution)/shard_map/all_to_all | solution.py:409
  15.7 0.0 copy-done.10
  15.7 0.2 fusion.24
  15.9 0.1 maximum_multiply_fusion.refs_2_.row_ref
  16.0 0.3 fusion.21
  16.3 0.1 reduce-precision_convert_fusion
  16.4 0.0 copy-start.7
  16.4 0.0 copy-start.9
  16.4 2.0 %copy_multiply_fusion = f32[32,2,72,128]{3,2,0,1:T(8,128)S(1)} fusion(f32[72]{0:T(128)S(1)} %compare_convert_fusion, f32[32,2,128,128]{3,2,1,0:T(8,128)} %param.18), kind=kLoop, calls=%fused_computation.1 | loop fusion | flops 589824 | bytes 4718880 | tf_op jit(solution)/shard_map/mul | solution.py:439
  18.5 0.8 copy-done.7
  19.3 0.0 copy-done.9
  19.3 1.6 %convolution_bitcast_fusion = f32[32,2,72,128]{3,2,1,0:T(8,128)S(1)} fusion(f32[72,128,1,1]{1,0,3,2:T(8,128)S(1)} %copy-done.9, f32[32,2,128,128]{3,2,1,0:T(8,128)S(1)} %copy-done.7), kind=kOutput, calls=%fused_computation.4 | convolution fusion | flops 452984832 | bytes 6590464 | tf_op jit(solution)/shard_map/ua,ciab->ciub/dot_general | solution.py:437
  21.0 0.0 copy-done.8
  21.0 1.1 fusion
  22.1 0.2 fusion.3
  22.3 0.0 copy-start.12
  22.3 0.0 copy-start
  22.4 0.0 copy-start.1
  22.4 0.0 copy-start.2
  22.4 0.0 copy-start.3
  22.4 0.0 copy-start.5
  22.4 1.6 %pad_maximum_fusion.refs_0_.ref_ref = f32[32,72,256]{2,1,0:T(8,128)} fusion(f32[32,72,128]{2,1,0:T(8,128)S(1)} %get-tuple-element.17, f32[32,72,128]{2,1,0:T(8,128)S(1)} %get-tuple-element.16), kind=kLoop, calls=%fused_computation | loop fusion | flops 589824 | bytes 4718592 | tf_op jit(solution)/shard_map/concatenate | solution.py:440
  24.0 0.1 add_multiply_fusion
  24.1 2.2 %fusion.6.contrast_ref = f32[16,72,128]{2,1,0:T(8,128)S(1)} fusion(f32[72,128]{1,0:T(8,128)S(1)} %add_multiply_fusion, f32[16]{0:T(128)S(1)} %copy-done.12), kind=kLoop, calls=%fused_computation.13 | loop fusion | flops 737280 | bytes 626752 | tf_op jit(solution)/shard_map/neg | solution.py:417
  26.3 82.5 %all-to-all-done.image_ref = f32[32,257,1,128]{3,2,1,0:T(1,128)} async-done(((f32[32,257,1,128]{3,2,1,0:T(1,128)}), f32[32,257,1,128]{3,2,1,0:T(1,128)}, u32[]{:S(2)}, u32[]{:S(2)}) %all-to-all-start) | async-done | bytes 4210720 | tf_op jit(solution)/shard_map/all_to_all | solution.py:409
  108.8 0.7 slice_convert_fusion
  109.5 0.1 copy.34
  109.6 0.1 copy.38.info_ref
  109.7 0.0 copy-start.11
  109.8 9.8 %owner_spectra.1 = (f32[16,72,256]{2,1,0:T(8,128)S(1)}, f32[16,72,256]{2,1,0:T(8,128)S(1)}, f32[64,72,256]{2,1,0:T(8,128)S(1)}) custom-call(s32[32,2,8]{2,1,0:T(2,128)S(1)} %copy.38.info_ref, f32[32,257,1,128]{3,2,1,0:T(1,128)} %all-to-all-done.image_ref, f32[16,72,128]{2,1,0:T(8,128)S(1)} %fusion.6.contrast_ref, f32[4,72,256]{2,1,0:T(8,128)S(1)} %copy-done.2, ...), custom_call_target="tpu_custom_call" | custom-call | tf_op jit(solution)/shard_map/owner_spectra/pallas_call | solution.py:293
  119.6 5.4 %collective-permute-start = (f32[16,72,256]{2,1,0:T(8,128)S(1)}, f32[16,72,256]{2,1,0:T(8,128)S(1)}, u32[]{:S(2)}, u32[]{:S(2)}) collective-permute-start(f32[16,72,256]{2,1,0:T(8,128)S(1)} %get-tuple-element.10), channel_id=1, source_target_pairs={{0,32},{32,0},{64,96},{96,64},{128,160},{160,128},{192,224},{224,1... | collective-permute-start | bytes 3538952 | tf_op jit(solution)/shard_map/ppermute | solution.py:452
  125.0 4.2 %owner_scores.1 = f32[32,1,128]{2,1,0:T(1,128)} custom-call(s32[32,2,8]{2,1,0:T(2,128)S(1)} %copy.38.info_ref, f32[64,72,256]{2,1,0:T(8,128)S(1)} %get-tuple-element.11.filt_ref, f32[32,72,256]{2,1,0:T(8,128)} %pad_maximum_fusion.refs_0_.ref_ref, bf16[512,256]{1,0:T(8,128)(2,1)S(1)} %maximum_maximum_fusion.refs_1_.col_ref, ...), custom_call_target="tpu_custom_call" | custom-call | tf_op jit(solution)/shard_map/owner_scores/pallas_call | solution.py:327
  129.2 0.0 collective-permute-done
  129.2 0.2 slice_add_fusion.1
  129.4 1.5 %collective-permute-start.1 = (f32[4,72,256]{2,1,0:T(8,128)S(1)}, f32[4,72,256]{2,1,0:T(8,128)S(1)}, u32[]{:S(2)}, u32[]{:S(2)}) collective-permute-start(f32[4,72,256]{2,1,0:T(8,128)S(1)} %get-tuple-element.20), channel_id=1, source_target_pairs={{0,64},{32,96},{64,128},{96,160},{128,192},{160,224},{192,0},{224,... | collective-permute-start | bytes 884744 | tf_op jit(solution)/shard_map/ppermute | solution.py:459
  130.9 2.6 %collective-permute-start.2 = (f32[4,72,256]{2,1,0:T(8,128)S(1)}, f32[4,72,256]{2,1,0:T(8,128)S(1)}, u32[]{:S(2)}, u32[]{:S(2)}) collective-permute-start(f32[4,72,256]{2,1,0:T(8,128)S(1)} %get-tuple-element.19), channel_id=1, source_target_pairs={{0,128},{32,160},{64,192},{96,224},{128,0},{160,32},{192,64},{224,... | collective-permute-start | bytes 884744 | tf_op jit(solution)/shard_map/ppermute | solution.py:459
  133.4 1.2 collective-permute-start.3
  134.6 0.2 convert_reduce_fusion
  134.8 3.8 %all-to-all-start.1 = ((f32[32,1,128]{2,1,0:T(1,128)}), f32[32,1,128]{2,1,0:T(1,128)S(1)}, u32[]{:S(2)}, u32[]{:S(2)}) async-start(f32[32,1,128]{2,1,0:T(1,128)} %owner_scores.1), calls=%async_computation.1 | async-start | bytes 32768 | tf_op jit(solution)/shard_map/all_to_all | solution.py:461
  138.7 8.5 %all-to-all-done.1.home_ref = f32[32,1,128]{2,1,0:T(1,128)S(1)} async-done(((f32[32,1,128]{2,1,0:T(1,128)}), f32[32,1,128]{2,1,0:T(1,128)S(1)}, u32[]{:S(2)}, u32[]{:S(2)}) %all-to-all-start.1) | async-done | bytes 16416 | tf_op jit(solution)/shard_map/all_to_all | solution.py:461
  147.2 0.0 collective-permute-done.1.a_ref
  147.2 0.0 collective-permute-done.2.b_ref
  147.2 0.0 collective-permute-done.3.c_ref
  147.2 0.0 copy-done.4
  147.2 0.0 copy-done.6
  147.2 2.1 %finish.1 = (f32[4,2,128,128]{3,2,1,0:T(8,128)}, f32[32,64]{1,0:T(8,128)}) custom-call(s32[32]{0:T(128)S(1)} %multiply_add_fusion.target_ref, f32[4,72,256]{2,1,0:T(8,128)S(1)} %get-tuple-element.21.mine_ref, f32[4,72,256]{2,1,0:T(8,128)S(1)} %collective-permute-done.1.a_ref, f32[4,72,256]{2,1,0:T(8,128)S(1)} %collective-permute-done.2.b_ref, ...), custom_call_target="tpu_custom_call" | custom-call | tf_op jit(solution)/shard_map/finish/pallas_call | solution.py:381
  (18 shorter events, 0.1 us)
Async XLA Ops:
  3.7 12.0 %copy-start.10 = (s32[64,2]{0,1:T(2,128)S(1)}, s32[64,2]{0,1:T(2,128)}, u32[]{:S(2)}) copy-start(s32[64,2]{0,1:T(2,128)} %param.23) | copy-start | bytes 1540
  3.7 105.1 %all-to-all-start = ((f32[32,257,1,128]{3,2,1,0:T(1,128)}), f32[32,257,1,128]{3,2,1,0:T(1,128)}, u32[]{:S(2)}, u32[]{:S(2)}) async-start(f32[32,257,1,128]{3,2,1,0:T(1,128)} %place_slots.1), calls=%async_computation | async-start | bytes 8421376 | tf_op jit(solution)/shard_map/all_to_all | solution.py:409
  16.4 2.9 %copy-start.7 = (f32[32,2,128,128]{3,2,1,0:T(8,128)S(1)}, f32[32,2,128,128]{3,2,1,0:T(8,128)}, u32[]{:S(2)}) copy-start(f32[32,2,128,128]{3,2,1,0:T(8,128)} %param.18) | copy-start | bytes 12582916
  16.4 2.9 %copy-start.9 = (f32[72,128,1,1]{1,0,3,2:T(8,128)S(1)}, f32[72,128,1,1]{1,0,3,2:T(8,128)}, u32[]{:S(2)}) copy-start(f32[72,128,1,1]{1,0,3,2:T(8,128)} %constant.99) | copy-start | bytes 110596
  19.3 1.7 %copy-start.8 = (f32[128,128,1,1]{1,0,2,3:T(8,128)S(1)}, f32[128,128,1,1]{1,0,2,3:T(8,128)}, u32[]{:S(2)}) copy-start(f32[128,128,1,1]{1,0,2,3:T(8,128)} %constant.100) | copy-start | bytes 196612
  22.3 1.8 %copy-start.12 = (f32[16]{0:T(128)S(1)}, f32[16]{0:T(128)}, u32[]{:S(2)}) copy-start(f32[16]{0:T(128)} %param.24) | copy-start | bytes 196
  22.3 87.4 %copy-start = (f32[17,72,256]{2,1,0:T(8,128)S(1)}, f32[17,72,256]{2,1,0:T(8,128)}, u32[]{:S(2)}) copy-start(f32[17,72,256]{2,1,0:T(8,128)} %constant.88.clone.row_ref) | copy-start | bytes 3760132
  22.4 87.3 %copy-start.1 = (bf16[768,256]{1,0:T(8,128)(2,1)S(1)}, bf16[768,256]{1,0:T(8,128)(2,1)}, u32[]{:S(2)}) copy-start(bf16[768,256]{1,0:T(8,128)(2,1)} %constant.91.clone.right_ref) | copy-start | bytes 1179652
  22.4 87.3 %copy-start.2 = (f32[4,72,256]{2,1,0:T(8,128)S(1)}, f32[4,72,256]{2,1,0:T(8,128)}, u32[]{:S(2)}) copy-start(f32[4,72,256]{2,1,0:T(8,128)} %constant.87.clone.turn_ref) | copy-start | bytes 884740
  22.4 87.3 %copy-start.3 = (bf16[288,256]{1,0:T(8,128)(2,1)S(1)}, bf16[288,256]{1,0:T(8,128)(2,1)}, u32[]{:S(2)}) copy-start(bf16[288,256]{1,0:T(8,128)(2,1)} %constant.90.clone.left_ref) | copy-start | bytes 442372
  22.4 87.3 %copy-start.5 = (f32[17,1,256]{2,1,0:T(1,128)S(1)}, f32[17,1,256]{2,1,0:T(1,128)}, u32[]{:S(2)}) copy-start(f32[17,1,256]{2,1,0:T(1,128)} %constant.89.clone.col_ref) | copy-start | bytes 52228
  109.7 15.3 %copy-start.11 = (s32[32]{0:T(128)S(1)}, s32[32]{0:T(128)}, u32[]{:S(2)}) copy-start(s32[32]{0:T(128)} %class_hbm.1) | copy-start | bytes 388
  119.6 9.6 %collective-permute-start = (f32[16,72,256]{2,1,0:T(8,128)S(1)}, f32[16,72,256]{2,1,0:T(8,128)S(1)}, u32[]{:S(2)}, u32[]{:S(2)}) collective-permute-start(f32[16,72,256]{2,1,0:T(8,128)S(1)} %get-tuple-element.10), channel_id=1, source_target_pairs={{0,32},{32,0},{64,96},{96,64},{128,160},{160,128},{192,224},{224,1... | collective-permute-start | bytes 3538952 | tf_op jit(solution)/shard_map/ppermute | solution.py:452
  129.2 18.1 %copy-start.4 = (bf16[128,128]{1,0:T(8,128)(2,1)S(1)}, bf16[128,128]{1,0:T(8,128)(2,1)}, u32[]{:S(2)}) copy-start(bf16[128,128]{1,0:T(8,128)(2,1)} %constant.92.clone.lanes_ref) | copy-start | bytes 98308
  129.2 18.1 %copy-start.6 = (bf16[64,80]{1,0:T(8,128)(2,1)S(1)}, bf16[64,80]{1,0:T(8,128)(2,1)}, u32[]{:S(2)}) copy-start(bf16[64,80]{1,0:T(8,128)(2,1)} %constant.93.clone.unfold_ref) | copy-start | bytes 30724
  129.4 17.9 %collective-permute-start.1 = (f32[4,72,256]{2,1,0:T(8,128)S(1)}, f32[4,72,256]{2,1,0:T(8,128)S(1)}, u32[]{:S(2)}, u32[]{:S(2)}) collective-permute-start(f32[4,72,256]{2,1,0:T(8,128)S(1)} %get-tuple-element.20), channel_id=1, source_target_pairs={{0,64},{32,96},{64,128},{96,160},{128,192},{160,224},{192,0},{224,... | collective-permute-start | bytes 884744 | tf_op jit(solution)/shard_map/ppermute | solution.py:459
  130.9 16.4 %collective-permute-start.2 = (f32[4,72,256]{2,1,0:T(8,128)S(1)}, f32[4,72,256]{2,1,0:T(8,128)S(1)}, u32[]{:S(2)}, u32[]{:S(2)}) collective-permute-start(f32[4,72,256]{2,1,0:T(8,128)S(1)} %get-tuple-element.19), channel_id=1, source_target_pairs={{0,128},{32,160},{64,192},{96,224},{128,0},{160,32},{192,64},{224,... | collective-permute-start | bytes 884744 | tf_op jit(solution)/shard_map/ppermute | solution.py:459
  133.4 13.8 %collective-permute-start.3 = (f32[4,72,256]{2,1,0:T(8,128)S(1)}, f32[4,72,256]{2,1,0:T(8,128)S(1)}, u32[]{:S(2)}, u32[]{:S(2)}) collective-permute-start(f32[4,72,256]{2,1,0:T(8,128)S(1)} %get-tuple-element.18), channel_id=1, source_target_pairs={{0,192},{32,224},{64,0},{96,32},{128,64},{160,96},{192,128},{224,1... | collective-permute-start | bytes 884744 | tf_op jit(solution)/shard_map/ppermute | solution.py:459
  134.8 12.4 %all-to-all-start.1 = ((f32[32,1,128]{2,1,0:T(1,128)}), f32[32,1,128]{2,1,0:T(1,128)S(1)}, u32[]{:S(2)}, u32[]{:S(2)}) async-start(f32[32,1,128]{2,1,0:T(1,128)} %owner_scores.1), calls=%async_computation.1 | async-start | bytes 32768 | tf_op jit(solution)/shard_map/all_to_all | solution.py:461

commit v5 on v4

--- a/solution.py
+++ b/solution.py
@@ -106,7 +106,6 @@
     stores = []
     for item in range(items):
         owner = lax.div(class_ref[item], class_local)
-        local = class_ref[item] - owner * class_local
         rank = count_ref[owner]
         count_ref[owner] = rank + 1
         loads[item].wait()
@@ -117,6 +116,7 @@
         )
         store.start()
         stores.append(store)
+        local = class_ref[item] - owner * class_local
         place = lax.div(local, own)
         other = lax.rem(lax.rem(place, cores) - core + cores, cores)
         step = lax.rem(lax.div(place, cores) - me_y + chips_y, chips_y)
@@ -157,11 +157,16 @@
     )(class_of, rotation_bin, shift_best, defocus_bin, shift_list.T, particles)
 
 
-def spectrum_kernel(step_sources, info_ref, image_ref, contrast_ref, turn_ref, row_ref, col_ref, left_ref, right_ref,
+def read_tag(tag_ref, source, slot, at):
+    return tag_ref[source, 0, slot * TAG + at].astype(jnp.int32)
+
+
+def spectrum_kernel(step_sources, image_ref, contrast_ref, turn_ref, row_ref, col_ref, left_ref, right_ref,
                     *refs):
-    keep_ref, give_ref, filt_ref, numer_ref, hold_ref, sems, in_sems = refs[-7:]
+    keep_ref, give_ref, filt_ref, local_ref, numer_ref, hold_ref, tag_ref, sems, in_sems, tag_sem = refs[-10:]
     side = image_ref.shape[-1]
     first = pl.program_id(0) * step_sources
+    lane = lax.broadcasted_iota(jnp.int32, (1, side), 1)
 
     def load(step):
         part = pl.ds(step * step_sources, step_sources)
@@ -171,13 +176,11 @@
 
     @pl.when(pl.program_id(0) == 0)
     def _():
+        tags = pltpu.make_async_copy(image_ref.at[:, 2 * side], tag_ref, tag_sem)
+        tags.start()
         load(0).start()
-
-    lane = lax.broadcasted_iota(jnp.int32, (1, side), 1)
-
-    @pl.when(pl.program_id(0) == 0)
-    def _():
         numer_ref[...] = jnp.zeros_like(numer_ref)
+        tags.wait()
 
     load(pl.program_id(0)).wait()
 
@@ -185,7 +188,7 @@
     def _():
         load(pl.program_id(0) + 1).start()
 
-    turns = [info_ref[first + item // 2, item % 2, 1] for item in range(2 * step_sources)]
+    turns = [read_tag(tag_ref, first + item // 2, item % 2, 1) for item in range(2 * step_sources)]
     parts = []
     for at in range(step_sources):
         highs, lows = [], []
@@ -212,7 +215,8 @@
         jnp.concatenate([high, low, high], axis=1), right_ref[...], preferred_element_type=jnp.float32
     )
     for item in range(2 * step_sources):
-        info = [info_ref[first + item // 2, item % 2, at] for at in range(7)]
+        info = [read_tag(tag_ref, first + item // 2, item % 2, at) for at in range(7)]
+        local_ref[2 * first + item] = info[0]
         rows = slice(item * HALF, (item + 1) * HALF)
         sign = jnp.where(turns[item] >= 2, -1.0, 1.0).astype(jnp.float32)
         real = spectrum[rows, :side]
@@ -250,12 +254,12 @@
             copy.wait()
 
 
-def score_kernel(step_sources, info_ref, filt_ref, ref_ref, col_ref, row_ref, score_ref):
+def score_kernel(step_sources, local_ref, filt_ref, ref_ref, col_ref, row_ref, score_ref):
     side = score_ref.shape[-1]
-    first = pl.program_id(0) * step_sources
+    first = pl.program_id(0) * step_sources * 2
     products = []
     for item in range(2 * step_sources):
-        ref = ref_ref[info_ref[first + item // 2, item % 2, 0]]
+        ref = ref_ref[local_ref[first + item]]
         ref_real, ref_imag = ref[:, :side], ref[:, side:]
         filt_real, filt_imag = filt_ref[item, :, :side], filt_ref[item, :, side:]
         products.append(
@@ -284,7 +288,7 @@
         score_ref[at] = jnp.where(lane < side // 2, sums[0], sums[1])
 
 
-def owner_spectra(info, images, contrast, turn, row, col, left, right, ready, class_local):
+def owner_spectra(images, contrast, turn, row, col, left, right, ready, class_local):
     sources, _, _, side = images.shape
     step_sources = 8
     whole = lambda x: pl.BlockSpec(x.shape, lambda i: (0,) * x.ndim)
@@ -297,30 +301,31 @@
             half,
             half,
             jax.ShapeDtypeStruct((2 * sources, HALF, 2 * side), jnp.float32),
+            jax.ShapeDtypeStruct((2 * sources,), jnp.int32),
         ),
-        in_specs=[
-            pl.BlockSpec(memory_space=pltpu.SMEM),
-            pl.BlockSpec(memory_space=pltpu.HBM),
-        ]
+        in_specs=[pl.BlockSpec(memory_space=pltpu.HBM)]
         + [whole(table) for table in tables]
         + [pl.BlockSpec(memory_space=pl.ANY)] * len(ready),
         out_specs=(
             pl.BlockSpec(memory_space=pltpu.HBM),
             pl.BlockSpec(memory_space=pltpu.HBM),
             pl.BlockSpec((2 * step_sources, HALF, 2 * side), lambda i: (i, 0, 0)),
+            pl.BlockSpec(memory_space=pltpu.SMEM),
         ),
         scratch_shapes=[
             pltpu.VMEM((class_local, HALF, 2 * side), jnp.float32),
             pltpu.VMEM((sources, 2 * side, side), jnp.float32),
+            pltpu.SMEM((sources, 1, side), jnp.float32),
             pltpu.SemaphoreType.DMA((2,)),
             pltpu.SemaphoreType.DMA((sources // step_sources,)),
+            pltpu.SemaphoreType.DMA,
         ],
         compiler_params=pltpu.CompilerParams(vmem_limit_bytes=32 * MIB),
         name="owner_spectra",
-    )(info, images, *tables, *ready)
-
-
-def owner_scores(info, filtered, refs, col, row):
+    )(images, *tables, *ready)
+
+
+def owner_scores(local, filtered, refs, col, row):
     items, _, wide = filtered.shape
     step_sources = 16
     whole = lambda x: pl.BlockSpec(x.shape, lambda i: (0,) * x.ndim)
@@ -336,7 +341,7 @@
         out_specs=pl.BlockSpec((step_sources, 1, wide // 2), lambda i: (i, 0, 0)),
         compiler_params=pltpu.CompilerParams(vmem_limit_bytes=40 * MIB),
         name="owner_scores",
-    )(info, filtered, refs, col, row)
+    )(local, filtered, refs, col, row)
 
 
 def finish_kernel(target_ref, mine_ref, a_ref, b_ref, c_ref, contrast_ref, lanes_ref, unfold_ref, home_ref,
@@ -440,14 +445,13 @@
     refs = jnp.concatenate([top[:, 0] + folded[:, 0], top[:, 1] - folded[:, 1]], axis=2)
 
     refs = pltpu.with_memory_space_constraint(refs, pltpu.HBM)
-    info = images[:, 2 * side, 0, : 2 * TAG].astype(jnp.int32).reshape(owners, 2, TAG)
     left, right = dft_constants(side)
     best_row, best_col = shift_constants(side)
-    keep, give, filtered = owner_spectra(
-        info, images, contrast, jnp.asarray(turn_constants(side)), jnp.asarray(best_row),
+    keep, give, filtered, local = owner_spectra(
+        images, contrast, jnp.asarray(turn_constants(side)), jnp.asarray(best_row),
         jnp.asarray(best_col), jnp.asarray(left), jnp.asarray(right), (refs, col, row), class_local,
     )
-    slot_scores = owner_scores(info, filtered, refs, col, row)
+    slot_scores = owner_scores(local, filtered, refs, col, row)
 
     got = lax.ppermute(give, "grp", [(i, i ^ 1) for i in range(groups)])
     got, slot_scores = lax.optimization_barrier((got, slot_scores))

time: 150 us -> 150 us (level)
  no operation moved by 1% of the time
where the time goes in v5:
time: 150 us; the launch traced here: 149 us
  waiting for transfers between devices  91 us (61%)
  starting transfers between devices  27 us (18%)
  Pallas kernels  19.2 us (13%)
  other arithmetic  7.21 us (5%)
  matrix products  2.73 us (2%)
    all_to_all x1, waiting for transfers between devices, body(): lax.all_to_all(send, 'cls', split_axis=0, concat_axis=0, tiled=True)  82.5 us
    all_to_all x1, starting transfers between devices, body(): lax.all_to_all(send, 'cls', split_axis=0, concat_axis=0, tiled=True)  11.9 us
    pallas_call x1, Pallas kernels, owner_spectra(): pl.pallas_call(functools.partial(spectrum_kernel, step_sources), grid=(so...  9.96 us
    all_to_all x1, waiting for transfers between devices, body(): lax.all_to_all(slot_scores, 'cls', split_axis=0, concat_axis=0, tiled=True)  8.54 us
    ppermute x1, starting transfers between devices, body(): got = lax.ppermute(give, 'grp', [(i, i ^ 1) for i in range(groups)])  5.42 us
    ppermute x3, starting transfers between devices, body(): blocks[step] = lax.ppermute(block, 'grp', pairs) if step else block  5.31 us
    all_to_all x1, starting transfers between devices, body(): lax.all_to_all(slot_scores, 'cls', split_axis=0, concat_axis=0, tiled=True)  4.37 us
    pallas_call x1, Pallas kernels, owner_scores(): pl.pallas_call(functools.partial(score_kernel, step_sources), grid=(items...  4.16 us
  transfers between devices with their start and end apart: 6, of which 2 were waited for; matrix products, arithmetic and copies ran while one was open for 7% of the time, Pallas kernels for 3%

profile of v5, /device:TPU:1, one launch (start us, length us, event | category | flops | bytes accessed | tf_op | source)
XLA Modules:
  0.0 149.1 jit_solution(14959429926244418646)
XLA Ops:
  0.6 3.0 %place_slots.1 = f32[32,257,1,128]{3,2,1,0:T(1,128)} custom-call(s32[32]{0:T(128)} %class_hbm.1, s32[32]{0:T(128)} %turn_hbm.1, s32[32]{0:T(128)} %best_hbm.1, s32[32]{0:T(128)} %bin_hbm.1, s32[2,64]{1,0:T(2,128)} %bitcast.18, f32[32,128,128]{2,1,0:T(8,128)} %image_ref.1), custom_call_target="tpu_custom_call" | custom-call | tf_op jit(solution)/shard_map/place_slots/pallas_call | solution.py:139
  3.6 0.0 copy-start.10
  3.6 11.9 %all-to-all-start = ((f32[32,257,1,128]{3,2,1,0:T(1,128)}), f32[32,257,1,128]{3,2,1,0:T(1,128)}, u32[]{:S(2)}, u32[]{:S(2)}) async-start(f32[32,257,1,128]{3,2,1,0:T(1,128)} %place_slots.1), calls=%async_computation | async-start | bytes 8421376 | tf_op jit(solution)/shard_map/all_to_all | solution.py:414
  15.6 0.0 copy-done.10
  15.7 0.2 fusion.24
  15.8 0.1 maximum_multiply_fusion.refs_2_.row_ref
  15.9 0.3 fusion.21
  16.2 0.1 reduce-precision_convert_fusion
  16.3 0.0 copy-start.7
  16.3 0.0 copy-start.9
  16.4 2.0 %copy_multiply_fusion = f32[32,2,72,128]{3,2,0,1:T(8,128)S(1)} fusion(f32[72]{0:T(128)S(1)} %compare_convert_fusion, f32[32,2,128,128]{3,2,1,0:T(8,128)} %param.18), kind=kLoop, calls=%fused_computation.1 | loop fusion | flops 589824 | bytes 4718880 | tf_op jit(solution)/shard_map/mul | solution.py:444
  18.4 0.8 copy-done.7
  19.2 0.0 copy-done.9
  19.2 1.6 %convolution_bitcast_fusion = f32[32,2,72,128]{3,2,1,0:T(8,128)S(1)} fusion(f32[72,128,1,1]{1,0,3,2:T(8,128)S(1)} %copy-done.9, f32[32,2,128,128]{3,2,1,0:T(8,128)S(1)} %copy-done.7), kind=kOutput, calls=%fused_computation.4 | convolution fusion | flops 452984832 | bytes 6590464 | tf_op jit(solution)/shard_map/ua,ciab->ciub/dot_general | solution.py:442
  20.9 0.0 copy-done.8
  20.9 1.1 fusion
  22.0 0.2 fusion.3
  22.2 0.0 copy-start.12
  22.3 0.0 copy-start
  22.3 0.0 copy-start.1
  22.3 0.0 copy-start.2
  22.3 0.0 copy-start.3
  22.3 0.0 copy-start.5
  22.3 1.6 %pad_maximum_fusion.refs_0_.ref_ref = f32[32,72,256]{2,1,0:T(8,128)} fusion(f32[32,72,128]{2,1,0:T(8,128)S(1)} %get-tuple-element.19, f32[32,72,128]{2,1,0:T(8,128)S(1)} %get-tuple-element.18), kind=kLoop, calls=%fused_computation | loop fusion | flops 589824 | bytes 4718592 | tf_op jit(solution)/shard_map/concatenate | solution.py:445
  24.0 0.1 add_multiply_fusion
  24.0 0.0 copy-done.12
  24.0 2.2 %fusion.6.contrast_ref = f32[16,72,128]{2,1,0:T(8,128)S(1)} fusion(f32[72,128]{1,0:T(8,128)S(1)} %add_multiply_fusion, f32[16]{0:T(128)S(1)} %copy-done.12), kind=kLoop, calls=%fused_computation.13 | loop fusion | flops 737280 | bytes 626752 | tf_op jit(solution)/shard_map/neg | solution.py:422
  26.2 0.0 copy-start.11
  26.2 82.5 %all-to-all-done.image_ref = f32[32,257,1,128]{3,2,1,0:T(1,128)} async-done(((f32[32,257,1,128]{3,2,1,0:T(1,128)}), f32[32,257,1,128]{3,2,1,0:T(1,128)}, u32[]{:S(2)}, u32[]{:S(2)}) %all-to-all-start) | async-done | bytes 4210720 | tf_op jit(solution)/shard_map/all_to_all | solution.py:414
  108.7 0.0 copy-done
  108.7 0.0 copy-done.3
  108.8 0.0 copy-done.5
  108.8 10.0 %owner_spectra.1 = (f32[16,72,256]{2,1,0:T(8,128)S(1)}, f32[16,72,256]{2,1,0:T(8,128)S(1)}, f32[64,72,256]{2,1,0:T(8,128)S(1)}, s32[64]{0:T(128)S(1)}) custom-call(f32[32,257,1,128]{3,2,1,0:T(1,128)} %all-to-all-done.image_ref, f32[16,72,128]{2,1,0:T(8,128)S(1)} %fusion.6.contrast_ref, f32[4,72,256]{2,1,0:T(8,128)S(1)} %copy-done.2, ...), custom_call_target="tpu_custom_call" | custom-call | tf_op jit(solution)/shard_map/owner_spectra/pallas_call | solution.py:297
  118.7 5.4 %collective-permute-start = (f32[16,72,256]{2,1,0:T(8,128)S(1)}, f32[16,72,256]{2,1,0:T(8,128)S(1)}, u32[]{:S(2)}, u32[]{:S(2)}) collective-permute-start(f32[16,72,256]{2,1,0:T(8,128)S(1)} %get-tuple-element.11), channel_id=1, source_target_pairs={{0,32},{32,0},{64,96},{96,64},{128,160},{160,128},{192,224},{224,1... | collective-permute-start | bytes 3538952 | tf_op jit(solution)/shard_map/ppermute | solution.py:456
  124.2 0.0 copy-done.11
  124.2 4.2 %owner_scores.1 = f32[32,1,128]{2,1,0:T(1,128)} custom-call(s32[64]{0:T(128)S(1)} %get-tuple-element.12.local_ref, f32[64,72,256]{2,1,0:T(8,128)S(1)} %get-tuple-element.13.filt_ref, f32[32,72,256]{2,1,0:T(8,128)} %pad_maximum_fusion.refs_0_.ref_ref, bf16[512,256]{1,0:T(8,128)(2,1)S(1)} %maximum_maximum_fusion.refs_1_.col_ref, ...), custom_call_target="tpu_custom_call" | custom-call | tf_op jit(solution)/shard_map/owner_scores/pallas_call | solution.py:332
  128.3 0.0 collective-permute-done
  128.3 0.2 slice_add_fusion.1
  128.5 1.6 %collective-permute-start.1 = (f32[4,72,256]{2,1,0:T(8,128)S(1)}, f32[4,72,256]{2,1,0:T(8,128)S(1)}, u32[]{:S(2)}, u32[]{:S(2)}) collective-permute-start(f32[4,72,256]{2,1,0:T(8,128)S(1)} %get-tuple-element.22), channel_id=1, source_target_pairs={{0,64},{32,96},{64,128},{96,160},{128,192},{160,224},{192,0},{224,... | collective-permute-start | bytes 884744 | tf_op jit(solution)/shard_map/ppermute | solution.py:463
  130.1 2.7 %collective-permute-start.2 = (f32[4,72,256]{2,1,0:T(8,128)S(1)}, f32[4,72,256]{2,1,0:T(8,128)S(1)}, u32[]{:S(2)}, u32[]{:S(2)}) collective-permute-start(f32[4,72,256]{2,1,0:T(8,128)S(1)} %get-tuple-element.21), channel_id=1, source_target_pairs={{0,128},{32,160},{64,192},{96,224},{128,0},{160,32},{192,64},{224,... | collective-permute-start | bytes 884744 | tf_op jit(solution)/shard_map/ppermute | solution.py:463
  132.8 1.1 collective-permute-start.3
  133.8 0.2 convert_reduce_fusion
  134.0 4.4 %all-to-all-start.1 = ((f32[32,1,128]{2,1,0:T(1,128)}), f32[32,1,128]{2,1,0:T(1,128)S(1)}, u32[]{:S(2)}, u32[]{:S(2)}) async-start(f32[32,1,128]{2,1,0:T(1,128)} %owner_scores.1), calls=%async_computation.1 | async-start | bytes 32768 | tf_op jit(solution)/shard_map/all_to_all | solution.py:465
  138.4 8.5 %all-to-all-done.1.home_ref = f32[32,1,128]{2,1,0:T(1,128)S(1)} async-done(((f32[32,1,128]{2,1,0:T(1,128)}), f32[32,1,128]{2,1,0:T(1,128)S(1)}, u32[]{:S(2)}, u32[]{:S(2)}) %all-to-all-start.1) | async-done | bytes 16416 | tf_op jit(solution)/shard_map/all_to_all | solution.py:465
  146.9 0.0 collective-permute-done.1.a_ref
  146.9 0.0 collective-permute-done.2.b_ref
  146.9 0.0 collective-permute-done.3.c_ref
  147.0 2.1 %finish.1 = (f32[4,2,128,128]{3,2,1,0:T(8,128)}, f32[32,64]{1,0:T(8,128)}) custom-call(s32[32]{0:T(128)S(1)} %multiply_add_fusion.target_ref, f32[4,72,256]{2,1,0:T(8,128)S(1)} %get-tuple-element.23.mine_ref, f32[4,72,256]{2,1,0:T(8,128)S(1)} %collective-permute-done.1.a_ref, f32[4,72,256]{2,1,0:T(8,128)S(1)} %collective-permute-done.2.b_ref, ...), custom_call_target="tpu_custom_call" | custom-call | tf_op jit(solution)/shard_map/finish/pallas_call | solution.py:386
  (15 shorter events, 0.1 us)
Async XLA Ops:
  3.6 12.0 %copy-start.10 = (s32[64,2]{0,1:T(2,128)S(1)}, s32[64,2]{0,1:T(2,128)}, u32[]{:S(2)}) copy-start(s32[64,2]{0,1:T(2,128)} %param.23) | copy-start | bytes 1540
  3.6 105.1 %all-to-all-start = ((f32[32,257,1,128]{3,2,1,0:T(1,128)}), f32[32,257,1,128]{3,2,1,0:T(1,128)}, u32[]{:S(2)}, u32[]{:S(2)}) async-start(f32[32,257,1,128]{3,2,1,0:T(1,128)} %place_slots.1), calls=%async_computation | async-start | bytes 8421376 | tf_op jit(solution)/shard_map/all_to_all | solution.py:414
  16.3 2.9 %copy-start.7 = (f32[32,2,128,128]{3,2,1,0:T(8,128)S(1)}, f32[32,2,128,128]{3,2,1,0:T(8,128)}, u32[]{:S(2)}) copy-start(f32[32,2,128,128]{3,2,1,0:T(8,128)} %param.18) | copy-start | bytes 12582916
  16.3 2.9 %copy-start.9 = (f32[72,128,1,1]{1,0,3,2:T(8,128)S(1)}, f32[72,128,1,1]{1,0,3,2:T(8,128)}, u32[]{:S(2)}) copy-start(f32[72,128,1,1]{1,0,3,2:T(8,128)} %constant.99) | copy-start | bytes 110596
  19.2 1.7 %copy-start.8 = (f32[128,128,1,1]{1,0,2,3:T(8,128)S(1)}, f32[128,128,1,1]{1,0,2,3:T(8,128)}, u32[]{:S(2)}) copy-start(f32[128,128,1,1]{1,0,2,3:T(8,128)} %constant.100) | copy-start | bytes 196612
  22.2 1.8 %copy-start.12 = (f32[16]{0:T(128)S(1)}, f32[16]{0:T(128)}, u32[]{:S(2)}) copy-start(f32[16]{0:T(128)} %param.24) | copy-start | bytes 196
  22.3 86.5 %copy-start = (f32[17,72,256]{2,1,0:T(8,128)S(1)}, f32[17,72,256]{2,1,0:T(8,128)}, u32[]{:S(2)}) copy-start(f32[17,72,256]{2,1,0:T(8,128)} %constant.88.clone.row_ref) | copy-start | bytes 3760132
  22.3 86.5 %copy-start.1 = (bf16[768,256]{1,0:T(8,128)(2,1)S(1)}, bf16[768,256]{1,0:T(8,128)(2,1)}, u32[]{:S(2)}) copy-start(bf16[768,256]{1,0:T(8,128)(2,1)} %constant.91.clone.right_ref) | copy-start | bytes 1179652
  22.3 86.5 %copy-start.2 = (f32[4,72,256]{2,1,0:T(8,128)S(1)}, f32[4,72,256]{2,1,0:T(8,128)}, u32[]{:S(2)}) copy-start(f32[4,72,256]{2,1,0:T(8,128)} %constant.87.clone.turn_ref) | copy-start | bytes 884740
  22.3 86.4 %copy-start.3 = (bf16[288,256]{1,0:T(8,128)(2,1)S(1)}, bf16[288,256]{1,0:T(8,128)(2,1)}, u32[]{:S(2)}) copy-start(bf16[288,256]{1,0:T(8,128)(2,1)} %constant.90.clone.left_ref) | copy-start | bytes 442372
  22.3 86.4 %copy-start.5 = (f32[17,1,256]{2,1,0:T(1,128)S(1)}, f32[17,1,256]{2,1,0:T(1,128)}, u32[]{:S(2)}) copy-start(f32[17,1,256]{2,1,0:T(1,128)} %constant.89.clone.col_ref) | copy-start | bytes 52228
  26.2 97.9 %copy-start.11 = (s32[32]{0:T(128)S(1)}, s32[32]{0:T(128)}, u32[]{:S(2)}) copy-start(s32[32]{0:T(128)} %class_hbm.1) | copy-start | bytes 388
  118.7 9.6 %collective-permute-start = (f32[16,72,256]{2,1,0:T(8,128)S(1)}, f32[16,72,256]{2,1,0:T(8,128)S(1)}, u32[]{:S(2)}, u32[]{:S(2)}) collective-permute-start(f32[16,72,256]{2,1,0:T(8,128)S(1)} %get-tuple-element.11), channel_id=1, source_target_pairs={{0,32},{32,0},{64,96},{96,64},{128,160},{160,128},{192,224},{224,1... | collective-permute-start | bytes 3538952 | tf_op jit(solution)/shard_map/ppermute | solution.py:456
  128.3 18.6 %copy-start.4 = (bf16[128,128]{1,0:T(8,128)(2,1)S(1)}, bf16[128,128]{1,0:T(8,128)(2,1)}, u32[]{:S(2)}) copy-start(bf16[128,128]{1,0:T(8,128)(2,1)} %constant.92.clone.lanes_ref) | copy-start | bytes 98308
  128.3 18.6 %copy-start.6 = (bf16[64,80]{1,0:T(8,128)(2,1)S(1)}, bf16[64,80]{1,0:T(8,128)(2,1)}, u32[]{:S(2)}) copy-start(bf16[64,80]{1,0:T(8,128)(2,1)} %constant.93.clone.unfold_ref) | copy-start | bytes 30724
  128.5 18.4 %collective-permute-start.1 = (f32[4,72,256]{2,1,0:T(8,128)S(1)}, f32[4,72,256]{2,1,0:T(8,128)S(1)}, u32[]{:S(2)}, u32[]{:S(2)}) collective-permute-start(f32[4,72,256]{2,1,0:T(8,128)S(1)} %get-tuple-element.22), channel_id=1, source_target_pairs={{0,64},{32,96},{64,128},{96,160},{128,192},{160,224},{192,0},{224,... | collective-permute-start | bytes 884744 | tf_op jit(solution)/shard_map/ppermute | solution.py:463
  130.1 16.9 %collective-permute-start.2 = (f32[4,72,256]{2,1,0:T(8,128)S(1)}, f32[4,72,256]{2,1,0:T(8,128)S(1)}, u32[]{:S(2)}, u32[]{:S(2)}) collective-permute-start(f32[4,72,256]{2,1,0:T(8,128)S(1)} %get-tuple-element.21), channel_id=1, source_target_pairs={{0,128},{32,160},{64,192},{96,224},{128,0},{160,32},{192,64},{224,... | collective-permute-start | bytes 884744 | tf_op jit(solution)/shard_map/ppermute | solution.py:463
  132.8 14.2 %collective-permute-start.3 = (f32[4,72,256]{2,1,0:T(8,128)S(1)}, f32[4,72,256]{2,1,0:T(8,128)S(1)}, u32[]{:S(2)}, u32[]{:S(2)}) collective-permute-start(f32[4,72,256]{2,1,0:T(8,128)S(1)} %get-tuple-element.20), channel_id=1, source_target_pairs={{0,192},{32,224},{64,0},{96,32},{128,64},{160,96},{192,128},{224,1... | collective-permute-start | bytes 884744 | tf_op jit(solution)/shard_map/ppermute | solution.py:463
  134.0 12.9 %all-to-all-start.1 = ((f32[32,1,128]{2,1,0:T(1,128)}), f32[32,1,128]{2,1,0:T(1,128)S(1)}, u32[]{:S(2)}, u32[]{:S(2)}) async-start(f32[32,1,128]{2,1,0:T(1,128)} %owner_scores.1), calls=%async_computation.1 | async-start | bytes 32768 | tf_op jit(solution)/shard_map/all_to_all | solution.py:465

commit v6 on v5

--- a/solution.py
+++ b/solution.py
@@ -229,17 +229,16 @@
         filt_ref[item, :, :side] = filt_real
         filt_ref[item, :, side:] = filt_imag
 
-        @pl.when(info[6] > 0)
-        def _(info=info, filt_real=filt_real, filt_imag=filt_imag):
-            target = info[5]
-            row_real, row_imag = row_ref[info[2], :, :side], row_ref[info[2], :, side:]
-            half_real = filt_real * row_real - filt_imag * row_imag
-            half_imag = filt_real * row_imag + filt_imag * row_real
-            col_real, col_imag = col_ref[info[3], :, :side], col_ref[info[3], :, side:]
-            numer_ref[target, :, :side] += half_real * col_real - half_imag * col_imag
-            numer_ref[target, :, side:] += half_real * col_imag + half_imag * col_real
-            hit = (lane == info[4]).astype(jnp.float32)
-            numer_ref[target, COUNT : COUNT + 1, :side] += hit
+        live = info[6] > 0
+        target = info[5]
+        row_real, row_imag = row_ref[info[2], :, :side], row_ref[info[2], :, side:]
+        half_real = filt_real * row_real - filt_imag * row_imag
+        half_imag = filt_real * row_imag + filt_imag * row_real
+        col_real, col_imag = col_ref[info[3], :, :side], col_ref[info[3], :, side:]
+        numer_ref[target, :, :side] += jnp.where(live, half_real * col_real - half_imag * col_imag, 0.0)
+        numer_ref[target, :, side:] += jnp.where(live, half_real * col_imag + half_imag * col_real, 0.0)
+        hit = ((lane == info[4]) & live).astype(jnp.float32)
+        numer_ref[target, COUNT : COUNT + 1, :side] += hit
 
     @pl.when(pl.program_id(0) == pl.num_programs(0) - 1)
     def _():

time: 150 us -> 148 us (0.987)
  Pallas kernels: 19.2 us -> 17.7 us
where the time goes in v6:
time: 148 us
  waiting for transfers between devices  91 us (61%)
  starting transfers between devices  27.5 us (19%)
  Pallas kernels  17.7 us (12%)
  other arithmetic  7.21 us (5%)
  matrix products  2.73 us (2%)
    all_to_all x1, waiting for transfers between devices, body(): lax.all_to_all(send, 'cls', split_axis=0, concat_axis=0, tiled=True)  82.4 us
    all_to_all x1, starting transfers between devices, body(): lax.all_to_all(send, 'cls', split_axis=0, concat_axis=0, tiled=True)  12 us
    all_to_all x1, waiting for transfers between devices, body(): lax.all_to_all(slot_scores, 'cls', split_axis=0, concat_axis=0, tiled=True)  8.54 us
    pallas_call x1, Pallas kernels, owner_spectra(): pl.pallas_call(functools.partial(spectrum_kernel, step_sources), grid=(so...  8.54 us
    ppermute x1, starting transfers between devices, body(): got = lax.ppermute(give, 'grp', [(i, i ^ 1) for i in range(groups)])  5.5 us
    ppermute x3, starting transfers between devices, body(): blocks[step] = lax.ppermute(block, 'grp', pairs) if step else block  5.1 us
    all_to_all x1, starting transfers between devices, body(): lax.all_to_all(slot_scores, 'cls', split_axis=0, concat_axis=0, tiled=True)  4.85 us
    pallas_call x1, Pallas kernels, owner_scores(): pl.pallas_call(functools.partial(score_kernel, step_sources), grid=(items...  4.12 us
  transfers between devices with their start and end apart: 6, of which 2 were waited for; matrix products, arithmetic and copies ran while one was open for 7% of the time, Pallas kernels for 3%

profile of v6, /device:TPU:1, one launch (start us, length us, event | category | flops | bytes accessed | tf_op | source)
XLA Modules:
  0.0 147.9 jit_solution(15474241042400607423)
XLA Ops:
  0.6 3.0 %place_slots.1 = f32[32,257,1,128]{3,2,1,0:T(1,128)} custom-call(s32[32]{0:T(128)} %class_hbm.1, s32[32]{0:T(128)} %turn_hbm.1, s32[32]{0:T(128)} %best_hbm.1, s32[32]{0:T(128)} %bin_hbm.1, s32[2,64]{1,0:T(2,128)} %bitcast.18, f32[32,128,128]{2,1,0:T(8,128)} %image_ref.1), custom_call_target="tpu_custom_call" | custom-call | tf_op jit(solution)/shard_map/place_slots/pallas_call | solution.py:139
  3.6 0.0 copy-start.10
  3.6 12.0 %all-to-all-start = ((f32[32,257,1,128]{3,2,1,0:T(1,128)}), f32[32,257,1,128]{3,2,1,0:T(1,128)}, u32[]{:S(2)}, u32[]{:S(2)}) async-start(f32[32,257,1,128]{3,2,1,0:T(1,128)} %place_slots.1), calls=%async_computation | async-start | bytes 8421376 | tf_op jit(solution)/shard_map/all_to_all | solution.py:413
  15.7 0.0 copy-done.10
  15.7 0.2 fusion.24
  15.8 0.1 maximum_multiply_fusion.refs_2_.row_ref
  15.9 0.3 fusion.21
  16.2 0.1 reduce-precision_convert_fusion
  16.4 0.0 copy-start.7
  16.4 0.0 copy-start.9
  16.4 2.0 %copy_multiply_fusion = f32[32,2,72,128]{3,2,0,1:T(8,128)S(1)} fusion(f32[72]{0:T(128)S(1)} %compare_convert_fusion, f32[32,2,128,128]{3,2,1,0:T(8,128)} %param.18), kind=kLoop, calls=%fused_computation.1 | loop fusion | flops 589824 | bytes 4718880 | tf_op jit(solution)/shard_map/mul | solution.py:443
  18.4 0.8 copy-done.7
  19.3 0.0 copy-done.9
  19.3 1.6 %convolution_bitcast_fusion = f32[32,2,72,128]{3,2,1,0:T(8,128)S(1)} fusion(f32[72,128,1,1]{1,0,3,2:T(8,128)S(1)} %copy-done.9, f32[32,2,128,128]{3,2,1,0:T(8,128)S(1)} %copy-done.7), kind=kOutput, calls=%fused_computation.4 | convolution fusion | flops 452984832 | bytes 6590464 | tf_op jit(solution)/shard_map/ua,ciab->ciub/dot_general | solution.py:441
  20.9 0.0 copy-done.8
  20.9 1.1 fusion
  22.0 0.2 fusion.3
  22.3 0.0 copy-start.12
  22.3 0.0 copy-start
  22.3 0.0 copy-start.1
  22.3 0.0 copy-start.2
  22.3 0.0 copy-start.3
  22.3 0.0 copy-start.5
  22.3 1.6 %pad_maximum_fusion.refs_0_.ref_ref = f32[32,72,256]{2,1,0:T(8,128)} fusion(f32[32,72,128]{2,1,0:T(8,128)S(1)} %get-tuple-element.19, f32[32,72,128]{2,1,0:T(8,128)S(1)} %get-tuple-element.18), kind=kLoop, calls=%fused_computation | loop fusion | flops 589824 | bytes 4718592 | tf_op jit(solution)/shard_map/concatenate | solution.py:444
  24.0 0.1 add_multiply_fusion
  24.0 0.0 copy-done.12
  24.1 2.2 %fusion.6.contrast_ref = f32[16,72,128]{2,1,0:T(8,128)S(1)} fusion(f32[72,128]{1,0:T(8,128)S(1)} %add_multiply_fusion, f32[16]{0:T(128)S(1)} %copy-done.12), kind=kLoop, calls=%fused_computation.13 | loop fusion | flops 737280 | bytes 626752 | tf_op jit(solution)/shard_map/neg | solution.py:421
  26.2 0.0 copy-start.11
  26.3 82.4 %all-to-all-done.image_ref = f32[32,257,1,128]{3,2,1,0:T(1,128)} async-done(((f32[32,257,1,128]{3,2,1,0:T(1,128)}), f32[32,257,1,128]{3,2,1,0:T(1,128)}, u32[]{:S(2)}, u32[]{:S(2)}) %all-to-all-start) | async-done | bytes 4210720 | tf_op jit(solution)/shard_map/all_to_all | solution.py:413
  108.7 0.0 copy-done
  108.7 0.0 copy-done.1
  108.7 8.5 %owner_spectra.1 = (f32[16,72,256]{2,1,0:T(8,128)S(1)}, f32[16,72,256]{2,1,0:T(8,128)S(1)}, f32[64,72,256]{2,1,0:T(8,128)S(1)}, s32[64]{0:T(128)S(1)}) custom-call(f32[32,257,1,128]{3,2,1,0:T(1,128)} %all-to-all-done.image_ref, f32[16,72,128]{2,1,0:T(8,128)S(1)} %fusion.6.contrast_ref, f32[4,72,256]{2,1,0:T(8,128)S(1)} %copy-done.2, ...), custom_call_target="tpu_custom_call" | custom-call | tf_op jit(solution)/shard_map/owner_spectra/pallas_call | solution.py:296
  117.2 5.5 %collective-permute-start = (f32[16,72,256]{2,1,0:T(8,128)S(1)}, f32[16,72,256]{2,1,0:T(8,128)S(1)}, u32[]{:S(2)}, u32[]{:S(2)}) collective-permute-start(f32[16,72,256]{2,1,0:T(8,128)S(1)} %get-tuple-element.11), channel_id=1, source_target_pairs={{0,32},{32,0},{64,96},{96,64},{128,160},{160,128},{192,224},{224,1... | collective-permute-start | bytes 3538952 | tf_op jit(solution)/shard_map/ppermute | solution.py:455
  122.8 4.1 %owner_scores.1 = f32[32,1,128]{2,1,0:T(1,128)} custom-call(s32[64]{0:T(128)S(1)} %get-tuple-element.12.local_ref, f32[64,72,256]{2,1,0:T(8,128)S(1)} %get-tuple-element.13.filt_ref, f32[32,72,256]{2,1,0:T(8,128)} %pad_maximum_fusion.refs_0_.ref_ref, bf16[512,256]{1,0:T(8,128)(2,1)S(1)} %maximum_maximum_fusion.refs_1_.col_ref, ...), custom_call_target="tpu_custom_call" | custom-call | tf_op jit(solution)/shard_map/owner_scores/pallas_call | solution.py:331
  126.9 0.0 collective-permute-done
  126.9 0.2 slice_add_fusion.1
  127.1 1.5 collective-permute-start.1
  128.5 2.5 %collective-permute-start.2 = (f32[4,72,256]{2,1,0:T(8,128)S(1)}, f32[4,72,256]{2,1,0:T(8,128)S(1)}, u32[]{:S(2)}, u32[]{:S(2)}) collective-permute-start(f32[4,72,256]{2,1,0:T(8,128)S(1)} %get-tuple-element.21), channel_id=1, source_target_pairs={{0,128},{32,160},{64,192},{96,224},{128,0},{160,32},{192,64},{224,... | collective-permute-start | bytes 884744 | tf_op jit(solution)/shard_map/ppermute | solution.py:462
  131.1 1.1 collective-permute-start.3
  132.2 0.2 convert_reduce_fusion
  132.3 4.9 %all-to-all-start.1 = ((f32[32,1,128]{2,1,0:T(1,128)}), f32[32,1,128]{2,1,0:T(1,128)S(1)}, u32[]{:S(2)}, u32[]{:S(2)}) async-start(f32[32,1,128]{2,1,0:T(1,128)} %owner_scores.1), calls=%async_computation.1 | async-start | bytes 32768 | tf_op jit(solution)/shard_map/all_to_all | solution.py:464
  137.2 8.5 %all-to-all-done.1.home_ref = f32[32,1,128]{2,1,0:T(1,128)S(1)} async-done(((f32[32,1,128]{2,1,0:T(1,128)}), f32[32,1,128]{2,1,0:T(1,128)S(1)}, u32[]{:S(2)}, u32[]{:S(2)}) %all-to-all-start.1) | async-done | bytes 16416 | tf_op jit(solution)/shard_map/all_to_all | solution.py:464
  145.8 0.0 collective-permute-done.1.a_ref
  145.8 0.0 collective-permute-done.2.b_ref
  145.8 0.0 collective-permute-done.3.c_ref
  145.8 0.0 copy-done.4
  145.8 0.0 copy-done.6
  145.8 2.1 %finish.1 = (f32[4,2,128,128]{3,2,1,0:T(8,128)}, f32[32,64]{1,0:T(8,128)}) custom-call(s32[32]{0:T(128)S(1)} %multiply_add_fusion.target_ref, f32[4,72,256]{2,1,0:T(8,128)S(1)} %get-tuple-element.23.mine_ref, f32[4,72,256]{2,1,0:T(8,128)S(1)} %collective-permute-done.1.a_ref, f32[4,72,256]{2,1,0:T(8,128)S(1)} %collective-permute-done.2.b_ref, ...), custom_call_target="tpu_custom_call" | custom-call | tf_op jit(solution)/shard_map/finish/pallas_call | solution.py:385
  (15 shorter events, 0.1 us)
Async XLA Ops:
  3.6 12.1 %copy-start.10 = (s32[64,2]{0,1:T(2,128)S(1)}, s32[64,2]{0,1:T(2,128)}, u32[]{:S(2)}) copy-start(s32[64,2]{0,1:T(2,128)} %param.23) | copy-start | bytes 1540
  3.6 105.1 %all-to-all-start = ((f32[32,257,1,128]{3,2,1,0:T(1,128)}), f32[32,257,1,128]{3,2,1,0:T(1,128)}, u32[]{:S(2)}, u32[]{:S(2)}) async-start(f32[32,257,1,128]{3,2,1,0:T(1,128)} %place_slots.1), calls=%async_computation | async-start | bytes 8421376 | tf_op jit(solution)/shard_map/all_to_all | solution.py:413
  16.4 2.9 %copy-start.7 = (f32[32,2,128,128]{3,2,1,0:T(8,128)S(1)}, f32[32,2,128,128]{3,2,1,0:T(8,128)}, u32[]{:S(2)}) copy-start(f32[32,2,128,128]{3,2,1,0:T(8,128)} %param.18) | copy-start | bytes 12582916
  16.4 2.9 %copy-start.9 = (f32[72,128,1,1]{1,0,3,2:T(8,128)S(1)}, f32[72,128,1,1]{1,0,3,2:T(8,128)}, u32[]{:S(2)}) copy-start(f32[72,128,1,1]{1,0,3,2:T(8,128)} %constant.99) | copy-start | bytes 110596
  19.3 1.7 %copy-start.8 = (f32[128,128,1,1]{1,0,2,3:T(8,128)S(1)}, f32[128,128,1,1]{1,0,2,3:T(8,128)}, u32[]{:S(2)}) copy-start(f32[128,128,1,1]{1,0,2,3:T(8,128)} %constant.100) | copy-start | bytes 196612
  22.3 1.8 %copy-start.12 = (f32[16]{0:T(128)S(1)}, f32[16]{0:T(128)}, u32[]{:S(2)}) copy-start(f32[16]{0:T(128)} %param.24) | copy-start | bytes 196
  22.3 86.4 %copy-start = (f32[17,72,256]{2,1,0:T(8,128)S(1)}, f32[17,72,256]{2,1,0:T(8,128)}, u32[]{:S(2)}) copy-start(f32[17,72,256]{2,1,0:T(8,128)} %constant.88.clone.row_ref) | copy-start | bytes 3760132
  22.3 86.4 %copy-start.1 = (bf16[768,256]{1,0:T(8,128)(2,1)S(1)}, bf16[768,256]{1,0:T(8,128)(2,1)}, u32[]{:S(2)}) copy-start(bf16[768,256]{1,0:T(8,128)(2,1)} %constant.91.clone.right_ref) | copy-start | bytes 1179652
  22.3 86.4 %copy-start.2 = (f32[4,72,256]{2,1,0:T(8,128)S(1)}, f32[4,72,256]{2,1,0:T(8,128)}, u32[]{:S(2)}) copy-start(f32[4,72,256]{2,1,0:T(8,128)} %constant.87.clone.turn_ref) | copy-start | bytes 884740
  22.3 86.4 %copy-start.3 = (bf16[288,256]{1,0:T(8,128)(2,1)S(1)}, bf16[288,256]{1,0:T(8,128)(2,1)}, u32[]{:S(2)}) copy-start(bf16[288,256]{1,0:T(8,128)(2,1)} %constant.90.clone.left_ref) | copy-start | bytes 442372
  22.3 86.4 %copy-start.5 = (f32[17,1,256]{2,1,0:T(1,128)S(1)}, f32[17,1,256]{2,1,0:T(1,128)}, u32[]{:S(2)}) copy-start(f32[17,1,256]{2,1,0:T(1,128)} %constant.89.clone.col_ref) | copy-start | bytes 52228
  26.2 96.5 %copy-start.11 = (s32[32]{0:T(128)S(1)}, s32[32]{0:T(128)}, u32[]{:S(2)}) copy-start(s32[32]{0:T(128)} %class_hbm.1) | copy-start | bytes 388
  117.2 9.6 %collective-permute-start = (f32[16,72,256]{2,1,0:T(8,128)S(1)}, f32[16,72,256]{2,1,0:T(8,128)S(1)}, u32[]{:S(2)}, u32[]{:S(2)}) collective-permute-start(f32[16,72,256]{2,1,0:T(8,128)S(1)} %get-tuple-element.11), channel_id=1, source_target_pairs={{0,32},{32,0},{64,96},{96,64},{128,160},{160,128},{192,224},{224,1... | collective-permute-start | bytes 3538952 | tf_op jit(solution)/shard_map/ppermute | solution.py:455
  126.9 18.9 %copy-start.4 = (bf16[128,128]{1,0:T(8,128)(2,1)S(1)}, bf16[128,128]{1,0:T(8,128)(2,1)}, u32[]{:S(2)}) copy-start(bf16[128,128]{1,0:T(8,128)(2,1)} %constant.92.clone.lanes_ref) | copy-start | bytes 98308
  126.9 18.9 %copy-start.6 = (bf16[64,80]{1,0:T(8,128)(2,1)S(1)}, bf16[64,80]{1,0:T(8,128)(2,1)}, u32[]{:S(2)}) copy-start(bf16[64,80]{1,0:T(8,128)(2,1)} %constant.93.clone.unfold_ref) | copy-start | bytes 30724
  127.1 18.7 %collective-permute-start.1 = (f32[4,72,256]{2,1,0:T(8,128)S(1)}, f32[4,72,256]{2,1,0:T(8,128)S(1)}, u32[]{:S(2)}, u32[]{:S(2)}) collective-permute-start(f32[4,72,256]{2,1,0:T(8,128)S(1)} %get-tuple-element.22), channel_id=1, source_target_pairs={{0,64},{32,96},{64,128},{96,160},{128,192},{160,224},{192,0},{224,... | collective-permute-start | bytes 884744 | tf_op jit(solution)/shard_map/ppermute | solution.py:462
  128.5 17.2 %collective-permute-start.2 = (f32[4,72,256]{2,1,0:T(8,128)S(1)}, f32[4,72,256]{2,1,0:T(8,128)S(1)}, u32[]{:S(2)}, u32[]{:S(2)}) collective-permute-start(f32[4,72,256]{2,1,0:T(8,128)S(1)} %get-tuple-element.21), channel_id=1, source_target_pairs={{0,128},{32,160},{64,192},{96,224},{128,0},{160,32},{192,64},{224,... | collective-permute-start | bytes 884744 | tf_op jit(solution)/shard_map/ppermute | solution.py:462
  131.1 14.7 %collective-permute-start.3 = (f32[4,72,256]{2,1,0:T(8,128)S(1)}, f32[4,72,256]{2,1,0:T(8,128)S(1)}, u32[]{:S(2)}, u32[]{:S(2)}) collective-permute-start(f32[4,72,256]{2,1,0:T(8,128)S(1)} %get-tuple-element.20), channel_id=1, source_target_pairs={{0,192},{32,224},{64,0},{96,32},{128,64},{160,96},{192,128},{224,1... | collective-permute-start | bytes 884744 | tf_op jit(solution)/shard_map/ppermute | solution.py:462
  132.3 13.4 %all-to-all-start.1 = ((f32[32,1,128]{2,1,0:T(1,128)}), f32[32,1,128]{2,1,0:T(1,128)S(1)}, u32[]{:S(2)}, u32[]{:S(2)}) async-start(f32[32,1,128]{2,1,0:T(1,128)} %owner_scores.1), calls=%async_computation.1 | async-start | bytes 32768 | tf_op jit(solution)/shard_map/all_to_all | solution.py:464

commit v7 on v6

--- a/solution.py
+++ b/solution.py
@@ -326,7 +326,7 @@
 
 def owner_scores(local, filtered, refs, col, row):
     items, _, wide = filtered.shape
-    step_sources = 16
+    step_sources = 32
     whole = lambda x: pl.BlockSpec(x.shape, lambda i: (0,) * x.ndim)
     return pl.pallas_call(
         functools.partial(score_kernel, step_sources),

time: 148 us -> 148 us (level)
  no operation moved by 1% of the time
where the time goes in v7:
time: 148 us
  waiting for transfers between devices  91 us (61%)
  starting transfers between devices  27.5 us (19%)
  Pallas kernels  17.5 us (12%)
  other arithmetic  7.21 us (5%)
  matrix products  2.73 us (2%)
    all_to_all x1, waiting for transfers between devices, body(): lax.all_to_all(send, 'cls', split_axis=0, concat_axis=0, tiled=True)  82.5 us
    all_to_all x1, starting transfers between devices, body(): lax.all_to_all(send, 'cls', split_axis=0, concat_axis=0, tiled=True)  12 us
    pallas_call x1, Pallas kernels, owner_spectra(): pl.pallas_call(functools.partial(spectrum_kernel, step_sources), grid=(so...  8.55 us
    all_to_all x1, waiting for transfers between devices, body(): lax.all_to_all(slot_scores, 'cls', split_axis=0, concat_axis=0, tiled=True)  8.54 us
    ppermute x1, starting transfers between devices, body(): got = lax.ppermute(give, 'grp', [(i, i ^ 1) for i in range(groups)])  5.46 us
    ppermute x3, starting transfers between devices, body(): blocks[step] = lax.ppermute(block, 'grp', pairs) if step else block  5.27 us
    all_to_all x1, starting transfers between devices, body(): lax.all_to_all(slot_scores, 'cls', split_axis=0, concat_axis=0, tiled=True)  4.77 us
    pallas_call x1, Pallas kernels, owner_scores(): pl.pallas_call(functools.partial(score_kernel, step_sources), grid=(items...  3.87 us
  transfers between devices with their start and end apart: 6, of which 2 were waited for; matrix products, arithmetic and copies ran while one was open for 7% of the time, Pallas kernels for 3%

profile of v7, /device:TPU:1, one launch (start us, length us, event | category | flops | bytes accessed | tf_op | source)
XLA Modules:
  0.0 147.8 jit_solution(13729119000848063105)
XLA Ops:
  0.6 2.9 %place_slots.1 = f32[32,257,1,128]{3,2,1,0:T(1,128)} custom-call(s32[32]{0:T(128)} %class_hbm.1, s32[32]{0:T(128)} %turn_hbm.1, s32[32]{0:T(128)} %best_hbm.1, s32[32]{0:T(128)} %bin_hbm.1, s32[2,64]{1,0:T(2,128)} %bitcast.18, f32[32,128,128]{2,1,0:T(8,128)} %image_ref.1), custom_call_target="tpu_custom_call" | custom-call | tf_op jit(solution)/shard_map/place_slots/pallas_call | solution.py:139
  3.6 0.0 copy-start.10
  3.6 12.0 %all-to-all-start = ((f32[32,257,1,128]{3,2,1,0:T(1,128)}), f32[32,257,1,128]{3,2,1,0:T(1,128)}, u32[]{:S(2)}, u32[]{:S(2)}) async-start(f32[32,257,1,128]{3,2,1,0:T(1,128)} %place_slots.1), calls=%async_computation | async-start | bytes 8421376 | tf_op jit(solution)/shard_map/all_to_all | solution.py:413
  15.6 0.0 copy-done.10
  15.7 0.2 fusion.24
  15.8 0.1 maximum_multiply_fusion.refs_2_.row_ref
  15.9 0.3 fusion.21
  16.2 0.1 reduce-precision_convert_fusion
  16.3 0.0 copy-start.7
  16.3 0.0 copy-start.9
  16.4 2.0 %copy_multiply_fusion = f32[32,2,72,128]{3,2,0,1:T(8,128)S(1)} fusion(f32[72]{0:T(128)S(1)} %compare_convert_fusion, f32[32,2,128,128]{3,2,1,0:T(8,128)} %param.18), kind=kLoop, calls=%fused_computation.1 | loop fusion | flops 589824 | bytes 4718880 | tf_op jit(solution)/shard_map/mul | solution.py:443
  18.4 0.8 copy-done.7
  19.2 0.0 copy-done.9
  19.2 1.6 %convolution_bitcast_fusion = f32[32,2,72,128]{3,2,1,0:T(8,128)S(1)} fusion(f32[72,128,1,1]{1,0,3,2:T(8,128)S(1)} %copy-done.9, f32[32,2,128,128]{3,2,1,0:T(8,128)S(1)} %copy-done.7), kind=kOutput, calls=%fused_computation.4 | convolution fusion | flops 452984832 | bytes 6590464 | tf_op jit(solution)/shard_map/ua,ciab->ciub/dot_general | solution.py:441
  20.9 0.0 copy-done.8
  20.9 1.1 fusion
  22.0 0.2 fusion.3
  22.2 0.0 copy-start.12
  22.3 0.0 copy-start
  22.3 0.0 copy-start.1
  22.3 0.0 copy-start.2
  22.3 0.0 copy-start.3
  22.3 0.0 copy-start.5
  22.3 1.6 %pad_maximum_fusion.refs_0_.ref_ref = f32[32,72,256]{2,1,0:T(8,128)} fusion(f32[32,72,128]{2,1,0:T(8,128)S(1)} %get-tuple-element.19, f32[32,72,128]{2,1,0:T(8,128)S(1)} %get-tuple-element.18), kind=kLoop, calls=%fused_computation | loop fusion | flops 589824 | bytes 4718592 | tf_op jit(solution)/shard_map/concatenate | solution.py:444
  24.0 0.1 add_multiply_fusion
  24.0 0.0 copy-done.12
  24.0 2.2 %fusion.6.contrast_ref = f32[16,72,128]{2,1,0:T(8,128)S(1)} fusion(f32[72,128]{1,0:T(8,128)S(1)} %add_multiply_fusion, f32[16]{0:T(128)S(1)} %copy-done.12), kind=kLoop, calls=%fused_computation.13 | loop fusion | flops 737280 | bytes 626752 | tf_op jit(solution)/shard_map/neg | solution.py:421
  26.2 0.0 copy-start.11
  26.2 82.5 %all-to-all-done.image_ref = f32[32,257,1,128]{3,2,1,0:T(1,128)} async-done(((f32[32,257,1,128]{3,2,1,0:T(1,128)}), f32[32,257,1,128]{3,2,1,0:T(1,128)}, u32[]{:S(2)}, u32[]{:S(2)}) %all-to-all-start) | async-done | bytes 4210720 | tf_op jit(solution)/shard_map/all_to_all | solution.py:413
  108.7 0.0 copy-done
  108.7 0.0 copy-done.1
  108.7 0.0 copy-done.2
  108.7 0.0 copy-done.3
  108.7 8.5 %owner_spectra.1 = (f32[16,72,256]{2,1,0:T(8,128)S(1)}, f32[16,72,256]{2,1,0:T(8,128)S(1)}, f32[64,72,256]{2,1,0:T(8,128)S(1)}, s32[64]{0:T(128)S(1)}) custom-call(f32[32,257,1,128]{3,2,1,0:T(1,128)} %all-to-all-done.image_ref, f32[16,72,128]{2,1,0:T(8,128)S(1)} %fusion.6.contrast_ref, f32[4,72,256]{2,1,0:T(8,128)S(1)} %copy-done.2, ...), custom_call_target="tpu_custom_call" | custom-call | tf_op jit(solution)/shard_map/owner_spectra/pallas_call | solution.py:296
  117.3 5.5 %collective-permute-start = (f32[16,72,256]{2,1,0:T(8,128)S(1)}, f32[16,72,256]{2,1,0:T(8,128)S(1)}, u32[]{:S(2)}, u32[]{:S(2)}) collective-permute-start(f32[16,72,256]{2,1,0:T(8,128)S(1)} %get-tuple-element.11), channel_id=1, source_target_pairs={{0,32},{32,0},{64,96},{96,64},{128,160},{160,128},{192,224},{224,1... | collective-permute-start | bytes 3538952 | tf_op jit(solution)/shard_map/ppermute | solution.py:455
  122.8 3.9 %owner_scores.1 = f32[32,1,128]{2,1,0:T(1,128)} custom-call(s32[64]{0:T(128)S(1)} %get-tuple-element.12.local_ref, f32[64,72,256]{2,1,0:T(8,128)S(1)} %get-tuple-element.13.filt_ref, f32[32,72,256]{2,1,0:T(8,128)} %pad_maximum_fusion.refs_0_.ref_ref, bf16[512,256]{1,0:T(8,128)(2,1)S(1)} %maximum_maximum_fusion.refs_1_.col_ref, ...), custom_call_target="tpu_custom_call" | custom-call | tf_op jit(solution)/shard_map/owner_scores/pallas_call | solution.py:331
  126.7 0.0 collective-permute-done
  126.7 0.2 slice_add_fusion.1
  126.8 1.6 %collective-permute-start.1 = (f32[4,72,256]{2,1,0:T(8,128)S(1)}, f32[4,72,256]{2,1,0:T(8,128)S(1)}, u32[]{:S(2)}, u32[]{:S(2)}) collective-permute-start(f32[4,72,256]{2,1,0:T(8,128)S(1)} %get-tuple-element.22), channel_id=1, source_target_pairs={{0,64},{32,96},{64,128},{96,160},{128,192},{160,224},{192,0},{224,... | collective-permute-start | bytes 884744 | tf_op jit(solution)/shard_map/ppermute | solution.py:462
  128.4 2.6 %collective-permute-start.2 = (f32[4,72,256]{2,1,0:T(8,128)S(1)}, f32[4,72,256]{2,1,0:T(8,128)S(1)}, u32[]{:S(2)}, u32[]{:S(2)}) collective-permute-start(f32[4,72,256]{2,1,0:T(8,128)S(1)} %get-tuple-element.21), channel_id=1, source_target_pairs={{0,128},{32,160},{64,192},{96,224},{128,0},{160,32},{192,64},{224,... | collective-permute-start | bytes 884744 | tf_op jit(solution)/shard_map/ppermute | solution.py:462
  131.0 1.1 collective-permute-start.3
  132.1 0.2 convert_reduce_fusion
  132.3 4.8 %all-to-all-start.1 = ((f32[32,1,128]{2,1,0:T(1,128)}), f32[32,1,128]{2,1,0:T(1,128)S(1)}, u32[]{:S(2)}, u32[]{:S(2)}) async-start(f32[32,1,128]{2,1,0:T(1,128)} %owner_scores.1), calls=%async_computation.1 | async-start | bytes 32768 | tf_op jit(solution)/shard_map/all_to_all | solution.py:464
  137.1 8.5 %all-to-all-done.1.home_ref = f32[32,1,128]{2,1,0:T(1,128)S(1)} async-done(((f32[32,1,128]{2,1,0:T(1,128)}), f32[32,1,128]{2,1,0:T(1,128)S(1)}, u32[]{:S(2)}, u32[]{:S(2)}) %all-to-all-start.1) | async-done | bytes 16416 | tf_op jit(solution)/shard_map/all_to_all | solution.py:464
  145.6 0.0 collective-permute-done.1.a_ref
  145.6 0.0 collective-permute-done.2.b_ref
  145.6 0.0 collective-permute-done.3.c_ref
  145.6 2.1 %finish.1 = (f32[4,2,128,128]{3,2,1,0:T(8,128)}, f32[32,64]{1,0:T(8,128)}) custom-call(s32[32]{0:T(128)S(1)} %multiply_add_fusion.target_ref, f32[4,72,256]{2,1,0:T(8,128)S(1)} %get-tuple-element.23.mine_ref, f32[4,72,256]{2,1,0:T(8,128)S(1)} %collective-permute-done.1.a_ref, f32[4,72,256]{2,1,0:T(8,128)S(1)} %collective-permute-done.2.b_ref, ...), custom_call_target="tpu_custom_call" | custom-call | tf_op jit(solution)/shard_map/finish/pallas_call | solution.py:385
  (15 shorter events, 0.1 us)
Async XLA Ops:
  3.6 12.1 %copy-start.10 = (s32[64,2]{0,1:T(2,128)S(1)}, s32[64,2]{0,1:T(2,128)}, u32[]{:S(2)}) copy-start(s32[64,2]{0,1:T(2,128)} %param.23) | copy-start | bytes 1540
  3.6 105.1 %all-to-all-start = ((f32[32,257,1,128]{3,2,1,0:T(1,128)}), f32[32,257,1,128]{3,2,1,0:T(1,128)}, u32[]{:S(2)}, u32[]{:S(2)}) async-start(f32[32,257,1,128]{3,2,1,0:T(1,128)} %place_slots.1), calls=%async_computation | async-start | bytes 8421376 | tf_op jit(solution)/shard_map/all_to_all | solution.py:413
  16.3 2.9 %copy-start.7 = (f32[32,2,128,128]{3,2,1,0:T(8,128)S(1)}, f32[32,2,128,128]{3,2,1,0:T(8,128)}, u32[]{:S(2)}) copy-start(f32[32,2,128,128]{3,2,1,0:T(8,128)} %param.18) | copy-start | bytes 12582916
  16.3 2.9 %copy-start.9 = (f32[72,128,1,1]{1,0,3,2:T(8,128)S(1)}, f32[72,128,1,1]{1,0,3,2:T(8,128)}, u32[]{:S(2)}) copy-start(f32[72,128,1,1]{1,0,3,2:T(8,128)} %constant.99) | copy-start | bytes 110596
  19.2 1.7 %copy-start.8 = (f32[128,128,1,1]{1,0,2,3:T(8,128)S(1)}, f32[128,128,1,1]{1,0,2,3:T(8,128)}, u32[]{:S(2)}) copy-start(f32[128,128,1,1]{1,0,2,3:T(8,128)} %constant.100) | copy-start | bytes 196612
  22.2 1.8 %copy-start.12 = (f32[16]{0:T(128)S(1)}, f32[16]{0:T(128)}, u32[]{:S(2)}) copy-start(f32[16]{0:T(128)} %param.24) | copy-start | bytes 196
  22.3 86.5 %copy-start = (f32[17,72,256]{2,1,0:T(8,128)S(1)}, f32[17,72,256]{2,1,0:T(8,128)}, u32[]{:S(2)}) copy-start(f32[17,72,256]{2,1,0:T(8,128)} %constant.88.clone.row_ref) | copy-start | bytes 3760132
  22.3 86.4 %copy-start.1 = (bf16[768,256]{1,0:T(8,128)(2,1)S(1)}, bf16[768,256]{1,0:T(8,128)(2,1)}, u32[]{:S(2)}) copy-start(bf16[768,256]{1,0:T(8,128)(2,1)} %constant.91.clone.right_ref) | copy-start | bytes 1179652
  22.3 86.4 %copy-start.2 = (f32[4,72,256]{2,1,0:T(8,128)S(1)}, f32[4,72,256]{2,1,0:T(8,128)}, u32[]{:S(2)}) copy-start(f32[4,72,256]{2,1,0:T(8,128)} %constant.87.clone.turn_ref) | copy-start | bytes 884740
  22.3 86.4 %copy-start.3 = (bf16[288,256]{1,0:T(8,128)(2,1)S(1)}, bf16[288,256]{1,0:T(8,128)(2,1)}, u32[]{:S(2)}) copy-start(bf16[288,256]{1,0:T(8,128)(2,1)} %constant.90.clone.left_ref) | copy-start | bytes 442372
  22.3 86.4 %copy-start.5 = (f32[17,1,256]{2,1,0:T(1,128)S(1)}, f32[17,1,256]{2,1,0:T(1,128)}, u32[]{:S(2)}) copy-start(f32[17,1,256]{2,1,0:T(1,128)} %constant.89.clone.col_ref) | copy-start | bytes 52228
  26.2 96.5 %copy-start.11 = (s32[32]{0:T(128)S(1)}, s32[32]{0:T(128)}, u32[]{:S(2)}) copy-start(s32[32]{0:T(128)} %class_hbm.1) | copy-start | bytes 388
  117.3 9.4 %collective-permute-start = (f32[16,72,256]{2,1,0:T(8,128)S(1)}, f32[16,72,256]{2,1,0:T(8,128)S(1)}, u32[]{:S(2)}, u32[]{:S(2)}) collective-permute-start(f32[16,72,256]{2,1,0:T(8,128)S(1)} %get-tuple-element.11), channel_id=1, source_target_pairs={{0,32},{32,0},{64,96},{96,64},{128,160},{160,128},{192,224},{224,1... | collective-permute-start | bytes 3538952 | tf_op jit(solution)/shard_map/ppermute | solution.py:455
  126.6 19.0 %copy-start.4 = (bf16[128,128]{1,0:T(8,128)(2,1)S(1)}, bf16[128,128]{1,0:T(8,128)(2,1)}, u32[]{:S(2)}) copy-start(bf16[128,128]{1,0:T(8,128)(2,1)} %constant.92.clone.lanes_ref) | copy-start | bytes 98308
  126.6 19.0 %copy-start.6 = (bf16[64,80]{1,0:T(8,128)(2,1)S(1)}, bf16[64,80]{1,0:T(8,128)(2,1)}, u32[]{:S(2)}) copy-start(bf16[64,80]{1,0:T(8,128)(2,1)} %constant.93.clone.unfold_ref) | copy-start | bytes 30724
  126.8 18.8 %collective-permute-start.1 = (f32[4,72,256]{2,1,0:T(8,128)S(1)}, f32[4,72,256]{2,1,0:T(8,128)S(1)}, u32[]{:S(2)}, u32[]{:S(2)}) collective-permute-start(f32[4,72,256]{2,1,0:T(8,128)S(1)} %get-tuple-element.22), channel_id=1, source_target_pairs={{0,64},{32,96},{64,128},{96,160},{128,192},{160,224},{192,0},{224,... | collective-permute-start | bytes 884744 | tf_op jit(solution)/shard_map/ppermute | solution.py:462
  128.4 17.2 %collective-permute-start.2 = (f32[4,72,256]{2,1,0:T(8,128)S(1)}, f32[4,72,256]{2,1,0:T(8,128)S(1)}, u32[]{:S(2)}, u32[]{:S(2)}) collective-permute-start(f32[4,72,256]{2,1,0:T(8,128)S(1)} %get-tuple-element.21), channel_id=1, source_target_pairs={{0,128},{32,160},{64,192},{96,224},{128,0},{160,32},{192,64},{224,... | collective-permute-start | bytes 884744 | tf_op jit(solution)/shard_map/ppermute | solution.py:462
  131.0 14.6 %collective-permute-start.3 = (f32[4,72,256]{2,1,0:T(8,128)S(1)}, f32[4,72,256]{2,1,0:T(8,128)S(1)}, u32[]{:S(2)}, u32[]{:S(2)}) collective-permute-start(f32[4,72,256]{2,1,0:T(8,128)S(1)} %get-tuple-element.20), channel_id=1, source_target_pairs={{0,192},{32,224},{64,0},{96,32},{128,64},{160,96},{192,128},{224,1... | collective-permute-start | bytes 884744 | tf_op jit(solution)/shard_map/ppermute | solution.py:462
  132.3 13.3 %all-to-all-start.1 = ((f32[32,1,128]{2,1,0:T(1,128)}), f32[32,1,128]{2,1,0:T(1,128)S(1)}, u32[]{:S(2)}, u32[]{:S(2)}) async-start(f32[32,1,128]{2,1,0:T(1,128)} %owner_scores.1), calls=%async_computation.1 | async-start | bytes 32768 | tf_op jit(solution)/shard_map/all_to_all | solution.py:464
